TPU v7x, 32 devices: a whole 2x2x4 slice. The times are simulated.
32 devices in a mesh: rows: 4 (over x, core), seq: 8 (over z, y).
Axes of the slice: x: 2, y: 2, z: 4, core: 2. Of those that a mesh axis runs over, the one named last changes fastest.
Arguments:
- tokens: bfloat16 [4, 1024, 768], P('rows', 'seq'), may hold values from -6 to 6
- memory: bfloat16 [4, 1024, 768], P('rows', 'seq'), may hold values from -6 to 6
- out_grad: bfloat16 [4, 1024, 768], P('rows', 'seq'), may hold values from -6 to 6
- table_lengths: int32 [4, 2], P('rows'), may hold values from 0 to 1024, as said below
- table_plots: int32 [4, 2], P('rows'), may hold values from 0 to 1, each once within a row
- self_gain: bfloat16 [768], P(('rows', 'seq')), may hold values from 0.099609375 to 1.8984375
- self_query: bfloat16 [768, 768], P(('rows', 'seq')), may hold values from -0.21875 to 0.21875
- self_key: bfloat16 [768, 768], P(('rows', 'seq')), may hold values from -0.21875 to 0.21875
- self_value: bfloat16 [768, 768], P(('rows', 'seq')), may hold values from -0.21875 to 0.21875
- self_output: bfloat16 [768, 768], P(('rows', 'seq')), may hold values from -1.75 to 1.75
- cross_gain: bfloat16 [768], P(('rows', 'seq')), may hold values from 0.099609375 to 1.8984375
- cross_query: bfloat16 [768, 768], P(('rows', 'seq')), may hold values from -0.21875 to 0.21875
- cross_key: bfloat16 [768, 768], P(('rows', 'seq')), may hold values from -0.21875 to 0.21875
- cross_value: bfloat16 [768, 768], P(('rows', 'seq')), may hold values from -0.21875 to 0.21875
- cross_output: bfloat16 [768, 768], P(('rows', 'seq')), may hold values from -1.75 to 1.75
- mlp_gain: bfloat16 [768], P(('rows', 'seq')), may hold values from 0.099609375 to 1.8984375
- mlp_gate: bfloat16 [768, 2048], P(('rows', 'seq')), may hold values from -0.21875 to 0.21875
- mlp_up: bfloat16 [768, 2048], P(('rows', 'seq')), may hold values from -0.21875 to 0.21875
- mlp_down: bfloat16 [2048, 768], P(('rows', 'seq')), may hold values from -0.125 to 0.125
Outputs:
- layer_out: bfloat16 [4, 1024, 768], P('rows', 'seq')
- tokens_grad: bfloat16 [4, 1024, 768], P('rows', 'seq')
- memory_grad: bfloat16 [4, 1024, 768], P('rows', 'seq')
- self_gain_grad: float32 [768], P(('rows', 'seq'))
- self_query_grad: float32 [768, 768], P(('rows', 'seq'))
- self_key_grad: float32 [768, 768], P(('rows', 'seq'))
- self_value_grad: float32 [768, 768], P(('rows', 'seq'))
- self_output_grad: float32 [768, 768], P(('rows', 'seq'))
- cross_gain_grad: float32 [768], P(('rows', 'seq'))
- cross_query_grad: float32 [768, 768], P(('rows', 'seq'))
- cross_key_grad: float32 [768, 768], P(('rows', 'seq'))
- cross_value_grad: float32 [768, 768], P(('rows', 'seq'))
- cross_output_grad: float32 [768, 768], P(('rows', 'seq'))
- mlp_gain_grad: float32 [768], P(('rows', 'seq'))
- mlp_gate_grad: float32 [768, 2048], P(('rows', 'seq'))
- mlp_up_grad: float32 [768, 2048], P(('rows', 'seq'))
- mlp_down_grad: float32 [2048, 768], P(('rows', 'seq'))
Inputs may be any that keep to these rules, and one draw needn't show every extreme that they name: `table_lengths`: every row's lengths sum to 1024. The rows come in aligned blocks of four (rows 0 to 3, 4 to 7 and so on); in each block one row drawn from the seed holds a single table over all 1024 positions, the first, and its other tables are empty; in the other three rows of each block every table has 64 to 960 positions. `table_plots`: each row's entries name each of the row's 2 plots once.
All inputs are finite; a program needn't handle non-finite values.
Results may differ from a plain program's by a relative error of at most 0.03.
Values may be sent and summed in bfloat16 or wider, within the bound.
A program may use at most 192 MiB of HBM per device.

v0:
```python
import functools

import jax
import jax.numpy as jnp
from jax import lax
from jax.experimental import pallas as pl
from jax.experimental.pallas import tpu as pltpu
from jax.sharding import PartitionSpec as P

HEADS = 12


SCALE = 0.125
EPS = 1e-06
NEG = -1e30
ROW, SEQ = "rows", "seq"
BOTH = (ROW, SEQ)
EQ0 = "rhqk,rkhd->rqhd"
EQ1 = "rhqk,rqhd->rkhd"
EQ2 = "rld,de->rle"
EQ3 = "rld,rle->de"
EQ4 = "rle,de->rld"
EQ5 = "rqhd,rkhd->rhqk"
EQ6 = "rqhd,rqhd->rhq"


def running_sum(lengths):
    ids = jnp.arange(lengths.shape[1], dtype=jnp.int32)
    upto = (ids[None, :] <= ids[:, None]).astype(lengths.dtype)
    return jnp.sum(lengths[:, None, :] * upto[None], axis=2)


def rms_forward(values, gain_vector):
    inverse = lax.rsqrt(jnp.mean(values * values, axis=-1, keepdims=True) + EPS)
    return (values * inverse * gain_vector, inverse)


def rms_backward(values, inverse, gain_vector, upstream):
    normed = values * inverse
    gain_grad = jnp.sum(upstream * normed, axis=(0, 1))
    scaled = upstream * gain_vector
    input_grad = inverse * (scaled - normed * jnp.mean(scaled * normed, axis=-1, keepdims=True))
    return (input_grad, gain_grad)


def matmul(operand, weight):
    return jnp.einsum(EQ2, operand, weight, preferred_element_type=jnp.float32)


def matmul_back(upstream, weight):
    return jnp.einsum(EQ4, upstream, weight, preferred_element_type=jnp.float32)


def weight_grad(operand, upstream):
    return jnp.einsum(EQ3, operand, upstream, preferred_element_type=jnp.float32)


def split_heads(values):
    return values.reshape(values.shape[0], values.shape[1], HEADS, values.shape[2] // HEADS)


def segment_of(places, table_ends):
    return jnp.sum((places[None, :, None] >= table_ends[:, None, :]).astype(jnp.int32), axis=2)


def pair_mask(query_seg, query_pos, key_seg, key_pos, causal):
    same_pair = query_seg[:, :, None] == key_seg[:, None, :]
    if causal:
        same_pair = jnp.logical_and(same_pair, key_pos[None, None, :] <= query_pos[None, :, None])
    return same_pair


def over_blocks(advance_block, fold_state, arrays, block_width):
    piece_rows = arrays[0].shape[1]
    block_count = piece_rows // block_width
    stacked = tuple(
        (
            jnp.moveaxis(
                member.reshape((member.shape[0], block_count, block_width) + member.shape[2:]), 1, 0
            )
            for member in arrays
        )
    )

    def advance(carried, block_items):
        block_index, block_parts = block_items
        return (advance_block(carried, block_parts, block_index * block_width), None)

    fold_state, ignored = lax.scan(
        advance, fold_state, (jnp.arange(block_count, dtype=jnp.int32), stacked)
    )
    return fold_state


def forward_fold(query_heads, query_seg, query_pos, key_segment, causal, block_width):

    def advance_block(fold_state, parts, first_row):
        key_block, value_block = parts
        key_pos = first_row + jnp.arange(key_block.shape[1], dtype=jnp.int32)
        allowed = pair_mask(query_seg, query_pos, key_segment(key_pos), key_pos, causal)

        def compute(current):
            running_max, running_sum, accumulated = current
            scores = (
                jnp.einsum(
                    EQ5,
                    query_heads,
                    split_heads(key_block),
                    preferred_element_type=jnp.float32,
                )
                * SCALE
            )
            scores = jnp.where(allowed[:, None], scores, NEG)
            new_max = jnp.maximum(running_max, jnp.max(scores, axis=-1))
            weights = jnp.where(allowed[:, None], jnp.exp(scores - new_max[..., None]), 0.0)
            factor = jnp.exp(running_max - new_max)
            new_sum = running_sum * factor + jnp.sum(weights, axis=-1)
            update = jnp.einsum(
                EQ0,
                weights.astype(jnp.bfloat16),
                split_heads(value_block),
                preferred_element_type=jnp.float32,
            )
            return (
                new_max,
                new_sum,
                accumulated * jnp.transpose(factor, (0, 2, 1))[..., None] + update,
            )

        return compute(fold_state)

    def forward_fold_piece(fold_state, shard_piece, first_row):
        return over_blocks(advance_block, fold_state, shard_piece, block_width)

    return forward_fold_piece


def finish(fold_state):
    running_max, running_sum, accumulated = fold_state
    attended = accumulated / jnp.transpose(running_sum, (0, 2, 1))[..., None]
    return (attended, running_max + jnp.log(running_sum))


def query_grad_fold(
    query_heads,
    out_heads,
    log_total,
    row_delta,
    query_seg,
    query_pos,
    key_segment,
    causal,
    block_width,
):

    def advance_block(fold_state, parts, first_row):
        key_block, value_block = parts
        key_pos = first_row + jnp.arange(key_block.shape[1], dtype=jnp.int32)
        allowed = pair_mask(query_seg, query_pos, key_segment(key_pos), key_pos, causal)

        def compute(current):
            key_heads = split_heads(key_block)
            scores = (
                jnp.einsum(
                    EQ5, query_heads, key_heads, preferred_element_type=jnp.float32
                )
                * SCALE
            )
            scores = jnp.where(allowed[:, None], scores, NEG)
            probabilities = jnp.where(allowed[:, None], jnp.exp(scores - log_total[..., None]), 0.0)
            prob_grad = jnp.einsum(
                EQ5,
                out_heads,
                split_heads(value_block),
                preferred_element_type=jnp.float32,
            )
            score_grad = (probabilities * (prob_grad - row_delta[..., None])).astype(jnp.bfloat16)
            return current + SCALE * jnp.einsum(
                EQ0, score_grad, key_heads, preferred_element_type=jnp.float32
            )

        return compute(fold_state)

    def query_fold_piece(fold_state, shard_piece, first_row):
        return over_blocks(advance_block, fold_state, shard_piece, block_width)

    return query_fold_piece


def key_grad_fold(
    key_heads,
    value_heads,
    key_seg,
    key_pos,
    total_rows,
    delta_rows,
    query_segment,
    causal,
    block_width,
):

    def advance_block(fold_state, parts, first_row):
        query_block, out_block = parts
        piece_rows = query_block.shape[1]
        query_pos = first_row + jnp.arange(piece_rows, dtype=jnp.int32)
        allowed = pair_mask(query_segment(query_pos), query_pos, key_seg, key_pos, causal)
        total_block = lax.dynamic_slice_in_dim(total_rows, first_row, piece_rows, 2)
        delta_block = lax.dynamic_slice_in_dim(delta_rows, first_row, piece_rows, 2)

        def compute(current):
            key_acc, value_acc = current
            query_heads = split_heads(query_block)
            out_heads = split_heads(out_block)
            scores = (
                jnp.einsum(
                    EQ5, query_heads, key_heads, preferred_element_type=jnp.float32
                )
                * SCALE
            )
            scores = jnp.where(allowed[:, None], scores, NEG)
            probabilities = jnp.where(
                allowed[:, None], jnp.exp(scores - total_block[..., None]), 0.0
            )
            value_acc = value_acc + jnp.einsum(
                EQ1,
                probabilities.astype(jnp.bfloat16),
                out_heads,
                preferred_element_type=jnp.float32,
            )
            prob_grad = jnp.einsum(
                EQ5, out_heads, value_heads, preferred_element_type=jnp.float32
            )
            score_grad = (probabilities * (prob_grad - delta_block[..., None])).astype(jnp.bfloat16)
            key_acc = key_acc + SCALE * jnp.einsum(
                EQ1, score_grad, query_heads, preferred_element_type=jnp.float32
            )
            return (key_acc, value_acc)

        return compute(fold_state)

    def key_fold_piece(fold_state, shard_piece, first_row):
        return over_blocks(advance_block, fold_state, shard_piece, block_width)

    return key_fold_piece


def body_general(
    tokens,
    memory,
    out_grad,
    table_lengths,
    table_plots,
    self_gain,
    self_query,
    self_key,
    self_value,
    self_output,
    cross_gain,
    cross_query,
    cross_key,
    cross_value,
    cross_output,
    mlp_gain,
    mlp_gate,
    mlp_up,
    mlp_down,
):
    def whole(shard):
        return lax.all_gather(shard, BOTH, axis=0, tiled=True)

    all_self_gain = whole(self_gain)
    all_self_query = whole(self_query)
    all_self_key = whole(self_key)
    all_self_value = whole(self_value)
    all_self_output = whole(self_output)
    all_cross_gain = whole(cross_gain)
    all_cross_query = whole(cross_query)
    all_cross_key = whole(cross_key)
    all_cross_value = whole(cross_value)
    all_cross_output = whole(cross_output)
    all_mlp_gain = whole(mlp_gain)
    all_mlp_gate = whole(mlp_gate)
    all_mlp_up = whole(mlp_up)
    all_mlp_down = whole(mlp_down)
    seq_count = lax.axis_size(SEQ)
    seq_index = lax.axis_index(SEQ)
    row_count = tokens.shape[0]
    positions = tokens.shape[1]
    memory_cols = memory.shape[1]
    width = tokens.shape[2]
    head_size = width // HEADS
    query_pos = seq_index * positions + jnp.arange(positions, dtype=jnp.int32)
    memory_pos = seq_index * memory_cols + jnp.arange(memory_cols, dtype=jnp.int32)
    table_ends = running_sum(table_lengths)
    tables = table_lengths.shape[1]
    table_ids = jnp.arange(tables, dtype=jnp.int32)
    plot_width = memory_cols * seq_count // tables

    def token_segment(places):
        return segment_of(places, table_ends)

    def token_plot(places):
        segments = segment_of(places, table_ends)
        return jnp.sum(
            jnp.where(segments[:, :, None] == table_ids[None, None, :], table_plots[:, None, :], 0),
            axis=2,
        )

    def memory_plot(places):
        return (places // plot_width)[None, :]

    def start_state():
        return (
            jnp.full((row_count, HEADS, positions), NEG, jnp.float32),
            jnp.zeros((row_count, HEADS, positions), jnp.float32),
            jnp.zeros((row_count, positions, HEADS, head_size), jnp.float32),
        )

    values = tokens.astype(jnp.float32)
    normed_one, inverse_one = rms_forward(values, all_self_gain.astype(jnp.float32))
    input_one = normed_one.astype(jnp.bfloat16)
    queries = matmul(input_one, all_self_query).astype(jnp.bfloat16)
    key_rows = matmul(input_one, all_self_key).astype(jnp.bfloat16)
    value_rows = matmul(input_one, all_self_value).astype(jnp.bfloat16)
    query_seg = token_segment(query_pos)
    self_fold = forward_fold(
        split_heads(queries), query_seg, query_pos, token_segment, True, positions
    )
    self_out, self_total = finish(
        self_fold(
            start_state(),
            (
                lax.all_gather(key_rows, SEQ, axis=1, tiled=True),
                lax.all_gather(value_rows, SEQ, axis=1, tiled=True),
            ),
            jnp.int32(0),
        )
    )
    self_att = self_out.reshape(row_count, positions, width).astype(jnp.bfloat16)
    first_sum = values + matmul(self_att, all_self_output)
    normed_two, inverse_two = rms_forward(first_sum, all_cross_gain.astype(jnp.float32))
    input_two = normed_two.astype(jnp.bfloat16)
    cross_rows = matmul(input_two, all_cross_query).astype(jnp.bfloat16)
    memory_keys = matmul(memory, all_cross_key).astype(jnp.bfloat16)
    memory_rows = matmul(memory, all_cross_value).astype(jnp.bfloat16)
    query_plot = token_plot(query_pos)
    cross_fold = forward_fold(
        split_heads(cross_rows), query_plot, query_pos, memory_plot, False, memory_cols
    )
    cross_out, cross_total = finish(
        cross_fold(
            start_state(),
            (
                lax.all_gather(memory_keys, SEQ, axis=1, tiled=True),
                lax.all_gather(memory_rows, SEQ, axis=1, tiled=True),
            ),
            jnp.int32(0),
        )
    )
    cross_att = cross_out.reshape(row_count, positions, width).astype(jnp.bfloat16)
    second_sum = first_sum + matmul(cross_att, all_cross_output)
    normed_three, inverse_three = rms_forward(second_sum, all_mlp_gain.astype(jnp.float32))
    input_three = normed_three.astype(jnp.bfloat16)
    gate_pre = matmul(input_three, all_mlp_gate)
    up_pre = matmul(input_three, all_mlp_up)

    def gated_unit(gate_value, up_value):
        return jax.nn.gelu(gate_value, approximate=True) * up_value

    hidden_value, gated_back = jax.vjp(gated_unit, gate_pre, up_pre)
    hidden = hidden_value.astype(jnp.bfloat16)
    layer_out = (second_sum + matmul(hidden, all_mlp_down)).astype(jnp.bfloat16)
    upstream = out_grad.astype(jnp.float32)
    grad_down = weight_grad(hidden, out_grad)
    hidden_grad = matmul_back(out_grad, all_mlp_down)
    gate_grad, up_grad = gated_back(hidden_grad)
    gate_low = gate_grad.astype(jnp.bfloat16)
    up_low = up_grad.astype(jnp.bfloat16)
    grad_gate = weight_grad(input_three, gate_low)
    grad_up = weight_grad(input_three, up_low)
    three_grad = matmul_back(gate_low, all_mlp_gate) + matmul_back(
        up_low, all_mlp_up
    )
    part_three, grad_gain_three = rms_backward(
        second_sum, inverse_three, all_mlp_gain.astype(jnp.float32), three_grad
    )
    second_grad = upstream + part_three
    cross_branch = second_grad.astype(jnp.bfloat16)
    grad_cross_output = weight_grad(cross_att, cross_branch)
    cross_dout = matmul_back(cross_branch, all_cross_output).astype(jnp.bfloat16)
    cross_heads = split_heads(cross_dout)
    cross_delta = jnp.einsum(EQ6, cross_heads.astype(jnp.float32), cross_out)
    cross_total_all, cross_delta_all = (
        lax.all_gather(cross_total, SEQ, axis=2, tiled=True),
        lax.all_gather(cross_delta, SEQ, axis=2, tiled=True),
    )
    cross_query_fold = query_grad_fold(
        split_heads(cross_rows),
        cross_heads,
        cross_total,
        cross_delta,
        query_plot,
        query_pos,
        memory_plot,
        False,
        memory_cols,
    )
    cross_rows_grad = cross_query_fold(
        jnp.zeros((row_count, positions, HEADS, head_size), jnp.float32),
        (
            lax.all_gather(memory_keys, SEQ, axis=1, tiled=True),
            lax.all_gather(memory_rows, SEQ, axis=1, tiled=True),
        ),
        jnp.int32(0),
    )
    cross_rows_low = cross_rows_grad.reshape(row_count, positions, width).astype(jnp.bfloat16)
    memory_fold = key_grad_fold(
        split_heads(memory_keys),
        split_heads(memory_rows),
        memory_plot(memory_pos),
        memory_pos,
        cross_total_all,
        cross_delta_all,
        token_plot,
        False,
        positions,
    )
    memory_zero = jnp.zeros((row_count, memory_cols, HEADS, head_size), jnp.float32)
    memory_key_grad, memory_value_grad = memory_fold(
        (memory_zero, memory_zero),
        (
            lax.all_gather(cross_rows, SEQ, axis=1, tiled=True),
            lax.all_gather(cross_dout, SEQ, axis=1, tiled=True),
        ),
        jnp.int32(0),
    )
    memory_key_low = memory_key_grad.reshape(row_count, memory_cols, width).astype(jnp.bfloat16)
    memory_value_low = memory_value_grad.reshape(row_count, memory_cols, width).astype(jnp.bfloat16)
    grad_cross_query = weight_grad(input_two, cross_rows_low)
    grad_cross_key = weight_grad(memory, memory_key_low)
    grad_cross_value = weight_grad(memory, memory_value_low)
    memory_grad = (
        matmul_back(memory_key_low, all_cross_key)
        + matmul_back(memory_value_low, all_cross_value)
    ).astype(jnp.bfloat16)
    two_grad = matmul_back(cross_rows_low, all_cross_query)
    part_two, grad_gain_two = rms_backward(
        first_sum, inverse_two, all_cross_gain.astype(jnp.float32), two_grad
    )
    first_grad = second_grad + part_two
    self_branch = first_grad.astype(jnp.bfloat16)
    grad_self_output = weight_grad(self_att, self_branch)
    self_dout = matmul_back(self_branch, all_self_output).astype(jnp.bfloat16)
    self_heads = split_heads(self_dout)
    self_delta = jnp.einsum(EQ6, self_heads.astype(jnp.float32), self_out)
    self_total_all, self_delta_all = (
        lax.all_gather(self_total, SEQ, axis=2, tiled=True),
        lax.all_gather(self_delta, SEQ, axis=2, tiled=True),
    )
    self_query_fold = query_grad_fold(
        split_heads(queries),
        self_heads,
        self_total,
        self_delta,
        query_seg,
        query_pos,
        token_segment,
        True,
        positions,
    )
    queries_grad = self_query_fold(
        jnp.zeros((row_count, positions, HEADS, head_size), jnp.float32),
        (
            lax.all_gather(key_rows, SEQ, axis=1, tiled=True),
            lax.all_gather(value_rows, SEQ, axis=1, tiled=True),
        ),
        jnp.int32(0),
    )
    queries_low = queries_grad.reshape(row_count, positions, width).astype(jnp.bfloat16)
    self_key_fold = key_grad_fold(
        split_heads(key_rows),
        split_heads(value_rows),
        query_seg,
        query_pos,
        self_total_all,
        self_delta_all,
        token_segment,
        True,
        positions,
    )
    token_zero = jnp.zeros((row_count, positions, HEADS, head_size), jnp.float32)
    key_grad, value_grad = self_key_fold(
        (token_zero, token_zero),
        (
            lax.all_gather(queries, SEQ, axis=1, tiled=True),
            lax.all_gather(self_dout, SEQ, axis=1, tiled=True),
        ),
        jnp.int32(0),
    )
    key_low = key_grad.reshape(row_count, positions, width).astype(jnp.bfloat16)
    value_low = value_grad.reshape(row_count, positions, width).astype(jnp.bfloat16)
    grad_self_query = weight_grad(input_one, queries_low)
    grad_self_key = weight_grad(input_one, key_low)
    grad_self_value = weight_grad(input_one, value_low)
    one_grad = (
        matmul_back(queries_low, all_self_query)
        + matmul_back(key_low, all_self_key)
        + matmul_back(value_low, all_self_value)
    )
    part_one, grad_gain_one = rms_backward(
        values, inverse_one, all_self_gain.astype(jnp.float32), one_grad
    )
    tokens_grad = (first_grad + part_one).astype(jnp.bfloat16)
    summed = tuple(
        (
            lax.psum_scatter(grad_gain_one, BOTH, scatter_dimension=0, tiled=True),
            lax.psum_scatter(grad_self_query, BOTH, scatter_dimension=0, tiled=True),
            lax.psum_scatter(grad_self_key, BOTH, scatter_dimension=0, tiled=True),
            lax.psum_scatter(grad_self_value, BOTH, scatter_dimension=0, tiled=True),
            lax.psum_scatter(grad_self_output, BOTH, scatter_dimension=0, tiled=True),
            lax.psum_scatter(grad_gain_two, BOTH, scatter_dimension=0, tiled=True),
            lax.psum_scatter(grad_cross_query, BOTH, scatter_dimension=0, tiled=True),
            lax.psum_scatter(grad_cross_key, BOTH, scatter_dimension=0, tiled=True),
            lax.psum_scatter(grad_cross_value, BOTH, scatter_dimension=0, tiled=True),
            lax.psum_scatter(grad_cross_output, BOTH, scatter_dimension=0, tiled=True),
            lax.psum_scatter(grad_gain_three, BOTH, scatter_dimension=0, tiled=True),
            lax.psum_scatter(grad_gate, BOTH, scatter_dimension=0, tiled=True),
            lax.psum_scatter(grad_up, BOTH, scatter_dimension=0, tiled=True),
            lax.psum_scatter(grad_down, BOTH, scatter_dimension=0, tiled=True),
        )
    )
    return (layer_out, tokens_grad, memory_grad) + summed


MESH = pl.DeviceIdType.MESH
BF = jnp.bfloat16
F32 = jnp.float32
QW = 1152
VMEM_LIMIT = 60 * 1024 * 1024


def coords():
    r = lax.axis_index(ROW)
    s = lax.axis_index(SEQ)
    return lax.div(r, 2), lax.rem(r, 2), lax.rem(s, 2), lax.div(s, 2)


def dev(x, c, y, z):
    return {ROW: 2 * x + c, SEQ: 2 * z + y}


def remote(src, dst, send_sem, recv_sem, to):
    return pltpu.make_async_remote_copy(
        src_ref=src,
        dst_ref=dst,
        send_sem=send_sem,
        recv_sem=recv_sem,
        device_id=dev(*to),
        device_id_type=MESH,
    )


def owner_of(x, c, y, z):
    return lax.div(z, 2), lax.rem(z, 2), y, 2 * c + x


def source_of(x, c, y, z):
    return lax.rem(z, 2), lax.div(z, 2), y, 2 * x + c


def is_fixed(x, c, y, z):
    same = jnp.logical_and(lax.div(z, 2) == x, lax.rem(z, 2) == c)
    return jnp.logical_and(same, 2 * c + x == z)


def greet(me, pairs=(), z_line=False, moves=False):
    x, c, y, z = me
    bar = pltpu.get_barrier_semaphore()

    def hello(to):
        pl.semaphore_signal(bar, 1, device_id=dev(*to), device_id_type=MESH)

    count = len(pairs)
    for to in pairs:
        hello(to)
    if z_line:

        @pl.when(z > 0)
        def _():
            hello((x, c, y, z - 1))

        @pl.when(z < 3)
        def _():
            hello((x, c, y, z + 1))

        count = count + jnp.where(z > 0, 1, 0) + jnp.where(z < 3, 1, 0)
    if moves:
        away = jnp.logical_not(is_fixed(*me))

        @pl.when(away)
        def _():
            hello(owner_of(*me))
            hello(source_of(*me))

        count = count + jnp.where(away, 2, 0)
    pl.semaphore_wait(bar, count)


class Move:
    def __init__(self, me, src, dst, sems, back=False):
        self.me = me
        to = source_of(*me) if back else owner_of(*me)
        self.far = remote(src, dst, sems.at[0], sems.at[1], to)
        self.near = pltpu.make_async_copy(src, dst, sems.at[0])
        self.fixed = is_fixed(*me)

    def start(self):
        @pl.when(self.fixed)
        def _():
            self.near.start()

        @pl.when(jnp.logical_not(self.fixed))
        def _():
            self.far.start()

    def arrive(self):
        @pl.when(self.fixed)
        def _():
            self.near.wait()

        @pl.when(jnp.logical_not(self.fixed))
        def _():
            self.far.wait_recv()

    def finish(self):
        @pl.when(jnp.logical_not(self.fixed))
        def _():
            self.far.wait_send()


class Gather4:
    def __init__(self, me, buf, sems):
        x, c, y, z = me
        g = 2 * x + c
        self.g = g
        xp, cp = (1 - x, c, y, z), (x, 1 - c, y, z)
        far = 2 * (1 - x) + c
        self.x_own = remote(buf.at[g], buf.at[g], sems.at[0], sems.at[1], xp)
        self.c_own = remote(buf.at[g], buf.at[g], sems.at[2], sems.at[3], cp)
        self.c_far = remote(buf.at[far], buf.at[far], sems.at[4], sems.at[5], cp)

    def start(self):
        self.x_own.start()
        self.c_own.start()

    def forward(self):
        self.x_own.wait_recv()
        self.c_far.start()

    def arrive(self):
        self.c_own.wait_recv()
        self.c_far.wait_recv()

    def finish(self):
        self.x_own.wait_send()
        self.c_own.wait_send()
        self.c_far.wait_send()


class Gather8:
    def __init__(self, me, buf, sems):
        x, c, y, z = me
        xp, cp, yp = (1 - x, c, y, z), (x, 1 - c, y, z), (x, c, 1 - y, z)
        self.c = c

        def piece(px, pc, py):
            return buf.at[2 * (2 * px + pc) + py]

        def send(p, k, to):
            return remote(p, p, sems.at[2 * k], sems.at[2 * k + 1], to)

        own, at_x = piece(x, c, y), piece(1 - x, c, y)
        at_y, at_d = piece(x, c, 1 - y), piece(1 - x, c, 1 - y)
        self.x_own = send(own, 0, xp)
        self.y_own = send(own, 1, yp)
        self.c_own = send(own, 2, cp)
        self.c_x = send(at_x, 3, cp)
        self.c_y = send(at_y, 4, cp)
        self.c_d = send(at_d, 5, cp)
        self.d_by_y = send(at_x, 6, yp)
        self.d_by_x = send(at_y, 6, xp)

    def start(self):
        self.x_own.start()
        self.y_own.start()
        self.c_own.start()

    def forward(self):
        self.x_own.wait_recv()

        @pl.when(self.c == 0)
        def _():
            self.d_by_y.start()

        self.c_x.start()
        self.y_own.wait_recv()

        @pl.when(self.c == 1)
        def _():
            self.d_by_x.start()

        self.c_y.start()

    def forward_far(self):
        self.d_by_y.wait_recv()
        self.c_d.start()

    def arrive(self):
        for one in (self.c_own, self.c_x, self.c_y, self.c_d):
            one.wait_recv()

    def finish(self):
        for one in (self.x_own, self.y_own, self.c_own, self.c_x, self.c_y, self.c_d, self.d_by_y):
            one.wait_send()


QB = 256


def dot(a, b):
    return lax.dot_general(a, b, (((1,), (0,)), ((), ())), preferred_element_type=F32)


def dot_nt(a, b):
    return lax.dot_general(a, b, (((1,), (1,)), ((), ())), preferred_element_type=F32)


def dot_tn(a, b):
    return lax.dot_general(a, b, (((0,), (0,)), ((), ())), preferred_element_type=F32)


def masked(scores, info, lanes, causal):
    keys = scores.shape[0]
    if causal:
        pos = lax.broadcasted_iota(jnp.int32, scores.shape, 0)
        allowed = jnp.logical_and(pos >= info[1:2, lanes], pos <= info[0:1, lanes])
        return jnp.where(allowed, scores, NEG)
    plot = info[2:3, lanes]
    half = keys // 2
    low = jnp.where(plot == 0, 0.0, NEG)
    high = jnp.where(plot == 1, 0.0, NEG)
    return jnp.concatenate([scores[:half] + low, scores[half:] + high], axis=0)


class GatherPlane:
    def __init__(self, me, buf, sems):
        x, c, y, z = me

        def send(p, k, to):
            piece = buf.at[2 * p + y]
            return remote(piece, piece, sems.at[0, k], sems.at[1, k], to)

        yp = (x, c, 1 - y, z)
        self.along = [send(z, k - 1, (x, c, y, lax.rem(z + k, 4))) for k in (1, 2, 3)]
        self.across = [send(z, 3, yp)]
        self.across += [send(lax.rem(z + 4 - k, 4), 3 + k, yp) for k in (1, 2, 3)]

    def start(self):
        for one in self.along:
            one.start()
        self.across[0].start()

    def forward(self, k):
        self.along[k - 1].wait_recv()
        self.across[k].start()

    def arrive(self):
        for one in self.across:
            one.wait_recv()

    def finish(self):
        for one in self.along + self.across:
            one.wait_send()


class SumPlane:
    def __init__(self, me, parts, by_y, by_z, sems, lanes=None):
        x, c, y, z = me
        self.y, self.z = y, z
        lanes = slice(None) if lanes is None else lanes
        self.mine = [parts.at[2 * lax.rem(z + k, 4) + y, :, lanes] for k in range(4)]
        self.by_y = [by_y.at[lax.rem(z + k, 4), :, lanes] for k in range(4)]
        self.by_z = [by_z.at[k, :, lanes] for k in range(3)]

        def theirs(k):
            return parts.at[2 * lax.rem(z + k, 4) + 1 - y, :, lanes]

        yp = (x, c, 1 - y, z)
        self.across = [
            remote(theirs(k), self.by_y[k], sems.at[0, k], sems.at[1, k], yp) for k in range(4)
        ]
        self.along = [
            remote(
                self.mine[k],
                self.by_z[k - 1],
                sems.at[0, 3 + k],
                sems.at[1, 3 + k],
                (x, c, y, lax.rem(z + k, 4)),
            )
            for k in (1, 2, 3)
        ]

    def start(self):
        for k in (2, 1, 3, 0):
            self.across[k].start()

    def fold(self):
        for k in (2, 1, 3, 0):
            self.across[k].wait_recv()
            add_into(self.mine[k], self.by_y[k])
            if k:
                self.along[k - 1].start()

    def end(self):
        for k in (1, 2, 3):
            self.along[k - 1].wait_recv()
            add_into(self.mine[0], self.by_z[k - 1])

    def finish(self):
        for one in self.across + self.along:
            one.wait_send()


class Sum8:
    def __init__(self, me, parts, by_c, by_y, by_x, sems):
        x, c, y, z = me
        self.me, self.parts = me, parts
        self.by_c, self.by_y, self.by_x = by_c, by_y, by_x
        xp, cp, yp = (1 - x, c, y, z), (x, 1 - c, y, z), (x, c, 1 - y, z)

        def send(src, dst, k, to):
            return remote(src, dst, sems.at[0, k], sems.at[1, k], to)

        self.first = [
            send(parts.at[2 * (2 * px + 1 - c) + py], by_c.at[px, py], 2 * px + py, cp)
            for px in range(2)
            for py in range(2)
        ]
        self.second = [send(by_c.at[px, 1 - y], by_y.at[px], 4 + px, yp) for px in range(2)]
        self.third = send(by_y.at[1 - x], by_x, 6, xp)

    def start(self):
        for one in self.first:
            one.start()

    def to_y(self):
        x, c, y, z = self.me
        for one in self.first:
            one.wait_recv()
        for px in range(2):
            add_into(self.by_c.at[px, 1 - y], self.parts.at[2 * (2 * px + c) + 1 - y])
            self.second[px].start()

    def to_x(self):
        x, c, y, z = self.me
        for one in self.second:
            one.wait_recv()
        add_into(self.by_y.at[1 - x], self.by_c.at[1 - x, y])
        add_into(self.by_y.at[1 - x], self.parts.at[2 * (2 * (1 - x) + c) + y])
        self.third.start()

    def end(self):
        x, c, y, z = self.me
        self.third.wait_recv()
        return (
            self.parts[2 * (2 * x + c) + y].astype(F32)
            + self.by_c[x, y].astype(F32)
            + self.by_y[x].astype(F32)
            + self.by_x[...].astype(F32)
        )

    def finish(self):
        for one in self.first + self.second + [self.third]:
            one.wait_send()


class Sum4:
    def __init__(self, me, parts, by_c, by_x, sems):
        x, c, y, z = me
        self.me, self.parts, self.by_c, self.by_x = me, parts, by_c, by_x
        xp, cp = (1 - x, c, y, z), (x, 1 - c, y, z)
        self.first = [
            remote(parts.at[2 * px + 1 - c], by_c.at[px], sems.at[0, px], sems.at[1, px], cp)
            for px in range(2)
        ]
        self.second = remote(by_c.at[1 - x], by_x, sems.at[0, 2], sems.at[1, 2], xp)

    def start(self):
        for one in self.first:
            one.start()

    def to_x(self):
        x, c, y, z = self.me
        for one in self.first:
            one.wait_recv()
        add_into(self.by_c.at[1 - x], self.parts.at[2 * (1 - x) + c])
        self.second.start()

    def end(self):
        x, c, y, z = self.me
        self.second.wait_recv()
        return (
            self.parts[2 * x + c].astype(F32)
            + self.by_c[x].astype(F32)
            + self.by_x[...].astype(F32)
        )

    def finish(self):
        for one in self.first + [self.second]:
            one.wait_send()


def chunks(rows, step, run):
    def one(i, carry):
        run(pl.ds(pl.multiple_of(i * step, step), step))
        return carry

    lax.fori_loop(0, rows // step, one, 0)


def add_into(into, more, step=16):
    def run(rows):
        total = into[rows, :].astype(F32) + more[rows, :].astype(F32)
        into[rows, :] = total.astype(into.dtype)

    chunks(into.shape[0], step, run)


def dma(*shape):
    return pltpu.SemaphoreType.DMA(shape)


ANYWHERE = pl.BlockSpec(memory_space=pl.ANY)
IN_VMEM = pl.BlockSpec(memory_space=pltpu.VMEM)


def attend_head(h, info, qt, kv, kvt, out, lse, causal):
    keys = kv.shape[0]
    rows = slice(64 * h, 64 * h + 64)
    for b in range(512 // QB):
        lanes = slice(QB * b, QB * b + QB)
        top = keys * (b + 1) * QB // 512 if causal else keys
        scores = dot(kv[:top, rows], qt[rows, lanes])
        scores = masked(scores, info, lanes, causal)
        high = jnp.max(scores, axis=0, keepdims=True)
        weights = jnp.exp(scores - high)
        total = jnp.sum(weights, axis=0, keepdims=True)
        out[rows, lanes] = dot(kvt[192 + 64 * h : 256 + 64 * h, :top], weights.astype(BF)) / total
        lse[h : h + 1, lanes] = high + jnp.log(total)


def attend_back_head(h, info, qt, kv, kvt, outer_t, out, lse, dq, dkv, dk_acc, dv_acc, causal):
    keys = kv.shape[0]
    rows = slice(64 * h, 64 * h + 64)
    value_rows = slice(192 + 64 * h, 256 + 64 * h)
    for b in reversed(range(512 // QB)):
        lanes = slice(QB * b, QB * b + QB)
        top = keys * (b + 1) * QB // 512 if causal else keys
        query, outer = qt[rows, lanes], outer_t[rows, lanes]
        delta = jnp.sum(outer.astype(F32) * out[rows, lanes], axis=0, keepdims=True)
        scores = masked(dot(kv[:top, rows], query), info, lanes, causal)
        prob = jnp.exp(scores - lse[h : h + 1, lanes])
        grad = (prob * (dot(kv[:top, value_rows], outer) - delta)).astype(BF)
        dq[rows, lanes] = (SCALE * dot(kvt[rows, :top], grad)).astype(BF)
        dk_new = dot_nt(query, grad)
        dv_new = dot_nt(outer, prob.astype(BF))
        if b == 512 // QB - 1:
            dk_acc[...] = dk_new
            dv_acc[...] = dv_new
        else:
            dk_acc[:, :top] += dk_new
            dv_acc[:, :top] += dv_new
    dkv[rows, :] = dk_acc[...].astype(BF)
    dkv[value_rows, :] = dv_acc[...].astype(BF)


def norm(values, gain):
    inverse = lax.rsqrt(jnp.mean(values * values, axis=-1, keepdims=True) + EPS)
    return (values * inverse * gain).astype(BF)


def norm_back(values, gain, upstream):
    inverse = lax.rsqrt(jnp.mean(values * values, axis=-1, keepdims=True) + EPS)
    normed = values * inverse
    scaled = upstream * gain
    grad = inverse * (scaled - normed * jnp.mean(scaled * normed, axis=-1, keepdims=True))
    return grad, jnp.sum(upstream * normed, axis=0, keepdims=True)


def gelu_parts(u):
    root = 0.7978845608028654
    square = u * u
    bend = jnp.tanh(root * u * (1.0 + 0.044715 * square))
    half = 0.5 * (1.0 + bend)
    slope = half + 0.5 * u * (1.0 - bend * bend) * (root * (1.0 + 0.134145 * square))
    return u * half, slope


class Names:
    pass


def layer_kernel(names, *refs):
    R = Names()
    for name, ref in zip(names, refs, strict=True):
        setattr(R, name, ref)
    me = coords()
    x, c, y, z = me
    g = 2 * x + c
    s = 2 * z + y
    group = ((1 - x, c, y, z), (x, 1 - c, y, z), (1 - x, 1 - c, y, z))
    line = tuple((x, c, y, lax.rem(z + k, 4)) for k in (1, 2, 3))
    greet(me, group + line + ((x, c, 1 - y, z),), moves=True)

    there = owner_of(*me)
    there_g = 2 * there[0] + there[1]
    move_x = Move(me, R.tok, R.X.at[2 * there_g + y], R.s_move.at[0])
    move_t = Move(me, R.tab, R.TAB, R.s_move.at[1])
    move_m = Move(me, R.mem, R.M.at[2 * there_g + y], R.s_move.at[2])
    move_d = Move(me, R.dout, R.DO.at[there_g], R.s_move.at[3])
    move_x.start()
    move_t.start()
    near_dn = pltpu.make_async_copy(R.down, R.DN.at[s], R.s_near.at[0])
    near_dn.start()

    gains = R.gains[...].astype(F32)
    for k in range(4):
        narrow = slice(192 * k, 192 * k + 192)
        wide = slice(512 * k, 512 * k + 512)
        top = jnp.concatenate(
            [w[:, narrow].astype(F32) for w in (R.ck, R.cv, R.sk, R.sv, R.sq, R.cq)], axis=1
        )
        bottom = jnp.concatenate(
            [R.gate[:, wide].astype(F32), R.up[:, wide].astype(F32), gains], axis=1
        )
        R.stage[k] = jnp.concatenate([top, bottom], axis=0).astype(BF)
    parts = [
        remote(
            R.stage.at[2 * to[0] + to[1]], R.land.at[g], R.s_part.at[0, i], R.s_part.at[1, i], to
        )
        for i, to in enumerate(group)
    ]
    for one in parts:
        one.start()
    move_m.start()
    move_d.start()
    top = jnp.concatenate([R.so[...].astype(F32), R.co[:, :384].astype(F32)], axis=1)
    bottom = jnp.concatenate([R.co[:, 384:].astype(F32), R.cq[...].astype(F32)], axis=1)
    R.FL[g, s] = jnp.concatenate([top, bottom], axis=0).astype(BF)
    R.land[g] = R.stage[g]

    gather_x = Gather8(me, R.X, R.s_x)
    gather_m = Gather8(me, R.M, R.s_m)
    gather_d = Gather4(me, R.DO, R.s_d)
    gather_1 = GatherPlane(me, R.P1, R.s_1)
    gather_2 = GatherPlane(me, R.P2, R.s_2)
    gather_f = GatherPlane(me, R.FL.at[g], R.s_f)
    gather_n = GatherPlane(me, R.DN, R.s_n)
    gather_ff = Gather4(me, R.FL, R.s_ff)
    move_x.arrive()
    gather_x.start()
    for one in parts:
        one.wait_recv()
    tops, bottoms = [], []
    for r in range(4):
        piece = R.land[r].astype(F32)
        tops.append(jnp.concatenate([piece[:24], piece[24:, 1024:]], axis=1))
        bottoms.append(piece[24:, :1024])
    R.P1[s] = jnp.concatenate(tops, axis=0).astype(BF)
    gather_1.start()
    for one in parts:
        one.wait_send()
    R.P2[s] = jnp.concatenate(bottoms, axis=0).astype(BF)
    gather_x.forward()
    gather_x.forward_far()
    for k in (1, 3, 2):
        gather_1.forward(k)
    move_m.arrive()
    gather_m.start()
    gather_f.start()
    gather_1.arrive()
    move_d.arrive()
    gather_d.start()

    def unpack(pieces, whole, width):
        for zz in range(4):

            def one(i, carry):
                lanes = pl.ds(pl.multiple_of(i * 256, 256), 256)
                low = pieces[2 * zz, :, lanes].astype(F32)
                high = pieces[2 * zz + 1, :, lanes].astype(F32)
                for r in range(4):
                    rows = slice(24 * r, 24 * r + 24)
                    both = jnp.concatenate([low[rows], high[rows]], axis=0)
                    whole[192 * r + 48 * zz : 192 * r + 48 * zz + 48, lanes] = both.astype(BF)
                return carry

            lax.fori_loop(0, width // 256, one, 0)

    unpack(R.P1, R.W1, 1280)
    gather_1.finish()
    gain_rows = R.W1[:, 1152:1280].astype(F32).T
    gain_one, gain_two, gain_three = (gain_rows[i : i + 1] for i in range(3))
    gather_x.arrive()
    gather_m.forward()
    gather_m.forward_far()
    gather_d.forward()
    gather_2.start()
    near_dn.wait()
    gather_n.start()
    move_t.arrive()
    end_one, end_two = R.TAB[0:1, 0:1], R.TAB[1:2, 0:1]
    plot_one, plot_two = R.TAB[2:3, 0:1], R.TAB[3:4, 0:1]
    lane = lax.broadcasted_iota(jnp.int32, (1, 512), 1)
    for i in range(4):
        lanes = slice(128 * i, 128 * i + 128)
        R.info[0:1, lanes] = lane[:, :128] + (2 * i + y) * 128
    qpos = R.info[0:1, :]
    past_one, past_two = qpos >= end_one, qpos >= end_two
    R.info[1:2, :] = jnp.where(past_two, end_two, jnp.where(past_one, end_one, 0))
    R.info[2:3, :] = jnp.where(past_two, 0, jnp.where(past_one, plot_two, plot_one))

    def pair_rows(buf, i):
        return jnp.concatenate([buf[2 * i], buf[2 * i + 1]], axis=0)

    def mine_rows(buf):
        return jnp.concatenate([buf[2 * i + y] for i in range(4)], axis=0)

    def keys_values(i, operand, columns, natural, turned):
        rows = pl.ds(pl.multiple_of(i * 256, 256), 256)
        product = dot(operand, R.W1[:, columns])
        natural[rows, :] = product.astype(BF)
        turned[:, rows] = product.T.astype(BF)

    def first_norm(i, carry):
        x1 = norm(pair_rows(R.X, i).astype(F32), gain_one)
        R.X1[2 * i] = x1[:128]
        R.X1[2 * i + 1] = x1[128:]
        keys_values(i, x1, slice(384, 768), R.KV, R.KVT)
        return carry

    lax.fori_loop(0, 4, first_norm, 0)
    product = SCALE * dot(mine_rows(R.X1), R.W1[:, 768:1024])
    R.QT[...] = product.T[:192].astype(BF)
    for k in (1, 3, 2):
        gather_f.forward(k)

    for h in range(3):
        attend_head(h, R.info, R.QT, R.KV, R.KVT, R.OUT1, R.LSE1, True)
        if h == 0:
            gather_f.arrive()
            gather_ff.start()
        if h == 1:
            gather_2.forward(1)
            gather_n.forward(1)
            gather_2.forward(3)
            gather_n.forward(3)
    R.A4[g] = R.OUT1[...].astype(BF)
    share_a = Gather4(me, R.A4, R.s_a)
    share_a.start()
    gather_ff.forward()
    gather_2.forward(2)
    gather_n.forward(2)
    gather_m.arrive()

    def memory_pair(i, carry):
        keys_values(i, pair_rows(R.M, i), slice(0, 384), R.MKV, R.MKVT)
        return carry

    lax.fori_loop(0, 2, memory_pair, 0)
    share_a.forward()
    lax.fori_loop(2, 4, memory_pair, 0)
    gather_ff.arrive()

    def unpack_full(r, carry):
        for zz in range(4):
            low, high = R.FL[r, 2 * zz].astype(F32), R.FL[r, 2 * zz + 1].astype(F32)
            rows = pl.ds(pl.multiple_of(192 * r + 48 * zz, 16), 48)
            R.WF[rows, :QW] = jnp.concatenate([low[:24], high[:24]], axis=0).astype(BF)
            R.WF[rows, QW:] = jnp.concatenate([low[24:], high[24:]], axis=0).astype(BF)
        return carry

    lax.fori_loop(0, 4, unpack_full, 0)
    share_a.arrive()

    def project(pieces, weight, i):
        lanes = slice(256 * i, 256 * i + 256)
        turned = pieces[:, :, lanes].astype(F32).reshape(768, 256)
        return dot(turned.T.astype(BF), weight)

    for i in range(2):
        rows = slice(256 * i, 256 * i + 256)
        before = jnp.concatenate([R.X[4 * i + y], R.X[4 * i + 2 + y]], axis=0).astype(F32)
        first = before + project(R.A4, R.WF[:, :768], i)
        R.FIRST[rows, :] = first
        x2 = norm(first, gain_two)
        R.X2[rows, :] = x2
        product = SCALE * dot(x2, R.W1[:, 896:1152])
        R.CQT[:, rows] = product.T[64:].astype(BF)
    for h in range(3):
        attend_head(h, R.info, R.CQT, R.MKV, R.MKVT, R.OUT2, R.LSE2, False)
    R.C4[g] = R.OUT2[...].astype(BF)
    share_c = Gather4(me, R.C4, R.s_c)
    share_c.start()
    gather_2.arrive()
    unpack(R.P2, R.W2, 1024)
    gather_2.finish()
    share_c.forward()
    gather_d.arrive()
    gather_n.arrive()
    share_c.arrive()
    for i in range(2):
        rows = slice(256 * i, 256 * i + 256)
        second = R.FIRST[rows, :] + project(R.C4, R.WF[:, 768:1536], i)
        R.SECOND[rows, :] = second
        R.X3[rows, :] = norm(second, gain_three)

    sum_dx = Sum4(me, R.DXP, R.by_c_dx, R.by_x_dx, R.s_dx)
    sum_out = Sum4(me, R.OP, R.by_c_out, R.by_x_out, R.s_out)

    def feed(core):
        at = [pl.ds(pl.multiple_of((2 * px + core) * 128, 128), 128) for px in range(2)]
        x3 = jnp.concatenate([R.X3[rows, :] for rows in at], axis=0)
        gate, up = dot(x3, R.W2[:, :512]), dot(x3, R.W2[:, 512:])
        active, slope = gelu_parts(gate)
        hidden = (active * up).astype(BF)
        outer = jnp.concatenate([R.DO[2 * px + core] for px in range(2)], axis=0)
        w_down = R.DN[...].reshape(512, 768)
        hidden_grad = dot_nt(outer, w_down)
        gate_grad = (hidden_grad * up * slope).astype(BF)
        up_grad = (hidden_grad * active).astype(BF)
        dx3 = (dot_nt(gate_grad, R.W2[:, :512]) + dot_nt(up_grad, R.W2[:, 512:])).astype(BF)
        out = dot(hidden, w_down).astype(BF)
        for px in range(2):
            half = slice(128 * px, 128 * px + 128)
            R.H[at[px], :] = hidden[half]
            R.GG[at[px], :512] = gate_grad[half]
            R.GG[at[px], 512:] = up_grad[half]
            R.DXP[2 * px + core] = dx3[half]
            R.OP[2 * px + core] = out[half]

    feed(1 - c)
    sum_dx.start()
    feed(c)
    sum_dx.to_x()
    sum_out.start()
    own = pl.ds(pl.multiple_of(g * 128, 128), 128)
    own_block = 2 * g + y
    x3_t = R.X3[...].astype(F32).T.astype(BF)
    R.W2G[...] = dot(x3_t, R.GG[:, :512])
    part, gain_grad_three = norm_back(R.SECOND[own, :], gain_three, sum_dx.end())
    second_grad = R.DO[g].astype(F32) + part
    R.SGRAD[...] = second_grad
    R.DS4[g] = second_grad.astype(BF)
    share_s = Gather4(me, R.DS4, R.s_s)
    share_s.start()

    def pack(whole, pieces, start, width):
        for t in range(8):
            rows = [whole[(8 * r + t) * 24 : (8 * r + t) * 24 + 24, :] for r in range(4)]
            pieces[t, :, start : start + width] = jnp.concatenate(rows, axis=0).astype(BF)

    pack(R.W2G, R.P2, 0, 512)
    share_s.forward()
    R.W2G[...] = dot(x3_t, R.GG[:, 512:])
    pack(R.W2G, R.P2, 512, 512)
    hidden_t = R.H[...].astype(F32).T.astype(BF)
    d_down = dot(hidden_t, R.DO[...].reshape(512, 768)).astype(BF)
    for t in range(8):
        R.DNG[t] = d_down[64 * t : 64 * t + 64]
    total_2 = SumPlane(me, R.P2, R.by_y_2, R.by_z_2, R.s_g2)
    total_n = SumPlane(me, R.DNG, R.by_y_n, R.by_z_n, R.s_gn)
    share_s.arrive()
    total_2.start()
    total_n.start()

    dsec = R.DS4[...].reshape(512, 768)
    mine_192 = pl.ds(pl.multiple_of(g * 192, 16), 192)
    R.OUTER[...] = dot_nt(R.WF[mine_192, 768:1536], dsec).astype(BF)
    for h in range(3):
        attend_back_head(
            h, R.info, R.CQT, R.MKV, R.MKVT, R.OUTER, R.OUT2, R.LSE2, R.DCQT, R.MDKV, R.dk, R.dv, False
        )
    R.DC4[g] = R.DCQT[...]
    share_q = Gather4(me, R.DC4, R.s_q)
    share_q.start()
    sum_out.to_x()

    def pack_24(whole, pieces):
        for t in range(8):
            rows = whole[24 * t : 24 * t + 24]
            pieces[t] = jnp.concatenate([rows[:, :384], rows[:, 384:]], axis=0).astype(BF)

    pack_24(dot(R.C4[g], dsec), R.CO8)
    total_c = SumPlane(me, R.CO8, R.by_y_c, R.by_z_c, R.s_gc)
    total_c.start()
    total_2.fold()
    total_n.fold()

    def memory_grad_pair(i, carry):
        lanes = pl.ds(pl.multiple_of(i * 256, 256), 256)
        turned = dot(R.W1[:, :384], R.MDKV[:, lanes]).astype(BF)
        R.MG[2 * i] = turned[:, :128]
        R.MG[2 * i + 1] = turned[:, 128:]
        return carry

    lax.fori_loop(0, 2, memory_grad_pair, 0)
    share_q.forward()
    lax.fori_loop(2, 4, memory_grad_pair, 0)
    sum_m = Sum8(me, R.MG, R.by_c_m, R.by_y_m, R.by_x_m, R.s_gm)
    sum_m.start()
    share_q.arrive()

    for i in range(2):
        rows = slice(256 * i, 256 * i + 256)
        turned = R.DC4[:, :, rows].reshape(768, 256)
        dx2 = dot(R.WF[:, 1536:], turned).T
        part, ignored = norm_back(R.FIRST[rows, :], gain_two, dx2)
        R.DFIRST[rows, :] = (dsec[rows].astype(F32) + part).astype(BF)
    dx2 = dot(R.WF[:, 1536:], R.DC4[:, :, own].reshape(768, 128)).T
    part, gain_grad_two = norm_back(R.FIRST[own, :], gain_two, dx2)
    R.SGRAD[...] += part

    R.OUTER[...] = dot_nt(R.WF[mine_192, :768], R.DFIRST[...]).astype(BF)
    sum_m.to_y()
    for h in range(3):
        attend_back_head(
            h, R.info, R.QT, R.KV, R.KVT, R.OUTER, R.OUT1, R.LSE1, R.DQT, R.DKV, R.dk, R.dv, True
        )
        if h == 0:
            total_c.fold()
            sum_m.to_x()

    def token_grad_pair(i, carry):
        lanes = pl.ds(pl.multiple_of(i * 256, 256), 256)
        half = pl.ds(pl.multiple_of(i * 128, 128), 128)
        turned = dot(R.W1[:, 384:768], R.DKV[:, lanes])
        query = dot(R.W1[:, 768:960], R.DQT[:, half])
        R.TG[2 * i] = (turned[:, :128] + jnp.where(y == 0, query, 0.0)).astype(BF)
        R.TG[2 * i + 1] = (turned[:, 128:] + jnp.where(y == 1, query, 0.0)).astype(BF)
        return carry

    lax.fori_loop(0, 4, token_grad_pair, 0)
    sum_t = Sum8(me, R.TG, R.by_c_t, R.by_y_t, R.by_x_t, R.s_gt)
    sum_t.start()
    memory_t = dot(R.MDKV[...], R.M[...].reshape(1024, 768))
    R.W1G[...] = memory_t.T
    pack(R.W1G, R.P1, 0, 384)
    total_1a = SumPlane(me, R.P1, R.by_y_1, R.by_z_1, R.s_g1a, slice(0, 384))
    total_1a.start()
    sum_t.to_y()
    turned = dot(R.DKV[...], R.X1[...].reshape(1024, 768))
    R.W1G[...] = turned.T
    pack(R.W1G, R.P1, 384, 384)
    sum_t.to_x()
    R.TURN[:192, :] = dot(R.DQT[...], mine_rows(R.X1))
    R.TURN[192:, :] = dot(R.DCQT[...], R.X2[...])
    R.W1G[...] = R.TURN[...].T
    pack(R.W1G, R.P1, 768, 384)
    pack_24(dot(R.A4[g], R.DFIRST[...]), R.SO8)
    dx1 = sum_t.end().T
    part, gain_grad_one = norm_back(R.X[own_block].astype(F32), gain_one, dx1)
    gain_grads = jnp.concatenate(
        [gain_grad_one, gain_grad_two, gain_grad_three, jnp.zeros((125, 768), F32)], axis=0
    )
    R.GAINS[...] = gain_grads.T
    pack(R.GAINS, R.P1, 1152, 128)
    total_1b = SumPlane(me, R.P1, R.by_y_1, R.by_z_1, R.s_g1b, slice(384, 1280))
    total_s = SumPlane(me, R.SO8, R.by_y_s, R.by_z_s, R.s_gs)
    total_1b.start()
    total_s.start()
    R.TBLOCK[...] = (R.SGRAD[...] + part).astype(BF)
    R.LBLOCK[...] = (R.SECOND[own, :] + sum_out.end()).astype(BF)
    R.MBLOCK[...] = sum_m.end().T.astype(BF)
    back = [
        Move(me, src, dst, R.s_back.at[i], back=True)
        for i, (src, dst) in enumerate(
            ((R.TBLOCK, R.tokens_out), (R.LBLOCK, R.layer_out), (R.MBLOCK, R.memory_out))
        )
    ]
    for one in back:
        one.start()
    total_1a.fold()
    total_1b.fold()
    total_s.fold()
    total_2.end()
    total_n.end()
    total_c.end()
    total_1a.end()
    total_1b.end()
    first_rows = R.P1[s].astype(F32)
    last_rows = R.P2[s].astype(F32)
    for r in range(4):
        rows = slice(24 * r, 24 * r + 24)
        bottom = jnp.concatenate([last_rows[rows], first_rows[rows, 1152:]], axis=1)
        R.stage[r] = jnp.concatenate([first_rows[rows, :1152], bottom], axis=0).astype(BF)
    finals = [
        remote(
            R.stage.at[2 * to[0] + to[1]], R.quarters_out.at[g], R.s_last.at[0, i], R.s_last.at[1, i], to
        )
        for i, to in enumerate(group)
    ]
    for one in finals:
        one.start()
    total_s.end()
    near = [
        pltpu.make_async_copy(src, dst, R.s_near.at[1 + i])
        for i, (src, dst) in enumerate(
            (
                (R.stage.at[g], R.quarters_out.at[g]),
                (R.CO8.at[s], R.co_out),
                (R.SO8.at[s], R.so_out),
                (R.DNG.at[s], R.down_out),
            )
        )
    ]
    for one in near:
        one.start()
    for one in near:
        one.wait()
    for one in finals:
        one.wait_recv()
    for one in back:
        one.arrive()
        one.finish()
    for one in finals:
        one.wait_send()
    for one in (move_x, move_t, move_m, move_d):
        one.finish()
    for one in (gather_x, gather_m, gather_d, gather_f, gather_n, gather_ff):
        one.finish()
    for one in (share_a, share_c, share_s, share_q, sum_dx, sum_out, sum_m, sum_t):
        one.finish()
    for one in (total_1a, total_1b, total_2, total_n, total_c, total_s):
        one.finish()


def run_layer(inputs):
    n, d = 128, 768

    def low(*shape):
        return pltpu.VMEM(shape, BF)

    def full(*shape):
        return pltpu.VMEM(shape, F32)

    outs = dict(
        quarters_out=(4, 48, QW),
        co_out=(48, 384),
        so_out=(48, 384),
        down_out=(64, d),
        tokens_out=(n, d),
        layer_out=(n, d),
        memory_out=(n, d),
    )
    scratch = dict(
        stage=low(4, 48, QW), land=low(4, 48, QW),
        X=low(8, n, d), M=low(8, n, d), DO=low(4, n, d), TAB=pltpu.VMEM((8, 128), jnp.int32),
        P1=low(8, 96, 1280), P2=low(8, 96, 1024), FL=low(4, 8, 48, QW), DN=low(8, 64, d),
        W1=low(768, 1280), W2=low(768, 1024), WF=low(768, 2304),
        info=pltpu.VMEM((8, 512), jnp.int32),
        X1=low(8, n, d), X2=low(512, d), X3=low(512, d),
        KV=low(1024, 384), KVT=low(384, 1024), MKV=low(1024, 384), MKVT=low(384, 1024),
        QT=low(192, 512), CQT=low(192, 512), OUT1=full(192, 512), OUT2=full(192, 512),
        LSE1=full(8, 512), LSE2=full(8, 512),
        A4=low(4, 192, 512), C4=low(4, 192, 512), DC4=low(4, 192, 512),
        FIRST=full(512, d), SECOND=full(512, d),
        H=low(512, 512), GG=low(512, 1024), DXP=low(4, n, d), OP=low(4, n, d),
        by_c_dx=low(2, n, d), by_x_dx=low(n, d), by_c_out=low(2, n, d), by_x_out=low(n, d),
        W2G=full(768, 512), by_y_2=low(4, 96, 1024), by_z_2=low(3, 96, 1024),
        DNG=low(8, 64, d), by_y_n=low(4, 64, d), by_z_n=low(3, 64, d),
        SGRAD=full(n, d), DS4=low(4, n, d), OUTER=low(192, 512),
        DCQT=low(192, 512), DQT=low(192, 512), MDKV=low(384, 1024), DKV=low(384, 1024),
        dk=full(64, 1024), dv=full(64, 1024),
        CO8=low(8, 48, 384), by_y_c=low(4, 48, 384), by_z_c=low(3, 48, 384),
        SO8=low(8, 48, 384), by_y_s=low(4, 48, 384), by_z_s=low(3, 48, 384),
        MG=low(8, d, n), by_c_m=low(2, 2, d, n), by_y_m=low(2, d, n), by_x_m=low(d, n),
        TG=low(8, d, n), by_c_t=low(2, 2, d, n), by_y_t=low(2, d, n), by_x_t=low(d, n),
        DFIRST=low(512, d),
        W1G=full(768, 384), TURN=full(384, 768), GAINS=full(768, 128),
        by_y_1=low(4, 96, 1280), by_z_1=low(3, 96, 1280),
        TBLOCK=low(n, d), LBLOCK=low(n, d), MBLOCK=low(n, d),
        s_move=dma(4, 2), s_near=dma(5), s_part=dma(2, 3), s_last=dma(2, 3), s_back=dma(3, 2),
        s_x=dma(14), s_m=dma(14), s_d=dma(6), s_ff=dma(6),
        s_1=dma(2, 7), s_2=dma(2, 7), s_f=dma(2, 7), s_n=dma(2, 7),
        s_a=dma(6), s_c=dma(6), s_s=dma(6), s_q=dma(6),
        s_dx=dma(2, 3), s_out=dma(2, 3), s_gm=dma(2, 7), s_gt=dma(2, 7),
        s_g1a=dma(2, 7), s_g1b=dma(2, 7), s_g2=dma(2, 7), s_gn=dma(2, 7), s_gc=dma(2, 7), s_gs=dma(2, 7),
    )
    names = tuple(inputs) + tuple(outs) + tuple(scratch)
    return pl.pallas_call(
        functools.partial(layer_kernel, names),
        out_shape=tuple(jax.ShapeDtypeStruct(shape, BF) for shape in outs.values()),
        in_specs=[spec for _, spec in inputs.values()],
        out_specs=tuple([ANYWHERE] * len(outs)),
        scratch_shapes=list(scratch.values()),
        compiler_params=pltpu.CompilerParams(
            collective_id=1, has_side_effects=True, vmem_limit_bytes=VMEM_LIMIT
        ),
        name="layer",
    )(*[a for a, _ in inputs.values()])


def body_planes(
    tokens, memory, out_grad, table_lengths, table_plots,
    self_gain, self_query, self_key, self_value, self_output,
    cross_gain, cross_query, cross_key, cross_value, cross_output,
    mlp_gain, mlp_gate, mlp_up, mlp_down,
):
    gains = jnp.stack([self_gain, cross_gain, mlp_gain], axis=1)
    gains = jnp.pad(gains, ((0, 0), (0, 125)))
    ends = running_sum(table_lengths)
    tab = jnp.concatenate([ends[0], table_plots[0], jnp.zeros((4,), jnp.int32)])
    tab = jnp.broadcast_to(tab[:, None], (8, 128))
    oa, co, so, down, tokens_mine, layer_mine, memory_mine = run_layer(
        dict(
            tok=(tokens[0], ANYWHERE), mem=(memory[0], ANYWHERE), dout=(out_grad[0], ANYWHERE),
            tab=(tab, IN_VMEM), gains=(gains, IN_VMEM),
            sq=(self_query, IN_VMEM), sk=(self_key, IN_VMEM), sv=(self_value, IN_VMEM), so=(self_output, IN_VMEM),
            cq=(cross_query, IN_VMEM), ck=(cross_key, IN_VMEM), cv=(cross_value, IN_VMEM), co=(cross_output, IN_VMEM),
            gate=(mlp_gate, IN_VMEM), up=(mlp_up, IN_VMEM), down=(mlp_down, ANYWHERE),
        )
    )
    oa = oa.astype(F32)

    def columns(top, start, width):
        part = oa[:, 24 * top : 24 * top + 24, start : start + width]
        return jnp.moveaxis(part, 0, 1).reshape(24, 4 * width)

    def halves(a):
        a = a.astype(F32)
        return jnp.concatenate([a[:24], a[24:]], axis=1)

    gain_sum = jnp.sum(oa[:, 24:, 1024:1027], axis=0)
    return (
        layer_mine[None], tokens_mine[None], memory_mine[None],
        gain_sum[:, 0], columns(0, 768, 192), columns(0, 384, 192), columns(0, 576, 192), halves(so),
        gain_sum[:, 1], columns(0, 960, 192), columns(0, 0, 192), columns(0, 192, 192), halves(co),
        gain_sum[:, 2], columns(1, 0, 512), columns(1, 512, 512), down.astype(F32),
    )


def solution(mesh):
    placed = (
        P(ROW, SEQ, None),
        P(ROW, SEQ, None),
        P(ROW, SEQ, None),
        P(ROW, None),
        P(ROW, None),
        P(BOTH),
        P(BOTH, None),
        P(BOTH, None),
        P(BOTH, None),
        P(BOTH, None),
        P(BOTH),
        P(BOTH, None),
        P(BOTH, None),
        P(BOTH, None),
        P(BOTH, None),
        P(BOTH),
        P(BOTH, None),
        P(BOTH, None),
        P(BOTH, None),
    )
    small = mesh.shape[ROW] == 4 and mesh.shape[SEQ] == 8
    return jax.shard_map(
        body_planes if small else body_general,
        mesh=mesh,
        in_specs=placed,
        out_specs=(
            P(ROW, SEQ, None),
            P(ROW, SEQ, None),
            P(ROW, SEQ, None),
            P(BOTH),
            P(BOTH, None),
            P(BOTH, None),
            P(BOTH, None),
            P(BOTH, None),
            P(BOTH),
            P(BOTH, None),
            P(BOTH, None),
            P(BOTH, None),
            P(BOTH, None),
            P(BOTH),
            P(BOTH, None),
            P(BOTH, None),
            P(BOTH, None),
        ),
        check_vma=False,
    )
```

profile of v0, /device:TPU:0, one launch (start us, length us, event | category | flops | bytes accessed | tf_op | source)
XLA Modules:
  0.0 277.4 jit_solution(16817831264396047610)
XLA Ops:
  0.7 0.6 copy-done.5
  1.5 0.6 pad.4.refs_4_
  2.1 0.7 copy-done.9
  2.8 0.6 copy-done.8
  3.6 0.7 broadcast_in_dim.8.refs_3_
  4.2 260.4 %layer.1 = (bf16[4,48,1152]{2,1,0:T(8,128)(2,1)}, bf16[48,384]{1,0:T(8,128)(2,1)}, bf16[48,384]{1,0:T(8,128)(2,1)}, bf16[64,768]{1,0:T(8,128)(2,1)}, bf16[128,76...) custom-call(bf16[128,768]{1,0:T(8,128)(2,1)} %bitcast.31, bf16[128,768]{1,0:T(8,128)(2,1)} %bitcast.32, ...), custom_call_target="tpu_custom_call" | custom-call | tf_op jit(solution)/shard_map/layer/pallas_call | solution.py:1501
  264.6 0.8 fusion.1
  265.5 0.6 pad_maximum_fusion.1
  266.1 0.6 pad_maximum_fusion
  267.0 0.7 reshape.108
  267.8 0.7 reshape.109
  268.6 0.7 reshape.110
  269.4 0.7 reshape.111
  270.1 0.7 reshape.112
  270.9 0.7 reshape.113
  271.7 0.7 slice_reduce_fusion.1
  272.4 0.7 copy.77
  273.1 0.7 copy.78
  274.1 0.7 convert_element_type.19
  274.8 0.7 copy.82
  275.4 0.3 copy-done.2
  275.8 0.7 copy.83
  276.4 0.3 copy-done.1
  276.8 0.7 copy.84
  (30 shorter events, 1.1 us)
Async XLA Ops:
  0.7 0.7 copy-start.5
  0.7 0.7 copy-start.6
  0.7 0.7 copy-start.7
  2.1 0.7 copy-start.9
  2.8 0.7 copy-start.8
  264.6 2.1 copy-start
  273.1 0.9 copy-start.4
  273.8 0.9 copy-start.3
  274.8 1.0 copy-start.2
  275.8 1.0 copy-start.1
where the time goes:
time: 279 us; the launch traced here: 277 us
  Pallas kernels  260 us (93%)
  local copies, waits for them, and re-layouts  14.1 us (5%)
    pallas_call x1, Pallas kernels, run_layer(): pl.pallas_call(functools.partial(layer_kernel, names), out_shape=tuple((j...  260 us
    reshape x8, local copies, waits for them, and re-layouts, columns(): return jnp.moveaxis(part, 0, 1).reshape(24, 4 * width)  5.81 us

commit v1 on v0

--- a/solution.py
+++ b/solution.py
@@ -814,8 +814,8 @@
         for k in (2, 1, 3, 0):
             self.across[k].start()
 
-    def fold(self):
-        for k in (2, 1, 3, 0):
+    def fold(self, steps=(2, 1, 3, 0)):
+        for k in steps:
             self.across[k].wait_recv()
             add_into(self.mine[k], self.by_y[k])
             if k:
@@ -832,51 +832,54 @@
 
 
 class Sum8:
-    def __init__(self, me, parts, by_c, by_y, by_x, sems):
+    def __init__(self, me, parts, by_c, by_x, by_y, sems):
         x, c, y, z = me
         self.me, self.parts = me, parts
-        self.by_c, self.by_y, self.by_x = by_c, by_y, by_x
+        self.by_c, self.by_x, self.by_y = by_c, by_x, by_y
         xp, cp, yp = (1 - x, c, y, z), (x, 1 - c, y, z), (x, c, 1 - y, z)
 
         def send(src, dst, k, to):
             return remote(src, dst, sems.at[0, k], sems.at[1, k], to)
 
+        self.order = [(1 - x, 1 - y), (1 - x, y), (x, 1 - y), (x, y)]
         self.first = [
-            send(parts.at[2 * (2 * px + 1 - c) + py], by_c.at[px, py], 2 * px + py, cp)
-            for px in range(2)
-            for py in range(2)
+            send(parts.at[2 * (2 * px + 1 - c) + py], by_c.at[px, py], k, cp)
+            for k, (px, py) in enumerate(self.order)
         ]
-        self.second = [send(by_c.at[px, 1 - y], by_y.at[px], 4 + px, yp) for px in range(2)]
-        self.third = send(by_y.at[1 - x], by_x, 6, xp)
+        self.second = [
+            send(by_c.at[1 - x, py], by_x.at[py], 4 + k, xp) for k, py in enumerate((1 - y, y))
+        ]
+        self.third = send(by_x.at[1 - y], by_y, 6, yp)
 
     def start(self):
         for one in self.first:
             one.start()
 
+    def to_x(self):
+        x, c, y, z = self.me
+        for k, py in enumerate((1 - y, y)):
+            self.first[k].wait_recv()
+            add_into(self.by_c.at[1 - x, py], self.parts.at[2 * (2 * (1 - x) + c) + py])
+            self.second[k].start()
+
     def to_y(self):
         x, c, y, z = self.me
-        for one in self.first:
-            one.wait_recv()
-        for px in range(2):
-            add_into(self.by_c.at[px, 1 - y], self.parts.at[2 * (2 * px + c) + 1 - y])
-            self.second[px].start()
-
-    def to_x(self):
-        x, c, y, z = self.me
-        for one in self.second:
-            one.wait_recv()
-        add_into(self.by_y.at[1 - x], self.by_c.at[1 - x, y])
-        add_into(self.by_y.at[1 - x], self.parts.at[2 * (2 * (1 - x) + c) + y])
+        self.first[2].wait_recv()
+        self.first[3].wait_recv()
+        add_into(self.by_c.at[x, 1 - y], self.parts.at[2 * (2 * x + c) + 1 - y])
+        self.second[0].wait_recv()
+        add_into(self.by_x.at[1 - y], self.by_c.at[x, 1 - y])
         self.third.start()
 
     def end(self):
         x, c, y, z = self.me
+        self.second[1].wait_recv()
         self.third.wait_recv()
         return (
             self.parts[2 * (2 * x + c) + y].astype(F32)
             + self.by_c[x, y].astype(F32)
-            + self.by_y[x].astype(F32)
-            + self.by_x[...].astype(F32)
+            + self.by_x[y].astype(F32)
+            + self.by_y[...].astype(F32)
         )
 
     def finish(self):
@@ -1018,106 +1021,104 @@
     x, c, y, z = me
     g = 2 * x + c
     s = 2 * z + y
-    group = ((1 - x, c, y, z), (x, 1 - c, y, z), (1 - x, 1 - c, y, z))
+    group = ((1 - x, c, y, z), (1 - x, 1 - c, y, z), (x, 1 - c, y, z))
     line = tuple((x, c, y, lax.rem(z + k, 4)) for k in (1, 2, 3))
     greet(me, group + line + ((x, c, 1 - y, z),), moves=True)
 
     there = owner_of(*me)
     there_g = 2 * there[0] + there[1]
     move_x = Move(me, R.tok, R.X.at[2 * there_g + y], R.s_move.at[0])
-    move_t = Move(me, R.tab, R.TAB, R.s_move.at[1])
+    move_t = Move(me, R.tabs, R.TAB, R.s_move.at[1])
     move_m = Move(me, R.mem, R.M.at[2 * there_g + y], R.s_move.at[2])
     move_d = Move(me, R.dout, R.DO.at[there_g], R.s_move.at[3])
     move_x.start()
-    move_t.start()
     near_dn = pltpu.make_async_copy(R.down, R.DN.at[s], R.s_near.at[0])
     near_dn.start()
-
     gains = R.gains[...].astype(F32)
+    blank = jnp.zeros((24, 64), F32)
     for k in range(4):
         narrow = slice(192 * k, 192 * k + 192)
+        top = [w[:, narrow].astype(F32) for w in (R.sk, R.sv, R.sq)] + [gains]
+        bottom = [w[:, narrow].astype(F32) for w in (R.ck, R.cv, R.cq)] + [blank]
+        R.stage_a[k] = jnp.concatenate(
+            [jnp.concatenate(top, axis=1), jnp.concatenate(bottom, axis=1)], axis=0
+        ).astype(BF)
+
+    def to_group(stage, land, sems):
+        return [
+            remote(stage.at[2 * to[0] + to[1]], land.at[g], sems.at[0, i], sems.at[1, i], to)
+            for i, to in enumerate(group)
+        ]
+
+    parts_a = to_group(R.stage_a, R.land_a, R.s_part_a)
+    for one in parts_a:
+        one.start()
+    for t in range(2):
+        length, plot = R.lengths[0, t], R.plots[0, t]
+        start = R.lengths[0, 0] if t else 0
+        R.tabs[t : t + 1, :] = jnp.full((1, 128), start + length, jnp.int32)
+        R.tabs[2 + t : 3 + t, :] = jnp.full((1, 128), plot, jnp.int32)
+    R.tabs[4:, :] = jnp.zeros((4, 128), jnp.int32)
+    move_t.start()
+
+    def halves_stacked(w):
+        w = w[...].astype(F32)
+        return jnp.concatenate([w[:, :384], w[:, 384:]], axis=0).astype(BF)
+
+    R.FO[g, s] = halves_stacked(R.so)
+    gather_o = GatherPlane(me, R.FO.at[g], R.s_fo)
+    gather_o.start()
+    R.FC[g, s] = halves_stacked(R.co)
+    R.FQ[g, s] = halves_stacked(R.cq)
+    gather_c = GatherPlane(me, R.FC.at[g], R.s_fc)
+    gather_q = GatherPlane(me, R.FQ.at[g], R.s_fq)
+    for k in range(4):
         wide = slice(512 * k, 512 * k + 512)
-        top = jnp.concatenate(
-            [w[:, narrow].astype(F32) for w in (R.ck, R.cv, R.sk, R.sv, R.sq, R.cq)], axis=1
-        )
-        bottom = jnp.concatenate(
-            [R.gate[:, wide].astype(F32), R.up[:, wide].astype(F32), gains], axis=1
-        )
-        R.stage[k] = jnp.concatenate([top, bottom], axis=0).astype(BF)
-    parts = [
-        remote(
-            R.stage.at[2 * to[0] + to[1]], R.land.at[g], R.s_part.at[0, i], R.s_part.at[1, i], to
-        )
-        for i, to in enumerate(group)
-    ]
-    for one in parts:
-        one.start()
-    move_m.start()
-    move_d.start()
-    top = jnp.concatenate([R.so[...].astype(F32), R.co[:, :384].astype(F32)], axis=1)
-    bottom = jnp.concatenate([R.co[:, 384:].astype(F32), R.cq[...].astype(F32)], axis=1)
-    R.FL[g, s] = jnp.concatenate([top, bottom], axis=0).astype(BF)
-    R.land[g] = R.stage[g]
-
+        R.stage_b[k, :24] = R.gate[:, wide]
+        R.stage_b[k, 24:] = R.up[:, wide]
+    R.land_a[g] = R.stage_a[g]
+    R.land_b[g] = R.stage_b[g]
     gather_x = Gather8(me, R.X, R.s_x)
     gather_m = Gather8(me, R.M, R.s_m)
     gather_d = Gather4(me, R.DO, R.s_d)
-    gather_1 = GatherPlane(me, R.P1, R.s_1)
+    gather_a = GatherPlane(me, R.PA, R.s_a)
+    gather_b = GatherPlane(me, R.PB, R.s_b)
     gather_2 = GatherPlane(me, R.P2, R.s_2)
-    gather_f = GatherPlane(me, R.FL.at[g], R.s_f)
     gather_n = GatherPlane(me, R.DN, R.s_n)
-    gather_ff = Gather4(me, R.FL, R.s_ff)
-    move_x.arrive()
-    gather_x.start()
-    for one in parts:
+    whole_o = Gather4(me, R.FO, R.s_wo)
+    whole_c = Gather4(me, R.FC, R.s_wc)
+    whole_q = Gather4(me, R.FQ, R.s_wq)
+
+    for one in parts_a:
         one.wait_recv()
     tops, bottoms = [], []
     for r in range(4):
-        piece = R.land[r].astype(F32)
-        tops.append(jnp.concatenate([piece[:24], piece[24:, 1024:]], axis=1))
-        bottoms.append(piece[24:, :1024])
-    R.P1[s] = jnp.concatenate(tops, axis=0).astype(BF)
-    gather_1.start()
-    for one in parts:
-        one.wait_send()
-    R.P2[s] = jnp.concatenate(bottoms, axis=0).astype(BF)
+        piece = R.land_a[r].astype(F32)
+        tops.append(piece[:24])
+        bottoms.append(piece[24:])
+    R.PA[s] = jnp.concatenate(tops, axis=0).astype(BF)
+    gather_a.start()
+    R.PB[s] = jnp.concatenate(bottoms, axis=0).astype(BF)
+    move_x.arrive()
+    gather_x.start()
+    parts_b = to_group(R.stage_b, R.land_b, R.s_part_b)
+    for one in parts_b:
+        one.start()
+    for k in (1, 3, 2):
+        gather_o.forward(k)
     gather_x.forward()
+    move_m.start()
+    for k in (1, 3, 2):
+        gather_a.forward(k)
     gather_x.forward_far()
-    for k in (1, 3, 2):
-        gather_1.forward(k)
-    move_m.arrive()
-    gather_m.start()
-    gather_f.start()
-    gather_1.arrive()
-    move_d.arrive()
-    gather_d.start()
-
-    def unpack(pieces, whole, width):
-        for zz in range(4):
-
-            def one(i, carry):
-                lanes = pl.ds(pl.multiple_of(i * 256, 256), 256)
-                low = pieces[2 * zz, :, lanes].astype(F32)
-                high = pieces[2 * zz + 1, :, lanes].astype(F32)
-                for r in range(4):
-                    rows = slice(24 * r, 24 * r + 24)
-                    both = jnp.concatenate([low[rows], high[rows]], axis=0)
-                    whole[192 * r + 48 * zz : 192 * r + 48 * zz + 48, lanes] = both.astype(BF)
-                return carry
-
-            lax.fori_loop(0, width // 256, one, 0)
-
-    unpack(R.P1, R.W1, 1280)
-    gather_1.finish()
-    gain_rows = R.W1[:, 1152:1280].astype(F32).T
-    gain_one, gain_two, gain_three = (gain_rows[i : i + 1] for i in range(3))
-    gather_x.arrive()
-    gather_m.forward()
-    gather_m.forward_far()
-    gather_d.forward()
-    gather_2.start()
-    near_dn.wait()
-    gather_n.start()
+    gather_o.arrive()
+    whole_o.start()
+    gather_b.start()
+    for one in parts_b:
+        one.wait_recv()
+    for half in range(2):
+        rows = [R.land_b[r].astype(F32)[24 * half : 24 * half + 24] for r in range(4)]
+        R.P2[s, :, 512 * half : 512 * half + 512] = jnp.concatenate(rows, axis=0).astype(BF)
     move_t.arrive()
     end_one, end_two = R.TAB[0:1, 0:1], R.TAB[1:2, 0:1]
     plot_one, plot_two = R.TAB[2:3, 0:1], R.TAB[3:4, 0:1]
@@ -1130,15 +1131,35 @@
     R.info[1:2, :] = jnp.where(past_two, end_two, jnp.where(past_one, end_one, 0))
     R.info[2:3, :] = jnp.where(past_two, 0, jnp.where(past_one, plot_two, plot_one))
 
+    def unpack(pieces, whole, width, step):
+        for zz in range(4):
+
+            def one(i, carry):
+                lanes = pl.ds(pl.multiple_of(i * step, step), step)
+                low = pieces[2 * zz, :, lanes].astype(F32)
+                high = pieces[2 * zz + 1, :, lanes].astype(F32)
+                for r in range(4):
+                    rows = slice(24 * r, 24 * r + 24)
+                    both = jnp.concatenate([low[rows], high[rows]], axis=0)
+                    whole[192 * r + 48 * zz : 192 * r + 48 * zz + 48, lanes] = both.astype(BF)
+                return carry
+
+            lax.fori_loop(0, width // step, one, 0)
+
+    gather_a.arrive()
+    unpack(R.PA, R.WA, 640, 128)
+    gain_rows = R.WA[:, 512:640].astype(F32).T
+    gain_one, gain_two, gain_three = (gain_rows[64 + i : 65 + i] for i in range(3))
+
     def pair_rows(buf, i):
         return jnp.concatenate([buf[2 * i], buf[2 * i + 1]], axis=0)
 
     def mine_rows(buf):
         return jnp.concatenate([buf[2 * i + y] for i in range(4)], axis=0)
 
-    def keys_values(i, operand, columns, natural, turned):
+    def keys_values(i, operand, weight, natural, turned):
         rows = pl.ds(pl.multiple_of(i * 256, 256), 256)
-        product = dot(operand, R.W1[:, columns])
+        product = dot(operand, weight[:, :384])
         natural[rows, :] = product.astype(BF)
         turned[:, rows] = product.T.astype(BF)
 
@@ -1146,84 +1167,122 @@
         x1 = norm(pair_rows(R.X, i).astype(F32), gain_one)
         R.X1[2 * i] = x1[:128]
         R.X1[2 * i + 1] = x1[128:]
-        keys_values(i, x1, slice(384, 768), R.KV, R.KVT)
+        keys_values(i, x1, R.WA, R.KV, R.KVT)
         return carry
 
+    gather_x.arrive()
     lax.fori_loop(0, 4, first_norm, 0)
-    product = SCALE * dot(mine_rows(R.X1), R.W1[:, 768:1024])
+    product = SCALE * dot(mine_rows(R.X1), R.WA[:, 384:640])
     R.QT[...] = product.T[:192].astype(BF)
-    for k in (1, 3, 2):
-        gather_f.forward(k)
-
+
+    def share_heads(buf, sems):
+        return [Gather4(me, buf.at[:, h], sems.at[h]) for h in range(3)]
+
+    share_1 = share_heads(R.A4, R.s_share1)
+    move_m.arrive()
+    gather_m.start()
+    move_d.start()
     for h in range(3):
         attend_head(h, R.info, R.QT, R.KV, R.KVT, R.OUT1, R.LSE1, True)
+        R.A4[g, h] = R.OUT1[64 * h : 64 * h + 64, :].astype(BF)
+        share_1[h].start()
         if h == 0:
-            gather_f.arrive()
-            gather_ff.start()
+            whole_o.forward()
+            gather_b.forward(1)
+            gather_b.forward(3)
         if h == 1:
-            gather_2.forward(1)
-            gather_n.forward(1)
-            gather_2.forward(3)
-            gather_n.forward(3)
-    R.A4[g] = R.OUT1[...].astype(BF)
-    share_a = Gather4(me, R.A4, R.s_a)
-    share_a.start()
-    gather_ff.forward()
-    gather_2.forward(2)
-    gather_n.forward(2)
-    gather_m.arrive()
-
-    def memory_pair(i, carry):
-        keys_values(i, pair_rows(R.M, i), slice(0, 384), R.MKV, R.MKVT)
-        return carry
-
-    lax.fori_loop(0, 2, memory_pair, 0)
-    share_a.forward()
-    lax.fori_loop(2, 4, memory_pair, 0)
-    gather_ff.arrive()
-
-    def unpack_full(r, carry):
-        for zz in range(4):
-            low, high = R.FL[r, 2 * zz].astype(F32), R.FL[r, 2 * zz + 1].astype(F32)
-            rows = pl.ds(pl.multiple_of(192 * r + 48 * zz, 16), 48)
-            R.WF[rows, :QW] = jnp.concatenate([low[:24], high[:24]], axis=0).astype(BF)
-            R.WF[rows, QW:] = jnp.concatenate([low[24:], high[24:]], axis=0).astype(BF)
-        return carry
-
-    lax.fori_loop(0, 4, unpack_full, 0)
-    share_a.arrive()
+            share_1[0].forward()
+            gather_b.forward(2)
+            gather_m.forward()
+    gather_m.forward_far()
+    gather_c.start()
+    gather_2.start()
+    near_dn.wait()
+    share_1[1].forward()
+    whole_o.arrive()
+
+    def unpack_full(pieces, whole):
+        def one(r, carry):
+            for zz in range(4):
+                low, high = pieces[r, 2 * zz].astype(F32), pieces[r, 2 * zz + 1].astype(F32)
+                rows = pl.ds(pl.multiple_of(192 * r + 48 * zz, 16), 48)
+                whole[rows, :384] = jnp.concatenate([low[:24], high[:24]], axis=0).astype(BF)
+                whole[rows, 384:] = jnp.concatenate([low[24:], high[24:]], axis=0).astype(BF)
+            return carry
+
+        lax.fori_loop(0, 4, one, 0)
+
+    unpack_full(R.FO, R.WO)
+    share_1[2].forward()
+    gather_b.arrive()
+    unpack(R.PB, R.WB, 640, 128)
+    for one in share_1:
+        one.arrive()
 
     def project(pieces, weight, i):
         lanes = slice(256 * i, 256 * i + 256)
-        turned = pieces[:, :, lanes].astype(F32).reshape(768, 256)
-        return dot(turned.T.astype(BF), weight)
+        turned = pieces[:, :, :, lanes].astype(F32).reshape(768, 256)
+        return dot(turned.T.astype(BF), weight[...])
 
     for i in range(2):
         rows = slice(256 * i, 256 * i + 256)
         before = jnp.concatenate([R.X[4 * i + y], R.X[4 * i + 2 + y]], axis=0).astype(F32)
-        first = before + project(R.A4, R.WF[:, :768], i)
+        first = before + project(R.A4, R.WO, i)
         R.FIRST[rows, :] = first
         x2 = norm(first, gain_two)
         R.X2[rows, :] = x2
-        product = SCALE * dot(x2, R.W1[:, 896:1152])
-        R.CQT[:, rows] = product.T[64:].astype(BF)
+        product = SCALE * dot(x2, R.WB[:, 384:640])
+        R.CQT[:, rows] = product.T[:192].astype(BF)
+    gather_m.arrive()
+
+    def memory_pair(i, carry):
+        keys_values(i, pair_rows(R.M, i), R.WB, R.MKV, R.MKVT)
+        return carry
+
+    lax.fori_loop(0, 4, memory_pair, 0)
+    for k in (1, 3, 2):
+        gather_c.forward(k)
+    gather_n.start()
+    gather_q.start()
+    gather_c.arrive()
+    whole_c.start()
+    move_d.arrive()
+    share_2 = share_heads(R.C4, R.s_share2)
     for h in range(3):
         attend_head(h, R.info, R.CQT, R.MKV, R.MKVT, R.OUT2, R.LSE2, False)
-    R.C4[g] = R.OUT2[...].astype(BF)
-    share_c = Gather4(me, R.C4, R.s_c)
-    share_c.start()
+        R.C4[g, h] = R.OUT2[64 * h : 64 * h + 64, :].astype(BF)
+        if h == 0:
+            whole_c.forward()
+        share_2[h].start()
+        if h:
+            share_2[h - 1].forward()
+    gather_d.start()
+    for k in (1, 3, 2):
+        gather_2.forward(k)
+    share_2[2].forward()
+    whole_c.arrive()
+    unpack_full(R.FC, R.WC)
+    for one in share_2:
+        one.arrive()
+    for i in range(2):
+        rows = slice(256 * i, 256 * i + 256)
+        second = R.FIRST[rows, :] + project(R.C4, R.WC, i)
+        R.SECOND[rows, :] = second
+        R.X3[rows, :] = norm(second, gain_three)
+    gather_d.forward()
+    for k in (1, 3, 2):
+        gather_n.forward(k)
+    for k in (1, 3, 2):
+        gather_q.forward(k)
     gather_2.arrive()
-    unpack(R.P2, R.W2, 1024)
+    unpack(R.P2, R.W2, 1024, 256)
+    for one in parts_a + parts_b:
+        one.wait_send()
     gather_2.finish()
-    share_c.forward()
+    gather_a.finish()
+    gather_b.finish()
     gather_d.arrive()
     gather_n.arrive()
-    share_c.arrive()
-    for i in range(2):
-        rows = slice(256 * i, 256 * i + 256)
-        second = R.FIRST[rows, :] + project(R.C4, R.WF[:, 768:1536], i)
-        R.SECOND[rows, :] = second
-        R.X3[rows, :] = norm(second, gain_three)
 
     sum_dx = Sum4(me, R.DXP, R.by_c_dx, R.by_x_dx, R.s_dx)
     sum_out = Sum4(me, R.OP, R.by_c_out, R.by_x_out, R.s_out)
@@ -1249,6 +1308,11 @@
             R.DXP[2 * px + core] = dx3[half]
             R.OP[2 * px + core] = out[half]
 
+    def pack(whole, pieces, start, width):
+        for t in range(8):
+            rows = [whole[(8 * r + t) * 24 : (8 * r + t) * 24 + 24, :] for r in range(4)]
+            pieces[t, :, start : start + width] = jnp.concatenate(rows, axis=0).astype(BF)
+
     feed(1 - c)
     sum_dx.start()
     feed(c)
@@ -1257,167 +1321,174 @@
     own = pl.ds(pl.multiple_of(g * 128, 128), 128)
     own_block = 2 * g + y
     x3_t = R.X3[...].astype(F32).T.astype(BF)
-    R.W2G[...] = dot(x3_t, R.GG[:, :512])
+    total_2 = [
+        SumPlane(me, R.P2, R.by_y_2, R.by_z_2, R.s_g2.at[i], slice(512 * i, 512 * i + 512))
+        for i in range(2)
+    ]
+    for i in range(2):
+        R.W2G[...] = dot(x3_t, R.GG[:, 512 * i : 512 * i + 512])
+        pack(R.W2G, R.P2, 512 * i, 512)
+        total_2[i].start()
+    hidden_t = R.H[...].astype(F32).T.astype(BF)
+    d_down = dot(hidden_t, R.DO[...].reshape(512, 768)).astype(BF)
+    for t in range(8):
+        R.DNG[t] = d_down[64 * t : 64 * t + 64]
+    total_n = SumPlane(me, R.DNG, R.by_y_n, R.by_z_n, R.s_gn)
+    total_n.start()
     part, gain_grad_three = norm_back(R.SECOND[own, :], gain_three, sum_dx.end())
     second_grad = R.DO[g].astype(F32) + part
     R.SGRAD[...] = second_grad
     R.DS4[g] = second_grad.astype(BF)
     share_s = Gather4(me, R.DS4, R.s_s)
     share_s.start()
-
-    def pack(whole, pieces, start, width):
-        for t in range(8):
-            rows = [whole[(8 * r + t) * 24 : (8 * r + t) * 24 + 24, :] for r in range(4)]
-            pieces[t, :, start : start + width] = jnp.concatenate(rows, axis=0).astype(BF)
-
-    pack(R.W2G, R.P2, 0, 512)
+    sum_out.to_x()
+    gather_q.arrive()
+    whole_q.start()
     share_s.forward()
-    R.W2G[...] = dot(x3_t, R.GG[:, 512:])
-    pack(R.W2G, R.P2, 512, 512)
-    hidden_t = R.H[...].astype(F32).T.astype(BF)
-    d_down = dot(hidden_t, R.DO[...].reshape(512, 768)).astype(BF)
-    for t in range(8):
-        R.DNG[t] = d_down[64 * t : 64 * t + 64]
-    total_2 = SumPlane(me, R.P2, R.by_y_2, R.by_z_2, R.s_g2)
-    total_n = SumPlane(me, R.DNG, R.by_y_n, R.by_z_n, R.s_gn)
     share_s.arrive()
-    total_2.start()
-    total_n.start()
 
     dsec = R.DS4[...].reshape(512, 768)
     mine_192 = pl.ds(pl.multiple_of(g * 192, 16), 192)
-    R.OUTER[...] = dot_nt(R.WF[mine_192, 768:1536], dsec).astype(BF)
+    R.OUTER[...] = dot_nt(R.WC[mine_192, :], dsec).astype(BF)
+    share_3 = share_heads(R.DC4, R.s_share3)
     for h in range(3):
         attend_back_head(
             h, R.info, R.CQT, R.MKV, R.MKVT, R.OUTER, R.OUT2, R.LSE2, R.DCQT, R.MDKV, R.dk, R.dv, False
         )
-    R.DC4[g] = R.DCQT[...]
-    share_q = Gather4(me, R.DC4, R.s_q)
-    share_q.start()
-    sum_out.to_x()
+        if h == 0:
+            whole_q.forward()
+        R.DC4[g, h] = R.DCQT[64 * h : 64 * h + 64, :]
+        share_3[h].start()
+        if h:
+            share_3[h - 1].forward()
 
     def pack_24(whole, pieces):
         for t in range(8):
             rows = whole[24 * t : 24 * t + 24]
             pieces[t] = jnp.concatenate([rows[:, :384], rows[:, 384:]], axis=0).astype(BF)
 
-    pack_24(dot(R.C4[g], dsec), R.CO8)
+    whole_q.arrive()
+    unpack_full(R.FQ, R.WQ)
+    pack_24(dot(R.C4[g].reshape(192, 512), dsec), R.CO8)
     total_c = SumPlane(me, R.CO8, R.by_y_c, R.by_z_c, R.s_gc)
     total_c.start()
-    total_2.fold()
-    total_n.fold()
-
-    def memory_grad_pair(i, carry):
-        lanes = pl.ds(pl.multiple_of(i * 256, 256), 256)
-        turned = dot(R.W1[:, :384], R.MDKV[:, lanes]).astype(BF)
-        R.MG[2 * i] = turned[:, :128]
-        R.MG[2 * i + 1] = turned[:, 128:]
-        return carry
-
-    lax.fori_loop(0, 2, memory_grad_pair, 0)
-    share_q.forward()
-    lax.fori_loop(2, 4, memory_grad_pair, 0)
-    sum_m = Sum8(me, R.MG, R.by_c_m, R.by_y_m, R.by_x_m, R.s_gm)
-    sum_m.start()
-    share_q.arrive()
+    share_3[2].forward()
+    for one in share_3:
+        one.arrive()
 
     for i in range(2):
         rows = slice(256 * i, 256 * i + 256)
-        turned = R.DC4[:, :, rows].reshape(768, 256)
-        dx2 = dot(R.WF[:, 1536:], turned).T
+        dx2 = dot(R.WQ[...], R.DC4[:, :, :, rows].reshape(768, 256)).T
         part, ignored = norm_back(R.FIRST[rows, :], gain_two, dx2)
         R.DFIRST[rows, :] = (dsec[rows].astype(F32) + part).astype(BF)
-    dx2 = dot(R.WF[:, 1536:], R.DC4[:, :, own].reshape(768, 128)).T
+    dx2 = dot(R.WQ[...], R.DC4[:, :, :, own].reshape(768, 128)).T
     part, gain_grad_two = norm_back(R.FIRST[own, :], gain_two, dx2)
     R.SGRAD[...] += part
 
-    R.OUTER[...] = dot_nt(R.WF[mine_192, :768], R.DFIRST[...]).astype(BF)
-    sum_m.to_y()
+    R.OUTER[...] = dot_nt(R.WO[mine_192, :], R.DFIRST[...]).astype(BF)
     for h in range(3):
         attend_back_head(
             h, R.info, R.QT, R.KV, R.KVT, R.OUTER, R.OUT1, R.LSE1, R.DQT, R.DKV, R.dk, R.dv, True
         )
-        if h == 0:
-            total_c.fold()
-            sum_m.to_x()
 
     def token_grad_pair(i, carry):
         lanes = pl.ds(pl.multiple_of(i * 256, 256), 256)
         half = pl.ds(pl.multiple_of(i * 128, 128), 128)
-        turned = dot(R.W1[:, 384:768], R.DKV[:, lanes])
-        query = dot(R.W1[:, 768:960], R.DQT[:, half])
+        turned = dot(R.WA[:, :384], R.DKV[:, lanes])
+        query = dot(R.WA[:, 384:576], R.DQT[:, half])
         R.TG[2 * i] = (turned[:, :128] + jnp.where(y == 0, query, 0.0)).astype(BF)
         R.TG[2 * i + 1] = (turned[:, 128:] + jnp.where(y == 1, query, 0.0)).astype(BF)
         return carry
 
     lax.fori_loop(0, 4, token_grad_pair, 0)
-    sum_t = Sum8(me, R.TG, R.by_c_t, R.by_y_t, R.by_x_t, R.s_gt)
+    sum_t = Sum8(me, R.TG, R.by_c_t, R.by_x_t, R.by_y_t, R.s_gt)
     sum_t.start()
-    memory_t = dot(R.MDKV[...], R.M[...].reshape(1024, 768))
-    R.W1G[...] = memory_t.T
-    pack(R.W1G, R.P1, 0, 384)
-    total_1a = SumPlane(me, R.P1, R.by_y_1, R.by_z_1, R.s_g1a, slice(0, 384))
-    total_1a.start()
+    R.W1G[...] = dot(R.DKV[...], R.X1[...].reshape(1024, 768)).T
+    pack(R.W1G, R.PA, 0, 384)
+    total_a = SumPlane(me, R.PA, R.by_y_a, R.by_z_a, R.s_ga, slice(0, 384))
+    sum_t.to_x()
+    total_a.start()
+
+    def memory_grad_pair(i, carry):
+        lanes = pl.ds(pl.multiple_of(i * 256, 256), 256)
+        turned = dot(R.WB[:, :384], R.MDKV[:, lanes]).astype(BF)
+        R.MG[2 * i] = turned[:, :128]
+        R.MG[2 * i + 1] = turned[:, 128:]
+        return carry
+
+    lax.fori_loop(0, 4, memory_grad_pair, 0)
+    sum_m = Sum8(me, R.MG, R.by_c_m, R.by_x_m, R.by_y_m, R.s_gm)
+    sum_m.start()
+    R.W1G[...] = dot(R.MDKV[...], R.M[...].reshape(1024, 768)).T
+    pack(R.W1G, R.PB, 0, 384)
+    R.TURN[:192, :] = dot(R.DCQT[...], R.X2[...])
+    R.TURN[192:, :] = jnp.zeros((64, 768), F32)
+    pack(R.TURN[...].T, R.PB, 384, 256)
+    total_b = SumPlane(me, R.PB, R.by_y_b, R.by_z_b, R.s_gb)
+    R.TURN[:192, :] = dot(R.DQT[...], mine_rows(R.X1))
+    pack_24(dot(R.A4[g].reshape(192, 512), R.DFIRST[...]), R.SO8)
+    total_s = SumPlane(me, R.SO8, R.by_y_s, R.by_z_s, R.s_gs)
+    for one in total_2:
+        one.fold()
+    total_n.fold()
+    total_c.fold()
     sum_t.to_y()
-    turned = dot(R.DKV[...], R.X1[...].reshape(1024, 768))
-    R.W1G[...] = turned.T
-    pack(R.W1G, R.P1, 384, 384)
-    sum_t.to_x()
-    R.TURN[:192, :] = dot(R.DQT[...], mine_rows(R.X1))
-    R.TURN[192:, :] = dot(R.DCQT[...], R.X2[...])
-    R.W1G[...] = R.TURN[...].T
-    pack(R.W1G, R.P1, 768, 384)
-    pack_24(dot(R.A4[g], R.DFIRST[...]), R.SO8)
+    sum_m.to_x()
+    total_b.start()
+    total_s.start()
+    total_a.fold()
     dx1 = sum_t.end().T
     part, gain_grad_one = norm_back(R.X[own_block].astype(F32), gain_one, dx1)
-    gain_grads = jnp.concatenate(
-        [gain_grad_one, gain_grad_two, gain_grad_three, jnp.zeros((125, 768), F32)], axis=0
-    )
-    R.GAINS[...] = gain_grads.T
-    pack(R.GAINS, R.P1, 1152, 128)
-    total_1b = SumPlane(me, R.P1, R.by_y_1, R.by_z_1, R.s_g1b, slice(384, 1280))
-    total_s = SumPlane(me, R.SO8, R.by_y_s, R.by_z_s, R.s_gs)
-    total_1b.start()
-    total_s.start()
+    R.TURN[192:193, :] = gain_grad_one
+    R.TURN[193:194, :] = gain_grad_two
+    R.TURN[194:195, :] = gain_grad_three
+    pack(R.TURN[...].T, R.PA, 384, 256)
+    total_g = SumPlane(me, R.PA, R.by_y_a, R.by_z_a, R.s_gg, slice(384, 640))
+    total_g.start()
     R.TBLOCK[...] = (R.SGRAD[...] + part).astype(BF)
     R.LBLOCK[...] = (R.SECOND[own, :] + sum_out.end()).astype(BF)
-    R.MBLOCK[...] = sum_m.end().T.astype(BF)
     back = [
         Move(me, src, dst, R.s_back.at[i], back=True)
         for i, (src, dst) in enumerate(
             ((R.TBLOCK, R.tokens_out), (R.LBLOCK, R.layer_out), (R.MBLOCK, R.memory_out))
         )
     ]
-    for one in back:
+    back[0].start()
+    back[1].start()
+    sum_m.to_y()
+    total_b.fold()
+    total_s.fold()
+    total_g.fold()
+    for one in total_2:
+        one.end()
+    rows_2 = R.P2[s].astype(F32)
+    for r in range(4):
+        rows = slice(24 * r, 24 * r + 24)
+        R.stage_b[r] = jnp.concatenate([rows_2[rows, :512], rows_2[rows, 512:]], axis=0).astype(BF)
+    last_b = to_group(R.stage_b, R.quarters_b, R.s_last_b)
+    for one in last_b:
         one.start()
-    total_1a.fold()
-    total_1b.fold()
-    total_s.fold()
-    total_2.end()
+    R.MBLOCK[...] = sum_m.end().T.astype(BF)
+    back[2].start()
     total_n.end()
     total_c.end()
-    total_1a.end()
-    total_1b.end()
-    first_rows = R.P1[s].astype(F32)
-    last_rows = R.P2[s].astype(F32)
+    total_a.end()
+    total_b.end()
+    total_g.end()
+    rows_a, rows_b = R.PA[s].astype(F32), R.PB[s].astype(F32)
     for r in range(4):
         rows = slice(24 * r, 24 * r + 24)
-        bottom = jnp.concatenate([last_rows[rows], first_rows[rows, 1152:]], axis=1)
-        R.stage[r] = jnp.concatenate([first_rows[rows, :1152], bottom], axis=0).astype(BF)
-    finals = [
-        remote(
-            R.stage.at[2 * to[0] + to[1]], R.quarters_out.at[g], R.s_last.at[0, i], R.s_last.at[1, i], to
-        )
-        for i, to in enumerate(group)
-    ]
-    for one in finals:
+        R.stage_a[r] = jnp.concatenate([rows_a[rows], rows_b[rows]], axis=0).astype(BF)
+    last_a = to_group(R.stage_a, R.quarters_a, R.s_last_a)
+    for one in last_a:
         one.start()
     total_s.end()
     near = [
         pltpu.make_async_copy(src, dst, R.s_near.at[1 + i])
         for i, (src, dst) in enumerate(
             (
-                (R.stage.at[g], R.quarters_out.at[g]),
+                (R.stage_a.at[g], R.quarters_a.at[g]),
+                (R.stage_b.at[g], R.quarters_b.at[g]),
                 (R.CO8.at[s], R.co_out),
                 (R.SO8.at[s], R.so_out),
                 (R.DNG.at[s], R.down_out),
@@ -1428,20 +1499,22 @@
         one.start()
     for one in near:
         one.wait()
-    for one in finals:
+    for one in last_a + last_b:
         one.wait_recv()
     for one in back:
         one.arrive()
         one.finish()
-    for one in finals:
+    for one in last_a + last_b:
         one.wait_send()
     for one in (move_x, move_t, move_m, move_d):
         one.finish()
-    for one in (gather_x, gather_m, gather_d, gather_f, gather_n, gather_ff):
+    for one in (gather_x, gather_m, gather_d, gather_o, gather_c, gather_q, gather_n):
         one.finish()
-    for one in (share_a, share_c, share_s, share_q, sum_dx, sum_out, sum_m, sum_t):
+    for one in (whole_o, whole_c, whole_q, share_s, sum_dx, sum_out, sum_m, sum_t):
         one.finish()
-    for one in (total_1a, total_1b, total_2, total_n, total_c, total_s):
+    for one in share_1 + share_2 + share_3 + total_2:
+        one.finish()
+    for one in (total_a, total_g, total_b, total_n, total_c, total_s):
         one.finish()
 
 
@@ -1455,7 +1528,8 @@
         return pltpu.VMEM(shape, F32)
 
     outs = dict(
-        quarters_out=(4, 48, QW),
+        quarters_a=(4, 48, 640),
+        quarters_b=(4, 48, 512),
         co_out=(48, 384),
         so_out=(48, 384),
         down_out=(64, d),
@@ -1464,16 +1538,18 @@
         memory_out=(n, d),
     )
     scratch = dict(
-        stage=low(4, 48, QW), land=low(4, 48, QW),
-        X=low(8, n, d), M=low(8, n, d), DO=low(4, n, d), TAB=pltpu.VMEM((8, 128), jnp.int32),
-        P1=low(8, 96, 1280), P2=low(8, 96, 1024), FL=low(4, 8, 48, QW), DN=low(8, 64, d),
-        W1=low(768, 1280), W2=low(768, 1024), WF=low(768, 2304),
+        stage_a=low(4, 48, 640), land_a=low(4, 48, 640), stage_b=low(4, 48, 512), land_b=low(4, 48, 512),
+        tabs=pltpu.VMEM((8, 128), jnp.int32), TAB=pltpu.VMEM((8, 128), jnp.int32),
+        X=low(8, n, d), M=low(8, n, d), DO=low(4, n, d),
+        PA=low(8, 96, 640), PB=low(8, 96, 640), P2=low(8, 96, 1024), DN=low(8, 64, d),
+        FO=low(4, 8, 48, 384), FC=low(4, 8, 48, 384), FQ=low(4, 8, 48, 384),
+        WA=low(768, 640), WB=low(768, 640), W2=low(768, 1024), WO=low(d, d), WC=low(d, d), WQ=low(d, d),
         info=pltpu.VMEM((8, 512), jnp.int32),
         X1=low(8, n, d), X2=low(512, d), X3=low(512, d),
         KV=low(1024, 384), KVT=low(384, 1024), MKV=low(1024, 384), MKVT=low(384, 1024),
         QT=low(192, 512), CQT=low(192, 512), OUT1=full(192, 512), OUT2=full(192, 512),
         LSE1=full(8, 512), LSE2=full(8, 512),
-        A4=low(4, 192, 512), C4=low(4, 192, 512), DC4=low(4, 192, 512),
+        A4=low(4, 3, 64, 512), C4=low(4, 3, 64, 512), DC4=low(4, 3, 64, 512),
         FIRST=full(512, d), SECOND=full(512, d),
         H=low(512, 512), GG=low(512, 1024), DXP=low(4, n, d), OP=low(4, n, d),
         by_c_dx=low(2, n, d), by_x_dx=low(n, d), by_c_out=low(2, n, d), by_x_out=low(n, d),
@@ -1484,18 +1560,18 @@
         dk=full(64, 1024), dv=full(64, 1024),
         CO8=low(8, 48, 384), by_y_c=low(4, 48, 384), by_z_c=low(3, 48, 384),
         SO8=low(8, 48, 384), by_y_s=low(4, 48, 384), by_z_s=low(3, 48, 384),
-        MG=low(8, d, n), by_c_m=low(2, 2, d, n), by_y_m=low(2, d, n), by_x_m=low(d, n),
-        TG=low(8, d, n), by_c_t=low(2, 2, d, n), by_y_t=low(2, d, n), by_x_t=low(d, n),
-        DFIRST=low(512, d),
-        W1G=full(768, 384), TURN=full(384, 768), GAINS=full(768, 128),
-        by_y_1=low(4, 96, 1280), by_z_1=low(3, 96, 1280),
+        MG=low(8, d, n), by_c_m=low(2, 2, d, n), by_x_m=low(2, d, n), by_y_m=low(d, n),
+        TG=low(8, d, n), by_c_t=low(2, 2, d, n), by_x_t=low(2, d, n), by_y_t=low(d, n),
+        DFIRST=low(512, d), W1G=full(768, 384), TURN=full(256, 768),
+        by_y_a=low(4, 96, 640), by_z_a=low(3, 96, 640), by_y_b=low(4, 96, 640), by_z_b=low(3, 96, 640),
         TBLOCK=low(n, d), LBLOCK=low(n, d), MBLOCK=low(n, d),
-        s_move=dma(4, 2), s_near=dma(5), s_part=dma(2, 3), s_last=dma(2, 3), s_back=dma(3, 2),
-        s_x=dma(14), s_m=dma(14), s_d=dma(6), s_ff=dma(6),
-        s_1=dma(2, 7), s_2=dma(2, 7), s_f=dma(2, 7), s_n=dma(2, 7),
-        s_a=dma(6), s_c=dma(6), s_s=dma(6), s_q=dma(6),
+        s_move=dma(4, 2), s_near=dma(6), s_part_a=dma(2, 3), s_part_b=dma(2, 3),
+        s_last_a=dma(2, 3), s_last_b=dma(2, 3), s_back=dma(3, 2),
+        s_x=dma(14), s_m=dma(14), s_d=dma(6), s_wo=dma(6), s_wc=dma(6), s_wq=dma(6), s_s=dma(6),
+        s_a=dma(2, 7), s_b=dma(2, 7), s_2=dma(2, 7), s_n=dma(2, 7), s_fo=dma(2, 7), s_fc=dma(2, 7), s_fq=dma(2, 7),
+        s_share1=dma(3, 6), s_share2=dma(3, 6), s_share3=dma(3, 6),
         s_dx=dma(2, 3), s_out=dma(2, 3), s_gm=dma(2, 7), s_gt=dma(2, 7),
-        s_g1a=dma(2, 7), s_g1b=dma(2, 7), s_g2=dma(2, 7), s_gn=dma(2, 7), s_gc=dma(2, 7), s_gs=dma(2, 7),
+        s_ga=dma(2, 7), s_gb=dma(2, 7), s_gg=dma(2, 7), s_g2=dma(2, 2, 7), s_gn=dma(2, 7), s_gc=dma(2, 7), s_gs=dma(2, 7),
     )
     names = tuple(inputs) + tuple(outs) + tuple(scratch)
     return pl.pallas_call(
@@ -1511,6 +1587,33 @@
     )(*[a for a, _ in inputs.values()])
 
 
+def outputs_kernel(
+    qa, qb, co, so, down, tokens, layer, memory,
+    layer_out, tokens_out, memory_out, gains_out,
+    sq, sk, sv, so_out, cq, ck, cv, co_out, gate, up, down_out,
+):
+    layer_out[...] = layer[...]
+    tokens_out[...] = tokens[...]
+    memory_out[...] = memory[...]
+    down_out[...] = down[...].astype(F32)
+    gains = jnp.zeros((24, 128), F32)
+    for k in range(4):
+        piece = qa[k].astype(F32)
+        gains = gains + piece[:24, 512:]
+        narrow = slice(192 * k, 192 * k + 192)
+        for row, outs in ((0, (sk, sv, sq)), (24, (ck, cv, cq))):
+            for i, out in enumerate(outs):
+                out[:, narrow] = piece[row : row + 24, 192 * i : 192 * i + 192]
+        piece = qb[k].astype(F32)
+        gate[:, 512 * k : 512 * k + 512] = piece[:24]
+        up[:, 512 * k : 512 * k + 512] = piece[24:]
+    gains_out[...] = gains
+    for piece, out in ((so, so_out), (co, co_out)):
+        rows = piece[...].astype(F32)
+        out[:, :384] = rows[:24]
+        out[:, 384:] = rows[24:]
+
+
 def body_planes(
     tokens, memory, out_grad, table_lengths, table_plots,
     self_gain, self_query, self_key, self_value, self_output,
@@ -1518,35 +1621,34 @@
     mlp_gain, mlp_gate, mlp_up, mlp_down,
 ):
     gains = jnp.stack([self_gain, cross_gain, mlp_gain], axis=1)
-    gains = jnp.pad(gains, ((0, 0), (0, 125)))
-    ends = running_sum(table_lengths)
-    tab = jnp.concatenate([ends[0], table_plots[0], jnp.zeros((4,), jnp.int32)])
-    tab = jnp.broadcast_to(tab[:, None], (8, 128))
-    oa, co, so, down, tokens_mine, layer_mine, memory_mine = run_layer(
+    gains = jnp.pad(gains, ((0, 0), (0, 61)))
+    in_smem = pl.BlockSpec(memory_space=pltpu.SMEM)
+    results = run_layer(
         dict(
             tok=(tokens[0], ANYWHERE), mem=(memory[0], ANYWHERE), dout=(out_grad[0], ANYWHERE),
-            tab=(tab, IN_VMEM), gains=(gains, IN_VMEM),
+            lengths=(table_lengths, in_smem), plots=(table_plots, in_smem), gains=(gains, IN_VMEM),
             sq=(self_query, IN_VMEM), sk=(self_key, IN_VMEM), sv=(self_value, IN_VMEM), so=(self_output, IN_VMEM),
             cq=(cross_query, IN_VMEM), ck=(cross_key, IN_VMEM), cv=(cross_value, IN_VMEM), co=(cross_output, IN_VMEM),
             gate=(mlp_gate, IN_VMEM), up=(mlp_up, IN_VMEM), down=(mlp_down, ANYWHERE),
         )
     )
-    oa = oa.astype(F32)
-
-    def columns(top, start, width):
-        part = oa[:, 24 * top : 24 * top + 24, start : start + width]
-        return jnp.moveaxis(part, 0, 1).reshape(24, 4 * width)
-
-    def halves(a):
-        a = a.astype(F32)
-        return jnp.concatenate([a[:24], a[24:]], axis=1)
-
-    gain_sum = jnp.sum(oa[:, 24:, 1024:1027], axis=0)
+    block = jax.ShapeDtypeStruct((128, 768), BF)
+    rows = jax.ShapeDtypeStruct((24, 768), F32)
+    wide = jax.ShapeDtypeStruct((24, 2048), F32)
+    outs = pl.pallas_call(
+        outputs_kernel,
+        out_shape=(block,) * 3
+        + (jax.ShapeDtypeStruct((24, 128), F32),)
+        + (rows,) * 8
+        + (wide, wide, jax.ShapeDtypeStruct((64, 768), F32)),
+        name="outputs",
+    )(*results)
+    layer, tokens_mine, memory_mine, gain_sums, sq, sk, sv, so, cq, ck, cv, co, gate, up, down = outs
     return (
-        layer_mine[None], tokens_mine[None], memory_mine[None],
-        gain_sum[:, 0], columns(0, 768, 192), columns(0, 384, 192), columns(0, 576, 192), halves(so),
-        gain_sum[:, 1], columns(0, 960, 192), columns(0, 0, 192), columns(0, 192, 192), halves(co),
-        gain_sum[:, 2], columns(1, 0, 512), columns(1, 512, 512), down.astype(F32),
+        layer[None], tokens_mine[None], memory_mine[None],
+        gain_sums[:, 64], sq, sk, sv, so,
+        gain_sums[:, 65], cq, ck, cv, co,
+        gain_sums[:, 66], gate, up, down,
     )
 
 

time: 279 us -> 238 us (0.85); the launches traced: 277 us -> 233 us
  Pallas kernels: 260 us -> 230 us
  local copies, waits for them, and re-layouts: 14.1 us -> 2.8 us
    pallas_call x1, Pallas kernels: 260 us -> 227 us  [run_layer(): pl.pallas_call(functools.partial(layer_kernel, names), out_shape=tuple((j...]
    reshape x8 -> x0, local copies, waits for them, and re-layouts: 5.81 us -> none  [columns(): return jnp.moveaxis(part, 0, 1).reshape(24, 4 * width)]
    unnamed x24 -> x8, local copies, waits for them, and re-layouts: 4.92 us -> 1.36 us
where the time goes in v1:
time: 238 us; the launch traced here: 233 us
  Pallas kernels  230 us (97%)
  local copies, waits for them, and re-layouts  2.8 us (1%)
    pallas_call x1, Pallas kernels, run_layer(): pl.pallas_call(functools.partial(layer_kernel, names), out_shape=tuple((j...  227 us

profile of v1, /device:TPU:0, one launch (start us, length us, event | category | flops | bytes accessed | tf_op | source)
XLA Modules:
  0.0 233.1 jit_solution(8370842206009773371)
XLA Ops:
  0.7 0.0 copy-start.1
  0.7 0.0 copy-start.2
  0.7 0.0 copy-start.3
  0.7 0.6 copy-done.1
  1.3 0.0 copy-done.2
  1.3 0.0 copy-done.3
  1.4 0.1 copy.42
  1.5 0.6 pad.4.refs_5_
  2.1 227.0 %layer.1 = (bf16[4,48,640]{2,1,0:T(8,128)(2,1)}, bf16[4,48,512]{2,1,0:T(8,128)(2,1)}, bf16[48,384]{1,0:T(8,128)(2,1)}, bf16[48,384]{1,0:T(8,128)(2,1)}, bf16[64,...) custom-call(bf16[128,768]{1,0:T(8,128)(2,1)} %bitcast.9, ...), custom_call_target="tpu_custom_call" | custom-call | tf_op jit(solution)/shard_map/layer/pallas_call | solution.py:1577
  229.1 2.6 %outputs.1 = (bf16[128,768]{1,0:T(8,128)(2,1)}, bf16[128,768]{1,0:T(8,128)(2,1)}, bf16[128,768]{1,0:T(8,128)(2,1)}, f32[24,128]{1,0:T(8,128)}, f32[24,768]{1,0:T...) custom-call(bf16[4,48,640]{2,1,0:T(8,128)(2,1)} %get-tuple-element.4, ...), custom_call_target="tpu_custom_call" | custom-call | tf_op jit(solution)/shard_map/outputs/pallas_call | solution.py:1638
  231.7 0.0 copy-start
  231.7 0.7 copy-done
  232.4 0.7 slice_reduce_fusion
  (1 shorter events, 0.0 us)
Async XLA Ops:
  0.7 0.7 copy-start.1
  0.7 0.7 copy-start.2
  0.7 0.7 copy-start.3
  231.7 0.7 copy-start

commit v2 on v1

--- a/solution.py
+++ b/solution.py
@@ -668,11 +668,9 @@
 
 
 class Gather8:
-    def __init__(self, me, buf, sems):
+    def __init__(self, me, buf, sems, split=False):
         x, c, y, z = me
         xp, cp, yp = (1 - x, c, y, z), (x, 1 - c, y, z), (x, c, 1 - y, z)
-        self.c = c
-
         def piece(px, pc, py):
             return buf.at[2 * (2 * px + pc) + py]
 
@@ -687,32 +685,39 @@
         self.c_x = send(at_x, 3, cp)
         self.c_y = send(at_y, 4, cp)
         self.c_d = send(at_d, 5, cp)
+        self.d_by_x = send(at_y, 6, xp)
         self.d_by_y = send(at_x, 6, yp)
-        self.d_by_x = send(at_y, 6, xp)
+        self.by_y = jnp.logical_and(c == 0, split)
 
     def start(self):
+        self.start_x()
+        self.start_y()
+
+    def start_x(self):
         self.x_own.start()
+        self.c_own.start()
+
+    def start_y(self):
         self.y_own.start()
-        self.c_own.start()
 
     def forward(self):
+        self.y_own.wait_recv()
+
+        @pl.when(jnp.logical_not(self.by_y))
+        def _():
+            self.d_by_x.start()
+
+        self.c_y.start()
         self.x_own.wait_recv()
 
-        @pl.when(self.c == 0)
+        @pl.when(self.by_y)
         def _():
             self.d_by_y.start()
 
         self.c_x.start()
-        self.y_own.wait_recv()
-
-        @pl.when(self.c == 1)
-        def _():
-            self.d_by_x.start()
-
-        self.c_y.start()
 
     def forward_far(self):
-        self.d_by_y.wait_recv()
+        self.d_by_x.wait_recv()
         self.c_d.start()
 
     def arrive(self):
@@ -720,7 +725,7 @@
             one.wait_recv()
 
     def finish(self):
-        for one in (self.x_own, self.y_own, self.c_own, self.c_x, self.c_y, self.c_d, self.d_by_y):
+        for one in (self.x_own, self.y_own, self.c_own, self.c_x, self.c_y, self.c_d, self.d_by_x):
             one.wait_send()
 
 
@@ -753,11 +758,11 @@
 
 
 class GatherPlane:
-    def __init__(self, me, buf, sems):
+    def __init__(self, me, buf, sems, lanes=None):
         x, c, y, z = me
 
         def send(p, k, to):
-            piece = buf.at[2 * p + y]
+            piece = buf.at[2 * p + y] if lanes is None else buf.at[2 * p + y, :, lanes]
             return remote(piece, piece, sems.at[0, k], sems.at[1, k], to)
 
         yp = (x, c, 1 - y, z)
@@ -765,9 +770,11 @@
         self.across = [send(z, 3, yp)]
         self.across += [send(lax.rem(z + 4 - k, 4), 3 + k, yp) for k in (1, 2, 3)]
 
-    def start(self):
+    def start_along(self):
         for one in self.along:
             one.start()
+
+    def start_across(self):
         self.across[0].start()
 
     def forward(self, k):
@@ -783,52 +790,203 @@
             one.wait_send()
 
 
+class GatherRelay:
+    def __init__(self, me, buf, sems, lanes=None):
+        self.me, self.buf, self.sems, self.lanes = me, buf, sems, lanes
+
+    def piece(self, p, y):
+        return self.buf.at[2 * p + y] if self.lanes is None else self.buf.at[2 * p + y, :, self.lanes]
+
+    def send(self, p, k, to):
+        piece = self.piece(p, self.me[2])
+        return remote(piece, piece, self.sems.at[0, k + p], self.sems.at[1, k + p], to)
+
+    def up(self, p):
+        x, c, y, z = self.me
+        return self.send(p, 0, (x, c, y, z + 1))
+
+    def down(self, p):
+        x, c, y, z = self.me
+        return self.send(p, 4, (x, c, y, z - 1))
+
+    def across(self, p):
+        x, c, y, z = self.me
+        return self.send(p, 8, (x, c, 1 - y, z))
+
+    def start_along(self):
+        z = self.me[3]
+
+        @pl.when(z < 3)
+        def _():
+            self.up(z).start()
+
+        @pl.when(z > 0)
+        def _():
+            self.down(z).start()
+
+    def start_across(self):
+        self.across(self.me[3]).start()
+
+    def forward(self, k):
+        z = self.me[3]
+
+        @pl.when(z - k >= 0)
+        def _():
+            p = z - k
+            self.up(p).wait_recv()
+            if k < 3:
+
+                @pl.when(z < 3)
+                def _():
+                    self.up(p).start()
+
+            self.across(p).start()
+
+        @pl.when(z + k <= 3)
+        def _():
+            p = z + k
+            self.down(p).wait_recv()
+            if k < 3:
+
+                @pl.when(z > 0)
+                def _():
+                    self.down(p).start()
+
+            self.across(p).start()
+
+    def arrive(self):
+        for p in range(4):
+            self.across(p).wait_recv()
+
+    def finish(self):
+        z = self.me[3]
+        for p in range(4):
+            self.across(p).wait_send()
+
+            @pl.when(jnp.logical_and(z < 3, p <= z))
+            def _():
+                self.up(p).wait_send()
+
+            @pl.when(jnp.logical_and(z > 0, p >= z))
+            def _():
+                self.down(p).wait_send()
+
+
 class SumPlane:
     def __init__(self, me, parts, by_y, by_z, sems, lanes=None):
-        x, c, y, z = me
-        self.y, self.z = y, z
-        lanes = slice(None) if lanes is None else lanes
-        self.mine = [parts.at[2 * lax.rem(z + k, 4) + y, :, lanes] for k in range(4)]
-        self.by_y = [by_y.at[lax.rem(z + k, 4), :, lanes] for k in range(4)]
-        self.by_z = [by_z.at[k, :, lanes] for k in range(3)]
-
-        def theirs(k):
-            return parts.at[2 * lax.rem(z + k, 4) + 1 - y, :, lanes]
-
-        yp = (x, c, 1 - y, z)
-        self.across = [
-            remote(theirs(k), self.by_y[k], sems.at[0, k], sems.at[1, k], yp) for k in range(4)
-        ]
-        self.along = [
-            remote(
-                self.mine[k],
-                self.by_z[k - 1],
-                sems.at[0, 3 + k],
-                sems.at[1, 3 + k],
-                (x, c, y, lax.rem(z + k, 4)),
-            )
-            for k in (1, 2, 3)
-        ]
+        self.me, self.parts, self.by_y, self.by_z, self.sems = me, parts, by_y, by_z, sems
+        self.lanes = slice(None) if lanes is None else lanes
+
+    def mine(self, p):
+        return self.parts.at[2 * p + self.me[2], :, self.lanes]
+
+    def from_y(self, p):
+        return self.by_y.at[p, :, self.lanes]
+
+    def slot(self, k):
+        return self.by_z.at[k, :, self.lanes]
+
+    def across(self, p):
+        x, c, y, z = self.me
+        theirs = self.parts.at[2 * p + 1 - y, :, self.lanes]
+        return remote(theirs, self.from_y(p), self.sems.at[0, p], self.sems.at[1, p], (x, c, 1 - y, z))
+
+    def up_slot(self, p):
+        return self.slot(p - 1)
+
+    def down_slot(self, q):
+        return self.slot(lax.rem(3 + q, 5))
+
+    def up(self, p):
+        x, c, y, z = self.me
+        k = 3 + p
+        return remote(self.mine(p), self.up_slot(p), self.sems.at[0, k], self.sems.at[1, k], (x, c, y, z + 1))
+
+    def down(self, q):
+        x, c, y, z = self.me
+        k = 7 + q
+        return remote(self.mine(q), self.down_slot(q), self.sems.at[0, k], self.sems.at[1, k], (x, c, y, z - 1))
 
     def start(self):
-        for k in (2, 1, 3, 0):
-            self.across[k].start()
-
-    def fold(self, steps=(2, 1, 3, 0)):
-        for k in steps:
-            self.across[k].wait_recv()
-            add_into(self.mine[k], self.by_y[k])
-            if k:
-                self.along[k - 1].start()
+        for p in (3, 0, 2, 1):
+            self.across(p).start()
+
+    def fold(self, steps=(3, 0, 2, 1)):
+        z = self.me[3]
+        for p in steps:
+            self.across(p).wait_recv()
+            add_into(self.mine(p), self.from_y(p))
+            if p > 0:
+
+                @pl.when(z == 0)
+                def _():
+                    self.up(p).start()
+
+            if p < 3:
+
+                @pl.when(z == 3)
+                def _():
+                    self.down(p).start()
+
+    def relay_up(self, p):
+        self.up(p).wait_recv()
+        add_into(self.mine(p), self.up_slot(p))
+        self.up(p).start()
+
+    def relay_down(self, q):
+        self.down(q).wait_recv()
+        add_into(self.mine(q), self.down_slot(q))
+        self.down(q).start()
+
+    def pass_one(self):
+        z = self.me[3]
+
+        @pl.when(z == 1)
+        def _():
+            self.relay_up(3)
+            self.relay_up(2)
+
+        @pl.when(z == 2)
+        def _():
+            self.relay_down(0)
+            self.relay_down(1)
+
+    def pass_two(self):
+        z = self.me[3]
+
+        @pl.when(z == 2)
+        def _():
+            self.relay_up(3)
+
+        @pl.when(z == 1)
+        def _():
+            self.relay_down(0)
 
     def end(self):
-        for k in (1, 2, 3):
-            self.along[k - 1].wait_recv()
-            add_into(self.mine[0], self.by_z[k - 1])
+        z = self.me[3]
+
+        @pl.when(z > 0)
+        def _():
+            self.up(z).wait_recv()
+            add_into(self.mine(z), self.up_slot(z))
+
+        @pl.when(z < 3)
+        def _():
+            self.down(z).wait_recv()
+            add_into(self.mine(z), self.down_slot(z))
 
     def finish(self):
-        for one in self.across + self.along:
-            one.wait_send()
+        z = self.me[3]
+        for p in range(4):
+            self.across(p).wait_send()
+
+            @pl.when(z < p)
+            def _():
+                self.up(p).wait_send()
+
+            @pl.when(z > p)
+            def _():
+                self.down(p).wait_send()
 
 
 class Sum8:
@@ -1013,6 +1171,9 @@
     pass
 
 
+FETCHED = "gains sk sv sq ck cv so co cq gate up".split()
+
+
 def layer_kernel(names, *refs):
     R = Names()
     for name, ref in zip(names, refs, strict=True):
@@ -1023,6 +1184,14 @@
     s = 2 * z + y
     group = ((1 - x, c, y, z), (1 - x, 1 - c, y, z), (x, 1 - c, y, z))
     line = tuple((x, c, y, lax.rem(z + k, 4)) for k in (1, 2, 3))
+    fetch = [
+        pltpu.make_async_copy(getattr(R, name), getattr(R, "v_" + name), R.s_fetch.at[i])
+        for i, name in enumerate(FETCHED)
+    ]
+    for one in fetch:
+        one.start()
+    near_dn = pltpu.make_async_copy(R.down, R.DN.at[s], R.s_near.at[0])
+    near_dn.start()
     greet(me, group + line + ((x, c, 1 - y, z),), moves=True)
 
     there = owner_of(*me)
@@ -1031,18 +1200,14 @@
     move_t = Move(me, R.tabs, R.TAB, R.s_move.at[1])
     move_m = Move(me, R.mem, R.M.at[2 * there_g + y], R.s_move.at[2])
     move_d = Move(me, R.dout, R.DO.at[there_g], R.s_move.at[3])
-    move_x.start()
-    near_dn = pltpu.make_async_copy(R.down, R.DN.at[s], R.s_near.at[0])
-    near_dn.start()
-    gains = R.gains[...].astype(F32)
-    blank = jnp.zeros((24, 64), F32)
+    for one in fetch[:6]:
+        one.wait()
+    gains = R.v_gains[...].astype(F32)
     for k in range(4):
         narrow = slice(192 * k, 192 * k + 192)
-        top = [w[:, narrow].astype(F32) for w in (R.sk, R.sv, R.sq)] + [gains]
-        bottom = [w[:, narrow].astype(F32) for w in (R.ck, R.cv, R.cq)] + [blank]
-        R.stage_a[k] = jnp.concatenate(
-            [jnp.concatenate(top, axis=1), jnp.concatenate(bottom, axis=1)], axis=0
-        ).astype(BF)
+        row = [w[:, narrow].astype(F32) for w in (R.v_sk, R.v_sv, R.v_sq)] + [gains]
+        row = jnp.concatenate(row + [w[:, narrow].astype(F32) for w in (R.v_ck, R.v_cv)], axis=1)
+        R.stage_a[k] = jnp.concatenate([row[:, :512], row[:, 512:]], axis=0).astype(BF)
 
     def to_group(stage, land, sems):
         return [
@@ -1053,6 +1218,7 @@
     parts_a = to_group(R.stage_a, R.land_a, R.s_part_a)
     for one in parts_a:
         one.start()
+    move_x.start()
     for t in range(2):
         length, plot = R.lengths[0, t], R.plots[0, t]
         start = R.lengths[0, 0] if t else 0
@@ -1065,60 +1231,73 @@
         w = w[...].astype(F32)
         return jnp.concatenate([w[:, :384], w[:, 384:]], axis=0).astype(BF)
 
-    R.FO[g, s] = halves_stacked(R.so)
+    for one in fetch[6:]:
+        one.wait()
+    for k in range(4):
+        wide = slice(512 * k, 512 * k + 512)
+        R.stage_b[k, :24] = R.v_gate[:, wide]
+        R.stage_b[k, 24:] = R.v_up[:, wide]
+    R.land_a[g] = R.stage_a[g]
+    R.land_b[g] = R.stage_b[g]
+    gather_x = Gather8(me, R.X, R.s_x, True)
+    gather_m = Gather8(me, R.M, R.s_m, True)
+    gather_d = Gather4(me, R.DO, R.s_d)
+    gather_a = GatherPlane(me, R.PA, R.s_a)
+    gather_b = GatherPlane(me, R.PB, R.s_b, slice(0, 384))
     gather_o = GatherPlane(me, R.FO.at[g], R.s_fo)
-    gather_o.start()
-    R.FC[g, s] = halves_stacked(R.co)
-    R.FQ[g, s] = halves_stacked(R.cq)
     gather_c = GatherPlane(me, R.FC.at[g], R.s_fc)
     gather_q = GatherPlane(me, R.FQ.at[g], R.s_fq)
-    for k in range(4):
-        wide = slice(512 * k, 512 * k + 512)
-        R.stage_b[k, :24] = R.gate[:, wide]
-        R.stage_b[k, 24:] = R.up[:, wide]
-    R.land_a[g] = R.stage_a[g]
-    R.land_b[g] = R.stage_b[g]
-    gather_x = Gather8(me, R.X, R.s_x)
-    gather_m = Gather8(me, R.M, R.s_m)
-    gather_d = Gather4(me, R.DO, R.s_d)
-    gather_a = GatherPlane(me, R.PA, R.s_a)
-    gather_b = GatherPlane(me, R.PB, R.s_b)
-    gather_2 = GatherPlane(me, R.P2, R.s_2)
-    gather_n = GatherPlane(me, R.DN, R.s_n)
+    gather_2 = GatherRelay(me, R.P2, R.s_2)
+    gather_n = GatherRelay(me, R.DN, R.s_n)
     whole_o = Gather4(me, R.FO, R.s_wo)
     whole_c = Gather4(me, R.FC, R.s_wc)
     whole_q = Gather4(me, R.FQ, R.s_wq)
 
+    R.FO[g, s] = halves_stacked(R.v_so)
+    gather_o.start_along()
+    gather_o.start_across()
+    R.FQ[g, s] = halves_stacked(R.v_cq)
+    R.FC[g, s] = halves_stacked(R.v_co)
     for one in parts_a:
         one.wait_recv()
-    tops, bottoms = [], []
+    whole = []
     for r in range(4):
         piece = R.land_a[r].astype(F32)
-        tops.append(piece[:24])
-        bottoms.append(piece[24:])
-    R.PA[s] = jnp.concatenate(tops, axis=0).astype(BF)
-    gather_a.start()
-    R.PB[s] = jnp.concatenate(bottoms, axis=0).astype(BF)
+        whole.append(jnp.concatenate([piece[:24], piece[24:]], axis=1))
+    whole = jnp.concatenate(whole, axis=0).astype(BF)
+    R.PA[s] = whole[:, :640]
+    R.PB[s, :, :384] = whole[:, 640:]
+    gather_a.start_across()
+    gather_b.start_across()
+    gather_q.start_across()
+    gather_c.start_across()
     move_x.arrive()
     gather_x.start()
+    gather_a.start_along()
     parts_b = to_group(R.stage_b, R.land_b, R.s_part_b)
     for one in parts_b:
         one.start()
+    move_m.start()
+    gather_b.start_along()
+    gather_q.start_along()
+    gather_c.start_along()
+    move_d.start()
+    gather_x.forward()
     for k in (1, 3, 2):
         gather_o.forward(k)
-    gather_x.forward()
-    move_m.start()
-    for k in (1, 3, 2):
-        gather_a.forward(k)
-    gather_x.forward_far()
-    gather_o.arrive()
-    whole_o.start()
-    gather_b.start()
+    gather_a.forward(1)
     for one in parts_b:
         one.wait_recv()
     for half in range(2):
         rows = [R.land_b[r].astype(F32)[24 * half : 24 * half + 24] for r in range(4)]
         R.P2[s, :, 512 * half : 512 * half + 512] = jnp.concatenate(rows, axis=0).astype(BF)
+    gather_2.start_along()
+    near_dn.wait()
+    gather_x.forward_far()
+    gather_o.arrive()
+    whole_o.start()
+    gather_a.forward(3)
+    gather_a.forward(2)
     move_t.arrive()
     end_one, end_two = R.TAB[0:1, 0:1], R.TAB[1:2, 0:1]
     plot_one, plot_two = R.TAB[2:3, 0:1], R.TAB[3:4, 0:1]
@@ -1171,6 +1350,9 @@
         return carry
 
     gather_x.arrive()
+    move_m.arrive()
+    gather_m.start()
+    whole_o.forward()
     lax.fori_loop(0, 4, first_norm, 0)
     product = SCALE * dot(mine_rows(R.X1), R.WA[:, 384:640])
     R.QT[...] = product.T[:192].astype(BF)
@@ -1179,26 +1361,24 @@
         return [Gather4(me, buf.at[:, h], sems.at[h]) for h in range(3)]
 
     share_1 = share_heads(R.A4, R.s_share1)
-    move_m.arrive()
-    gather_m.start()
-    move_d.start()
+    for k in (1, 3, 2):
+        gather_b.forward(k)
     for h in range(3):
         attend_head(h, R.info, R.QT, R.KV, R.KVT, R.OUT1, R.LSE1, True)
         R.A4[g, h] = R.OUT1[64 * h : 64 * h + 64, :].astype(BF)
         share_1[h].start()
-        if h == 0:
-            whole_o.forward()
-            gather_b.forward(1)
-            gather_b.forward(3)
-        if h == 1:
-            share_1[0].forward()
-            gather_b.forward(2)
-            gather_m.forward()
+    gather_m.forward()
+    for k in (1, 3, 2):
+        gather_q.forward(k)
+    for k in (1, 3, 2):
+        gather_c.forward(k)
+    gather_2.start_across()
+    gather_n.start_across()
+    for h in range(3):
+        share_1[h].forward()
     gather_m.forward_far()
-    gather_c.start()
-    gather_2.start()
-    near_dn.wait()
-    share_1[1].forward()
+    gather_2.forward(1)
+    gather_n.start_along()
     whole_o.arrive()
 
     def unpack_full(pieces, whole):
@@ -1213,9 +1393,6 @@
         lax.fori_loop(0, 4, one, 0)
 
     unpack_full(R.FO, R.WO)
-    share_1[2].forward()
-    gather_b.arrive()
-    unpack(R.PB, R.WB, 640, 128)
     for one in share_1:
         one.arrive()
 
@@ -1229,10 +1406,17 @@
         before = jnp.concatenate([R.X[4 * i + y], R.X[4 * i + 2 + y]], axis=0).astype(F32)
         first = before + project(R.A4, R.WO, i)
         R.FIRST[rows, :] = first
-        x2 = norm(first, gain_two)
-        R.X2[rows, :] = x2
-        product = SCALE * dot(x2, R.WB[:, 384:640])
-        R.CQT[:, rows] = product.T[:192].astype(BF)
+        R.X2[rows, :] = norm(first, gain_two)
+    gather_q.arrive()
+    whole_q.start()
+    gather_2.forward(2)
+    gather_n.forward(1)
+    gather_b.arrive()
+    unpack(R.PB, R.WB, 384, 128)
+    gather_c.arrive()
+    whole_c.start()
+    move_d.arrive()
+    gather_d.start()
     gather_m.arrive()
 
     def memory_pair(i, carry):
@@ -1240,26 +1424,33 @@
         return carry
 
     lax.fori_loop(0, 4, memory_pair, 0)
-    for k in (1, 3, 2):
-        gather_c.forward(k)
-    gather_n.start()
-    gather_q.start()
-    gather_c.arrive()
-    whole_c.start()
-    move_d.arrive()
+    whole_q.forward()
+    gather_2.forward(3)
+    gather_n.forward(2)
+    whole_q.arrive()
+    unpack_full(R.FQ, R.WQ)
+    for k in range(4):
+
+        @pl.when(g == k)
+        def _():
+            R.WCQ[...] = R.WQ[:, 192 * k : 192 * k + 192]
+
+    for i in range(2):
+        rows = slice(256 * i, 256 * i + 256)
+        product = SCALE * dot(R.X2[rows, :], R.WCQ[...])
+        R.CQT[:, rows] = product.T.astype(BF)
     share_2 = share_heads(R.C4, R.s_share2)
     for h in range(3):
         attend_head(h, R.info, R.CQT, R.MKV, R.MKVT, R.OUT2, R.LSE2, False)
         R.C4[g, h] = R.OUT2[64 * h : 64 * h + 64, :].astype(BF)
+        share_2[h].start()
         if h == 0:
             whole_c.forward()
-        share_2[h].start()
-        if h:
-            share_2[h - 1].forward()
-    gather_d.start()
-    for k in (1, 3, 2):
-        gather_2.forward(k)
-    share_2[2].forward()
+        if h == 1:
+            gather_n.forward(3)
+            gather_d.forward()
+    for h in range(3):
+        share_2[h].forward()
     whole_c.arrive()
     unpack_full(R.FC, R.WC)
     for one in share_2:
@@ -1269,11 +1460,6 @@
         second = R.FIRST[rows, :] + project(R.C4, R.WC, i)
         R.SECOND[rows, :] = second
         R.X3[rows, :] = norm(second, gain_three)
-    gather_d.forward()
-    for k in (1, 3, 2):
-        gather_n.forward(k)
-    for k in (1, 3, 2):
-        gather_q.forward(k)
     gather_2.arrive()
     unpack(R.P2, R.W2, 1024, 256)
     for one in parts_a + parts_b:
@@ -1322,12 +1508,12 @@
     own_block = 2 * g + y
     x3_t = R.X3[...].astype(F32).T.astype(BF)
     total_2 = [
-        SumPlane(me, R.P2, R.by_y_2, R.by_z_2, R.s_g2.at[i], slice(512 * i, 512 * i + 512))
-        for i in range(2)
+        SumPlane(me, R.P2, R.by_y_2, R.by_z_2, R.s_g2.at[i], slice(256 * i, 256 * i + 256))
+        for i in range(4)
     ]
-    for i in range(2):
-        R.W2G[...] = dot(x3_t, R.GG[:, 512 * i : 512 * i + 512])
-        pack(R.W2G, R.P2, 512 * i, 512)
+    for i in range(4):
+        R.W2G[...] = dot(x3_t, R.GG[:, 256 * i : 256 * i + 256])
+        pack(R.W2G, R.P2, 256 * i, 256)
         total_2[i].start()
     hidden_t = R.H[...].astype(F32).T.astype(BF)
     d_down = dot(hidden_t, R.DO[...].reshape(512, 768)).astype(BF)
@@ -1341,10 +1527,10 @@
     R.DS4[g] = second_grad.astype(BF)
     share_s = Gather4(me, R.DS4, R.s_s)
     share_s.start()
+    total_2[0].fold()
+    share_s.forward()
     sum_out.to_x()
-    gather_q.arrive()
-    whole_q.start()
-    share_s.forward()
+    total_2[1].fold()
     share_s.arrive()
 
     dsec = R.DS4[...].reshape(512, 768)
@@ -1355,24 +1541,54 @@
         attend_back_head(
             h, R.info, R.CQT, R.MKV, R.MKVT, R.OUTER, R.OUT2, R.LSE2, R.DCQT, R.MDKV, R.dk, R.dv, False
         )
-        if h == 0:
-            whole_q.forward()
         R.DC4[g, h] = R.DCQT[64 * h : 64 * h + 64, :]
         share_3[h].start()
-        if h:
-            share_3[h - 1].forward()
+        if h == 0:
+            total_2[2].fold()
+            total_2[0].pass_one()
+        if h == 1:
+            share_3[0].forward()
+            total_2[1].pass_one()
 
     def pack_24(whole, pieces):
         for t in range(8):
             rows = whole[24 * t : 24 * t + 24]
             pieces[t] = jnp.concatenate([rows[:, :384], rows[:, 384:]], axis=0).astype(BF)
 
-    whole_q.arrive()
-    unpack_full(R.FQ, R.WQ)
+    def memory_grad_pair(i, carry):
+        lanes = pl.ds(pl.multiple_of(i * 256, 256), 256)
+        turned = dot(R.WB[:, :384], R.MDKV[:, lanes]).astype(BF)
+        R.MG[2 * i] = turned[:, :128]
+        R.MG[2 * i + 1] = turned[:, 128:]
+        return carry
+
+    total_2[3].fold()
+    total_2[0].pass_two()
+    lax.fori_loop(0, 4, memory_grad_pair, 0)
+    sum_m = Sum8(me, R.MG, R.by_c_m, R.by_x_m, R.by_y_m, R.s_gm)
+    share_3[1].forward()
     pack_24(dot(R.C4[g].reshape(192, 512), dsec), R.CO8)
     total_c = SumPlane(me, R.CO8, R.by_y_c, R.by_z_c, R.s_gc)
     total_c.start()
+    R.W1G[...] = dot(R.MDKV[...], R.M[...].reshape(1024, 768)).T
+    pack(R.W1G, R.PB, 0, 384)
+    R.TURN[:192, :] = dot(R.DCQT[...], R.X2[...])
+    R.TURN[192:, :] = jnp.zeros((64, 768), F32)
+    pack(R.TURN[...].T, R.PB, 384, 256)
+    total_b = SumPlane(me, R.PB, R.by_y_b, R.by_z_b, R.s_gb)
+    total_b.start()
     share_3[2].forward()
+    sum_m.start()
+    back = [
+        Move(me, src, dst, R.s_back.at[i], back=True)
+        for i, (src, dst) in enumerate(
+            ((R.TBLOCK, R.tokens_out), (R.LBLOCK, R.layer_out), (R.MBLOCK, R.memory_out))
+        )
+    ]
+    R.LBLOCK[...] = (R.SECOND[own, :] + sum_out.end()).astype(BF)
+    back[1].start()
+    total_2[2].pass_one()
+    total_2[1].pass_two()
     for one in share_3:
         one.arrive()
 
@@ -1386,10 +1602,19 @@
     R.SGRAD[...] += part
 
     R.OUTER[...] = dot_nt(R.WO[mine_192, :], R.DFIRST[...]).astype(BF)
+    sum_m.to_x()
+    total_n.fold()
+    total_2[3].pass_one()
     for h in range(3):
         attend_back_head(
             h, R.info, R.QT, R.KV, R.KVT, R.OUTER, R.OUT1, R.LSE1, R.DQT, R.DKV, R.dk, R.dv, True
         )
+        if h == 0:
+            total_c.fold()
+            total_2[2].pass_two()
+        if h == 1:
+            total_n.pass_one()
+            total_2[3].pass_two()
 
     def token_grad_pair(i, carry):
         lanes = pl.ds(pl.multiple_of(i * 256, 256), 256)
@@ -1403,39 +1628,24 @@
     lax.fori_loop(0, 4, token_grad_pair, 0)
     sum_t = Sum8(me, R.TG, R.by_c_t, R.by_x_t, R.by_y_t, R.s_gt)
     sum_t.start()
+    sum_m.to_y()
     R.W1G[...] = dot(R.DKV[...], R.X1[...].reshape(1024, 768)).T
     pack(R.W1G, R.PA, 0, 384)
     total_a = SumPlane(me, R.PA, R.by_y_a, R.by_z_a, R.s_ga, slice(0, 384))
     sum_t.to_x()
     total_a.start()
-
-    def memory_grad_pair(i, carry):
-        lanes = pl.ds(pl.multiple_of(i * 256, 256), 256)
-        turned = dot(R.WB[:, :384], R.MDKV[:, lanes]).astype(BF)
-        R.MG[2 * i] = turned[:, :128]
-        R.MG[2 * i + 1] = turned[:, 128:]
-        return carry
-
-    lax.fori_loop(0, 4, memory_grad_pair, 0)
-    sum_m = Sum8(me, R.MG, R.by_c_m, R.by_x_m, R.by_y_m, R.s_gm)
-    sum_m.start()
-    R.W1G[...] = dot(R.MDKV[...], R.M[...].reshape(1024, 768)).T
-    pack(R.W1G, R.PB, 0, 384)
-    R.TURN[:192, :] = dot(R.DCQT[...], R.X2[...])
-    R.TURN[192:, :] = jnp.zeros((64, 768), F32)
-    pack(R.TURN[...].T, R.PB, 384, 256)
-    total_b = SumPlane(me, R.PB, R.by_y_b, R.by_z_b, R.s_gb)
     R.TURN[:192, :] = dot(R.DQT[...], mine_rows(R.X1))
     pack_24(dot(R.A4[g].reshape(192, 512), R.DFIRST[...]), R.SO8)
     total_s = SumPlane(me, R.SO8, R.by_y_s, R.by_z_s, R.s_gs)
-    for one in total_2:
-        one.fold()
-    total_n.fold()
-    total_c.fold()
+    total_b.fold()
+    total_c.pass_one()
+    total_n.pass_two()
+    R.MBLOCK[...] = sum_m.end().T.astype(BF)
+    back[2].start()
     sum_t.to_y()
-    sum_m.to_x()
-    total_b.start()
     total_s.start()
+    total_b.pass_one()
+    total_c.pass_two()
     total_a.fold()
     dx1 = sum_t.end().T
     part, gain_grad_one = norm_back(R.X[own_block].astype(F32), gain_one, dx1)
@@ -1446,19 +1656,8 @@
     total_g = SumPlane(me, R.PA, R.by_y_a, R.by_z_a, R.s_gg, slice(384, 640))
     total_g.start()
     R.TBLOCK[...] = (R.SGRAD[...] + part).astype(BF)
-    R.LBLOCK[...] = (R.SECOND[own, :] + sum_out.end()).astype(BF)
-    back = [
-        Move(me, src, dst, R.s_back.at[i], back=True)
-        for i, (src, dst) in enumerate(
-            ((R.TBLOCK, R.tokens_out), (R.LBLOCK, R.layer_out), (R.MBLOCK, R.memory_out))
-        )
-    ]
     back[0].start()
-    back[1].start()
-    sum_m.to_y()
-    total_b.fold()
-    total_s.fold()
-    total_g.fold()
+    total_b.pass_two()
     for one in total_2:
         one.end()
     rows_2 = R.P2[s].astype(F32)
@@ -1468,18 +1667,24 @@
     last_b = to_group(R.stage_b, R.quarters_b, R.s_last_b)
     for one in last_b:
         one.start()
-    R.MBLOCK[...] = sum_m.end().T.astype(BF)
-    back[2].start()
+    total_s.fold()
+    total_a.pass_one()
+    total_g.fold()
     total_n.end()
     total_c.end()
+    total_a.pass_two()
+    total_s.pass_one()
+    total_g.pass_one()
+    total_b.end()
+    total_s.pass_two()
+    total_g.pass_two()
     total_a.end()
-    total_b.end()
     total_g.end()
     rows_a, rows_b = R.PA[s].astype(F32), R.PB[s].astype(F32)
     for r in range(4):
         rows = slice(24 * r, 24 * r + 24)
-        R.stage_a[r] = jnp.concatenate([rows_a[rows], rows_b[rows]], axis=0).astype(BF)
-    last_a = to_group(R.stage_a, R.quarters_a, R.s_last_a)
+        R.stage_z[r] = jnp.concatenate([rows_a[rows], rows_b[rows]], axis=0).astype(BF)
+    last_a = to_group(R.stage_z, R.quarters_a, R.s_last_a)
     for one in last_a:
         one.start()
     total_s.end()
@@ -1487,7 +1692,7 @@
         pltpu.make_async_copy(src, dst, R.s_near.at[1 + i])
         for i, (src, dst) in enumerate(
             (
-                (R.stage_a.at[g], R.quarters_a.at[g]),
+                (R.stage_z.at[g], R.quarters_a.at[g]),
                 (R.stage_b.at[g], R.quarters_b.at[g]),
                 (R.CO8.at[s], R.co_out),
                 (R.SO8.at[s], R.so_out),
@@ -1538,12 +1743,14 @@
         memory_out=(n, d),
     )
     scratch = dict(
-        stage_a=low(4, 48, 640), land_a=low(4, 48, 640), stage_b=low(4, 48, 512), land_b=low(4, 48, 512),
+        stage_a=low(4, 48, 512), land_a=low(4, 48, 512), stage_z=low(4, 48, 640), stage_b=low(4, 48, 512), land_b=low(4, 48, 512),
+        **{"v_" + name: pltpu.VMEM(inputs[name][0].shape, BF) for name in FETCHED},
+        s_fetch=dma(len(FETCHED)),
         tabs=pltpu.VMEM((8, 128), jnp.int32), TAB=pltpu.VMEM((8, 128), jnp.int32),
         X=low(8, n, d), M=low(8, n, d), DO=low(4, n, d),
         PA=low(8, 96, 640), PB=low(8, 96, 640), P2=low(8, 96, 1024), DN=low(8, 64, d),
         FO=low(4, 8, 48, 384), FC=low(4, 8, 48, 384), FQ=low(4, 8, 48, 384),
-        WA=low(768, 640), WB=low(768, 640), W2=low(768, 1024), WO=low(d, d), WC=low(d, d), WQ=low(d, d),
+        WA=low(768, 640), WB=low(768, 384), WCQ=low(768, 192), W2=low(768, 1024), WO=low(d, d), WC=low(d, d), WQ=low(d, d),
         info=pltpu.VMEM((8, 512), jnp.int32),
         X1=low(8, n, d), X2=low(512, d), X3=low(512, d),
         KV=low(1024, 384), KVT=low(384, 1024), MKV=low(1024, 384), MKVT=low(384, 1024),
@@ -1553,25 +1760,25 @@
         FIRST=full(512, d), SECOND=full(512, d),
         H=low(512, 512), GG=low(512, 1024), DXP=low(4, n, d), OP=low(4, n, d),
         by_c_dx=low(2, n, d), by_x_dx=low(n, d), by_c_out=low(2, n, d), by_x_out=low(n, d),
-        W2G=full(768, 512), by_y_2=low(4, 96, 1024), by_z_2=low(3, 96, 1024),
-        DNG=low(8, 64, d), by_y_n=low(4, 64, d), by_z_n=low(3, 64, d),
+        W2G=full(768, 256), by_y_2=low(4, 96, 1024), by_z_2=low(5, 96, 1024),
+        DNG=low(8, 64, d), by_y_n=low(4, 64, d), by_z_n=low(5, 64, d),
         SGRAD=full(n, d), DS4=low(4, n, d), OUTER=low(192, 512),
         DCQT=low(192, 512), DQT=low(192, 512), MDKV=low(384, 1024), DKV=low(384, 1024),
         dk=full(64, 1024), dv=full(64, 1024),
-        CO8=low(8, 48, 384), by_y_c=low(4, 48, 384), by_z_c=low(3, 48, 384),
-        SO8=low(8, 48, 384), by_y_s=low(4, 48, 384), by_z_s=low(3, 48, 384),
+        CO8=low(8, 48, 384), by_y_c=low(4, 48, 384), by_z_c=low(5, 48, 384),
+        SO8=low(8, 48, 384), by_y_s=low(4, 48, 384), by_z_s=low(5, 48, 384),
         MG=low(8, d, n), by_c_m=low(2, 2, d, n), by_x_m=low(2, d, n), by_y_m=low(d, n),
         TG=low(8, d, n), by_c_t=low(2, 2, d, n), by_x_t=low(2, d, n), by_y_t=low(d, n),
         DFIRST=low(512, d), W1G=full(768, 384), TURN=full(256, 768),
-        by_y_a=low(4, 96, 640), by_z_a=low(3, 96, 640), by_y_b=low(4, 96, 640), by_z_b=low(3, 96, 640),
+        by_y_a=low(4, 96, 640), by_z_a=low(5, 96, 640), by_y_b=low(4, 96, 640), by_z_b=low(5, 96, 640),
         TBLOCK=low(n, d), LBLOCK=low(n, d), MBLOCK=low(n, d),
         s_move=dma(4, 2), s_near=dma(6), s_part_a=dma(2, 3), s_part_b=dma(2, 3),
         s_last_a=dma(2, 3), s_last_b=dma(2, 3), s_back=dma(3, 2),
         s_x=dma(14), s_m=dma(14), s_d=dma(6), s_wo=dma(6), s_wc=dma(6), s_wq=dma(6), s_s=dma(6),
-        s_a=dma(2, 7), s_b=dma(2, 7), s_2=dma(2, 7), s_n=dma(2, 7), s_fo=dma(2, 7), s_fc=dma(2, 7), s_fq=dma(2, 7),
+        s_a=dma(2, 12), s_b=dma(2, 12), s_2=dma(2, 12), s_n=dma(2, 12), s_fo=dma(2, 12), s_fc=dma(2, 12), s_fq=dma(2, 12),
         s_share1=dma(3, 6), s_share2=dma(3, 6), s_share3=dma(3, 6),
         s_dx=dma(2, 3), s_out=dma(2, 3), s_gm=dma(2, 7), s_gt=dma(2, 7),
-        s_ga=dma(2, 7), s_gb=dma(2, 7), s_gg=dma(2, 7), s_g2=dma(2, 2, 7), s_gn=dma(2, 7), s_gc=dma(2, 7), s_gs=dma(2, 7),
+        s_ga=dma(2, 11), s_gb=dma(2, 11), s_gg=dma(2, 11), s_g2=dma(4, 2, 11), s_gn=dma(2, 11), s_gc=dma(2, 11), s_gs=dma(2, 11),
     )
     names = tuple(inputs) + tuple(outs) + tuple(scratch)
     return pl.pallas_call(
@@ -1626,10 +1833,10 @@
     results = run_layer(
         dict(
             tok=(tokens[0], ANYWHERE), mem=(memory[0], ANYWHERE), dout=(out_grad[0], ANYWHERE),
-            lengths=(table_lengths, in_smem), plots=(table_plots, in_smem), gains=(gains, IN_VMEM),
-            sq=(self_query, IN_VMEM), sk=(self_key, IN_VMEM), sv=(self_value, IN_VMEM), so=(self_output, IN_VMEM),
-            cq=(cross_query, IN_VMEM), ck=(cross_key, IN_VMEM), cv=(cross_value, IN_VMEM), co=(cross_output, IN_VMEM),
-            gate=(mlp_gate, IN_VMEM), up=(mlp_up, IN_VMEM), down=(mlp_down, ANYWHERE),
+            lengths=(table_lengths, in_smem), plots=(table_plots, in_smem), gains=(gains, ANYWHERE),
+            sq=(self_query, ANYWHERE), sk=(self_key, ANYWHERE), sv=(self_value, ANYWHERE), so=(self_output, ANYWHERE),
+            cq=(cross_query, ANYWHERE), ck=(cross_key, ANYWHERE), cv=(cross_value, ANYWHERE), co=(cross_output, ANYWHERE),
+            gate=(mlp_gate, ANYWHERE), up=(mlp_up, ANYWHERE), down=(mlp_down, ANYWHERE),
         )
     )
     block = jax.ShapeDtypeStruct((128, 768), BF)

time: 238 us -> 186 us (0.78); the launches traced: 233 us -> 186 us
  Pallas kernels: 230 us -> 182 us
    pallas_call x1, Pallas kernels: 227 us -> 180 us  [run_layer(): pl.pallas_call(functools.partial(layer_kernel, names), out_shape=tuple((j...]
where the time goes in v2:
time: 186 us
  Pallas kernels  182 us (98%)
  local copies, waits for them, and re-layouts  2.8 us (2%)
    pallas_call x1, Pallas kernels, run_layer(): pl.pallas_call(functools.partial(layer_kernel, names), out_shape=tuple((j...  180 us

profile of v2, /device:TPU:0, one launch (start us, length us, event | category | flops | bytes accessed | tf_op | source)
XLA Modules:
  0.0 185.7 jit_solution(4213894179843803019)
XLA Ops:
  0.7 0.0 copy-start.1
  0.7 0.0 copy-start.2
  0.7 0.0 copy-start.3
  0.7 0.6 copy-done.1
  1.3 0.0 copy-done.2
  1.3 0.0 copy-done.3
  1.4 0.1 copy.42
  1.5 0.6 pad.4.refs_5_
  2.1 179.6 %layer.1 = (bf16[4,48,640]{2,1,0:T(8,128)(2,1)}, bf16[4,48,512]{2,1,0:T(8,128)(2,1)}, bf16[48,384]{1,0:T(8,128)(2,1)}, bf16[48,384]{1,0:T(8,128)(2,1)}, bf16[64,...) custom-call(bf16[128,768]{1,0:T(8,128)(2,1)} %bitcast.9, ...), custom_call_target="tpu_custom_call" | custom-call | tf_op jit(solution)/shard_map/layer/pallas_call | solution.py:1784
  181.6 2.6 %outputs.1 = (bf16[128,768]{1,0:T(8,128)(2,1)}, bf16[128,768]{1,0:T(8,128)(2,1)}, bf16[128,768]{1,0:T(8,128)(2,1)}, f32[24,128]{1,0:T(8,128)}, f32[24,768]{1,0:T...) custom-call(bf16[4,48,640]{2,1,0:T(8,128)(2,1)} %get-tuple-element.4, ...), custom_call_target="tpu_custom_call" | custom-call | tf_op jit(solution)/shard_map/outputs/pallas_call | solution.py:1845
  184.3 0.0 copy-start
  184.3 0.7 copy-done
  185.0 0.7 slice_reduce_fusion
  (1 shorter events, 0.0 us)
Async XLA Ops:
  0.7 0.7 copy-start.1
  0.7 0.7 copy-start.2
  0.7 0.7 copy-start.3
  184.3 0.7 copy-start

commit v3 on v2

--- a/solution.py
+++ b/solution.py
@@ -561,16 +561,11 @@
 
 
 def owner_of(x, c, y, z):
-    return lax.div(z, 2), lax.rem(z, 2), y, 2 * c + x
-
-
-def source_of(x, c, y, z):
-    return lax.rem(z, 2), lax.div(z, 2), y, 2 * x + c
+    return lax.rem(z, 2), lax.div(z, 2), y, 2 * c + x
 
 
 def is_fixed(x, c, y, z):
-    same = jnp.logical_and(lax.div(z, 2) == x, lax.rem(z, 2) == c)
-    return jnp.logical_and(same, 2 * c + x == z)
+    return 2 * c + x == z
 
 
 def greet(me, pairs=(), z_line=False, moves=False):
@@ -600,17 +595,14 @@
         @pl.when(away)
         def _():
             hello(owner_of(*me))
-            hello(source_of(*me))
-
-        count = count + jnp.where(away, 2, 0)
+
+        count = count + jnp.where(away, 1, 0)
     pl.semaphore_wait(bar, count)
 
 
 class Move:
-    def __init__(self, me, src, dst, sems, back=False):
-        self.me = me
-        to = source_of(*me) if back else owner_of(*me)
-        self.far = remote(src, dst, sems.at[0], sems.at[1], to)
+    def __init__(self, me, src, dst, sems):
+        self.far = remote(src, dst, sems.at[0], sems.at[1], owner_of(*me))
         self.near = pltpu.make_async_copy(src, dst, sems.at[0])
         self.fixed = is_fixed(*me)
 
@@ -639,15 +631,14 @@
 
 
 class Gather4:
-    def __init__(self, me, buf, sems):
+    def __init__(self, me, buf, sems, tokens=False):
         x, c, y, z = me
-        g = 2 * x + c
-        self.g = g
         xp, cp = (1 - x, c, y, z), (x, 1 - c, y, z)
-        far = 2 * (1 - x) + c
+        g = x + 2 * c if tokens else 2 * x + c
+        far = 1 - x + 2 * c if tokens else 2 * (1 - x) + c
         self.x_own = remote(buf.at[g], buf.at[g], sems.at[0], sems.at[1], xp)
-        self.c_own = remote(buf.at[g], buf.at[g], sems.at[2], sems.at[3], cp)
-        self.c_far = remote(buf.at[far], buf.at[far], sems.at[4], sems.at[5], cp)
+        self.c_own = remote(buf.at[g], buf.at[g], sems.at[0], sems.at[2], cp)
+        self.c_far = remote(buf.at[far], buf.at[far], sems.at[0], sems.at[3], cp)
 
     def start(self):
         self.x_own.start()
@@ -672,10 +663,10 @@
         x, c, y, z = me
         xp, cp, yp = (1 - x, c, y, z), (x, 1 - c, y, z), (x, c, 1 - y, z)
         def piece(px, pc, py):
-            return buf.at[2 * (2 * px + pc) + py]
+            return buf.at[2 * (px + 2 * pc) + py]
 
         def send(p, k, to):
-            return remote(p, p, sems.at[2 * k], sems.at[2 * k + 1], to)
+            return remote(p, p, sems.at[0], sems.at[1 + k], to)
 
         own, at_x = piece(x, c, y), piece(1 - x, c, y)
         at_y, at_d = piece(x, c, 1 - y), piece(1 - x, c, 1 - y)
@@ -763,7 +754,7 @@
 
         def send(p, k, to):
             piece = buf.at[2 * p + y] if lanes is None else buf.at[2 * p + y, :, lanes]
-            return remote(piece, piece, sems.at[0, k], sems.at[1, k], to)
+            return remote(piece, piece, sems.at[0], sems.at[1 + k], to)
 
         yp = (x, c, 1 - y, z)
         self.along = [send(z, k - 1, (x, c, y, lax.rem(z + k, 4))) for k in (1, 2, 3)]
@@ -799,7 +790,7 @@
 
     def send(self, p, k, to):
         piece = self.piece(p, self.me[2])
-        return remote(piece, piece, self.sems.at[0, k + p], self.sems.at[1, k + p], to)
+        return remote(piece, piece, self.sems.at[0], self.sems.at[1 + k + p], to)
 
     def up(self, p):
         x, c, y, z = self.me
@@ -889,7 +880,7 @@
     def across(self, p):
         x, c, y, z = self.me
         theirs = self.parts.at[2 * p + 1 - y, :, self.lanes]
-        return remote(theirs, self.from_y(p), self.sems.at[0, p], self.sems.at[1, p], (x, c, 1 - y, z))
+        return remote(theirs, self.from_y(p), self.sems.at[0], self.sems.at[1 + p], (x, c, 1 - y, z))
 
     def up_slot(self, p):
         return self.slot(p - 1)
@@ -899,13 +890,13 @@
 
     def up(self, p):
         x, c, y, z = self.me
-        k = 3 + p
-        return remote(self.mine(p), self.up_slot(p), self.sems.at[0, k], self.sems.at[1, k], (x, c, y, z + 1))
+        send, recv = self.sems.at[0], self.sems.at[4 + p]
+        return remote(self.mine(p), self.up_slot(p), send, recv, (x, c, y, z + 1))
 
     def down(self, q):
         x, c, y, z = self.me
-        k = 7 + q
-        return remote(self.mine(q), self.down_slot(q), self.sems.at[0, k], self.sems.at[1, k], (x, c, y, z - 1))
+        send, recv = self.sems.at[0], self.sems.at[5 + lax.rem(3 + q, 5)]
+        return remote(self.mine(q), self.down_slot(q), send, recv, (x, c, y, z - 1))
 
     def start(self):
         for p in (3, 0, 2, 1):
@@ -989,6 +980,43 @@
                 self.down(p).wait_send()
 
 
+class SumPlaneDirect(SumPlane):
+    def straight(self, k):
+        x, c, y, z = self.me
+        p = lax.rem(z + k, 4)
+        send, recv = self.sems.at[0], self.sems.at[4 + k]
+        return remote(self.mine(p), self.slot(k - 1), send, recv, (x, c, y, p))
+
+    def start(self):
+        for k in (2, 1, 3, 0):
+            self.across(lax.rem(self.me[3] + k, 4)).start()
+
+    def fold(self, steps=(2, 1, 3, 0)):
+        for k in steps:
+            p = lax.rem(self.me[3] + k, 4)
+            self.across(p).wait_recv()
+            add_into(self.mine(p), self.from_y(p))
+            if k:
+                self.straight(k).start()
+
+    def pass_one(self):
+        pass
+
+    def pass_two(self):
+        pass
+
+    def end(self):
+        for k in (1, 2, 3):
+            self.straight(k).wait_recv()
+            add_into(self.mine(self.me[3]), self.slot(k - 1))
+
+    def finish(self):
+        for p in range(4):
+            self.across(p).wait_send()
+        for k in (1, 2, 3):
+            self.straight(k).wait_send()
+
+
 class Sum8:
     def __init__(self, me, parts, by_c, by_x, by_y, sems):
         x, c, y, z = me
@@ -997,11 +1025,11 @@
         xp, cp, yp = (1 - x, c, y, z), (x, 1 - c, y, z), (x, c, 1 - y, z)
 
         def send(src, dst, k, to):
-            return remote(src, dst, sems.at[0, k], sems.at[1, k], to)
+            return remote(src, dst, sems.at[0], sems.at[1 + k], to)
 
         self.order = [(1 - x, 1 - y), (1 - x, y), (x, 1 - y), (x, y)]
         self.first = [
-            send(parts.at[2 * (2 * px + 1 - c) + py], by_c.at[px, py], k, cp)
+            send(parts.at[2 * (px + 2 * (1 - c)) + py], by_c.at[px, py], k, cp)
             for k, (px, py) in enumerate(self.order)
         ]
         self.second = [
@@ -1017,14 +1045,14 @@
         x, c, y, z = self.me
         for k, py in enumerate((1 - y, y)):
             self.first[k].wait_recv()
-            add_into(self.by_c.at[1 - x, py], self.parts.at[2 * (2 * (1 - x) + c) + py])
+            add_into(self.by_c.at[1 - x, py], self.parts.at[2 * (1 - x + 2 * c) + py])
             self.second[k].start()
 
     def to_y(self):
         x, c, y, z = self.me
         self.first[2].wait_recv()
         self.first[3].wait_recv()
-        add_into(self.by_c.at[x, 1 - y], self.parts.at[2 * (2 * x + c) + 1 - y])
+        add_into(self.by_c.at[x, 1 - y], self.parts.at[2 * (x + 2 * c) + 1 - y])
         self.second[0].wait_recv()
         add_into(self.by_x.at[1 - y], self.by_c.at[x, 1 - y])
         self.third.start()
@@ -1034,7 +1062,7 @@
         self.second[1].wait_recv()
         self.third.wait_recv()
         return (
-            self.parts[2 * (2 * x + c) + y].astype(F32)
+            self.parts[2 * (x + 2 * c) + y].astype(F32)
             + self.by_c[x, y].astype(F32)
             + self.by_x[y].astype(F32)
             + self.by_y[...].astype(F32)
@@ -1051,10 +1079,10 @@
         self.me, self.parts, self.by_c, self.by_x = me, parts, by_c, by_x
         xp, cp = (1 - x, c, y, z), (x, 1 - c, y, z)
         self.first = [
-            remote(parts.at[2 * px + 1 - c], by_c.at[px], sems.at[0, px], sems.at[1, px], cp)
+            remote(parts.at[px + 2 * (1 - c)], by_c.at[px], sems.at[0], sems.at[1 + px], cp)
             for px in range(2)
         ]
-        self.second = remote(by_c.at[1 - x], by_x, sems.at[0, 2], sems.at[1, 2], xp)
+        self.second = remote(by_c.at[1 - x], by_x, sems.at[0], sems.at[3], xp)
 
     def start(self):
         for one in self.first:
@@ -1064,14 +1092,14 @@
         x, c, y, z = self.me
         for one in self.first:
             one.wait_recv()
-        add_into(self.by_c.at[1 - x], self.parts.at[2 * (1 - x) + c])
+        add_into(self.by_c.at[1 - x], self.parts.at[1 - x + 2 * c])
         self.second.start()
 
     def end(self):
         x, c, y, z = self.me
         self.second.wait_recv()
         return (
-            self.parts[2 * x + c].astype(F32)
+            self.parts[x + 2 * c].astype(F32)
             + self.by_c[x].astype(F32)
             + self.by_x[...].astype(F32)
         )
@@ -1171,7 +1199,7 @@
     pass
 
 
-FETCHED = "gains sk sv sq ck cv so co cq gate up".split()
+FETCHED = ("sk", "sv", "sq", "ck", "cv", "so", "co", "cq", "gate", "up")
 
 
 def layer_kernel(names, *refs):
@@ -1181,6 +1209,7 @@
     me = coords()
     x, c, y, z = me
     g = 2 * x + c
+    t = x + 2 * c
     s = 2 * z + y
     group = ((1 - x, c, y, z), (1 - x, 1 - c, y, z), (x, 1 - c, y, z))
     line = tuple((x, c, y, lax.rem(z + k, 4)) for k in (1, 2, 3))
@@ -1194,15 +1223,19 @@
     near_dn.start()
     greet(me, group + line + ((x, c, 1 - y, z),), moves=True)
 
-    there = owner_of(*me)
-    there_g = 2 * there[0] + there[1]
-    move_x = Move(me, R.tok, R.X.at[2 * there_g + y], R.s_move.at[0])
+    move_x = Move(me, R.tok, R.X.at[s], R.s_move.at[0])
     move_t = Move(me, R.tabs, R.TAB, R.s_move.at[1])
-    move_m = Move(me, R.mem, R.M.at[2 * there_g + y], R.s_move.at[2])
-    move_d = Move(me, R.dout, R.DO.at[there_g], R.s_move.at[3])
-    for one in fetch[:6]:
+    move_m = Move(me, R.mem, R.M.at[s], R.s_move.at[2])
+    move_d = Move(me, R.dout, R.DO.at[z], R.s_move.at[3])
+    for one in fetch[:5]:
         one.wait()
-    gains = R.v_gains[...].astype(F32)
+    row = lax.broadcasted_iota(jnp.int32, (8, 128), 0)
+    gains = jnp.zeros((8, 128), F32)
+    for i, one in enumerate((R.g1, R.g2, R.g3)):
+        one = jnp.concatenate([one[...].astype(F32), jnp.zeros((1, 104), F32)], axis=1)
+        gains = jnp.where(row == i, one, gains)
+    gains = jnp.concatenate([gains, jnp.zeros((120, 128), F32)], axis=0).T[:24, :64]
+    blank = jnp.zeros((24, 64), F32)
     for k in range(4):
         narrow = slice(192 * k, 192 * k + 192)
         row = [w[:, narrow].astype(F32) for w in (R.v_sk, R.v_sv, R.v_sq)] + [gains]
@@ -1211,7 +1244,7 @@
 
     def to_group(stage, land, sems):
         return [
-            remote(stage.at[2 * to[0] + to[1]], land.at[g], sems.at[0, i], sems.at[1, i], to)
+            remote(stage.at[2 * to[0] + to[1]], land.at[g], sems.at[0], sems.at[1 + i], to)
             for i, to in enumerate(group)
         ]
 
@@ -1219,11 +1252,11 @@
     for one in parts_a:
         one.start()
     move_x.start()
-    for t in range(2):
-        length, plot = R.lengths[0, t], R.plots[0, t]
-        start = R.lengths[0, 0] if t else 0
-        R.tabs[t : t + 1, :] = jnp.full((1, 128), start + length, jnp.int32)
-        R.tabs[2 + t : 3 + t, :] = jnp.full((1, 128), plot, jnp.int32)
+    for i in range(2):
+        length, plot = R.lengths[0, i], R.plots[0, i]
+        start = R.lengths[0, 0] if i else 0
+        R.tabs[i : i + 1, :] = jnp.full((1, 128), start + length, jnp.int32)
+        R.tabs[2 + i : 3 + i, :] = jnp.full((1, 128), plot, jnp.int32)
     R.tabs[4:, :] = jnp.zeros((4, 128), jnp.int32)
     move_t.start()
 
@@ -1231,7 +1264,7 @@
         w = w[...].astype(F32)
         return jnp.concatenate([w[:, :384], w[:, 384:]], axis=0).astype(BF)
 
-    for one in fetch[6:]:
+    for one in fetch[5:]:
         one.wait()
     for k in range(4):
         wide = slice(512 * k, 512 * k + 512)
@@ -1241,7 +1274,7 @@
     R.land_b[g] = R.stage_b[g]
     gather_x = Gather8(me, R.X, R.s_x, True)
     gather_m = Gather8(me, R.M, R.s_m, True)
-    gather_d = Gather4(me, R.DO, R.s_d)
+    gather_d = Gather4(me, R.DO, R.s_d, tokens=True)
     gather_a = GatherPlane(me, R.PA, R.s_a)
     gather_b = GatherPlane(me, R.PB, R.s_b, slice(0, 384))
     gather_o = GatherPlane(me, R.FO.at[g], R.s_fo)
@@ -1268,9 +1301,6 @@
     R.PA[s] = whole[:, :640]
     R.PB[s, :, :384] = whole[:, 640:]
     gather_a.start_across()
-    gather_b.start_across()
-    gather_q.start_across()
-    gather_c.start_across()
     move_x.arrive()
     gather_x.start()
     gather_a.start_along()
@@ -1282,10 +1312,11 @@
     gather_q.start_along()
     gather_c.start_along()
     move_d.start()
-    gather_x.forward()
     for k in (1, 3, 2):
         gather_o.forward(k)
     gather_a.forward(1)
+    gather_x.forward()
+    gather_b.start_across()
     for one in parts_b:
         one.wait_recv()
     for half in range(2):
@@ -1298,6 +1329,8 @@
     whole_o.start()
     gather_a.forward(3)
     gather_a.forward(2)
+    gather_q.start_across()
+    gather_c.start_across()
     move_t.arrive()
     end_one, end_two = R.TAB[0:1, 0:1], R.TAB[1:2, 0:1]
     plot_one, plot_two = R.TAB[2:3, 0:1], R.TAB[3:4, 0:1]
@@ -1350,9 +1383,6 @@
         return carry
 
     gather_x.arrive()
-    move_m.arrive()
-    gather_m.start()
-    whole_o.forward()
     lax.fori_loop(0, 4, first_norm, 0)
     product = SCALE * dot(mine_rows(R.X1), R.WA[:, 384:640])
     R.QT[...] = product.T[:192].astype(BF)
@@ -1361,24 +1391,26 @@
         return [Gather4(me, buf.at[:, h], sems.at[h]) for h in range(3)]
 
     share_1 = share_heads(R.A4, R.s_share1)
-    for k in (1, 3, 2):
-        gather_b.forward(k)
+    move_m.arrive()
+    gather_m.start()
     for h in range(3):
         attend_head(h, R.info, R.QT, R.KV, R.KVT, R.OUT1, R.LSE1, True)
         R.A4[g, h] = R.OUT1[64 * h : 64 * h + 64, :].astype(BF)
         share_1[h].start()
+    for k in (1, 3, 2):
+        gather_b.forward(k)
+    for k in (1, 3, 2):
+        gather_q.forward(k)
+    whole_o.forward()
+    for h in range(3):
+        share_1[h].forward()
     gather_m.forward()
     for k in (1, 3, 2):
-        gather_q.forward(k)
-    for k in (1, 3, 2):
         gather_c.forward(k)
+    gather_2.forward(1)
+    gather_n.start_along()
     gather_2.start_across()
     gather_n.start_across()
-    for h in range(3):
-        share_1[h].forward()
-    gather_m.forward_far()
-    gather_2.forward(1)
-    gather_n.start_along()
     whole_o.arrive()
 
     def unpack_full(pieces, whole):
@@ -1409,14 +1441,12 @@
         R.X2[rows, :] = norm(first, gain_two)
     gather_q.arrive()
     whole_q.start()
-    gather_2.forward(2)
-    gather_n.forward(1)
+    gather_m.forward_far()
     gather_b.arrive()
     unpack(R.PB, R.WB, 384, 128)
     gather_c.arrive()
     whole_c.start()
     move_d.arrive()
-    gather_d.start()
     gather_m.arrive()
 
     def memory_pair(i, carry):
@@ -1424,9 +1454,9 @@
         return carry
 
     lax.fori_loop(0, 4, memory_pair, 0)
+    gather_2.forward(2)
+    gather_n.forward(1)
     whole_q.forward()
-    gather_2.forward(3)
-    gather_n.forward(2)
     whole_q.arrive()
     unpack_full(R.FQ, R.WQ)
     for k in range(4):
@@ -1444,13 +1474,13 @@
         attend_head(h, R.info, R.CQT, R.MKV, R.MKVT, R.OUT2, R.LSE2, False)
         R.C4[g, h] = R.OUT2[64 * h : 64 * h + 64, :].astype(BF)
         share_2[h].start()
-        if h == 0:
-            whole_c.forward()
-        if h == 1:
-            gather_n.forward(3)
-            gather_d.forward()
+    gather_d.start()
+    whole_c.forward()
+    gather_2.forward(3)
+    gather_n.forward(2)
     for h in range(3):
         share_2[h].forward()
+    gather_n.forward(3)
     whole_c.arrive()
     unpack_full(R.FC, R.WC)
     for one in share_2:
@@ -1460,6 +1490,7 @@
         second = R.FIRST[rows, :] + project(R.C4, R.WC, i)
         R.SECOND[rows, :] = second
         R.X3[rows, :] = norm(second, gain_three)
+    gather_d.forward()
     gather_2.arrive()
     unpack(R.P2, R.W2, 1024, 256)
     for one in parts_a + parts_b:
@@ -1474,25 +1505,25 @@
     sum_out = Sum4(me, R.OP, R.by_c_out, R.by_x_out, R.s_out)
 
     def feed(core):
-        at = [pl.ds(pl.multiple_of((2 * px + core) * 128, 128), 128) for px in range(2)]
-        x3 = jnp.concatenate([R.X3[rows, :] for rows in at], axis=0)
+        at = pl.ds(pl.multiple_of(core * 256, 256), 256)
+        x3 = R.X3[at, :]
         gate, up = dot(x3, R.W2[:, :512]), dot(x3, R.W2[:, 512:])
         active, slope = gelu_parts(gate)
         hidden = (active * up).astype(BF)
-        outer = jnp.concatenate([R.DO[2 * px + core] for px in range(2)], axis=0)
+        outer = jnp.concatenate([R.DO[2 * core + px] for px in range(2)], axis=0)
         w_down = R.DN[...].reshape(512, 768)
         hidden_grad = dot_nt(outer, w_down)
         gate_grad = (hidden_grad * up * slope).astype(BF)
         up_grad = (hidden_grad * active).astype(BF)
         dx3 = (dot_nt(gate_grad, R.W2[:, :512]) + dot_nt(up_grad, R.W2[:, 512:])).astype(BF)
         out = dot(hidden, w_down).astype(BF)
+        R.H[at, :] = hidden
+        R.GG[at, :512] = gate_grad
+        R.GG[at, 512:] = up_grad
         for px in range(2):
             half = slice(128 * px, 128 * px + 128)
-            R.H[at[px], :] = hidden[half]
-            R.GG[at[px], :512] = gate_grad[half]
-            R.GG[at[px], 512:] = up_grad[half]
-            R.DXP[2 * px + core] = dx3[half]
-            R.OP[2 * px + core] = out[half]
+            R.DXP[2 * core + px] = dx3[half]
+            R.OP[2 * core + px] = out[half]
 
     def pack(whole, pieces, start, width):
         for t in range(8):
@@ -1504,11 +1535,11 @@
     feed(c)
     sum_dx.to_x()
     sum_out.start()
-    own = pl.ds(pl.multiple_of(g * 128, 128), 128)
-    own_block = 2 * g + y
+    own = pl.ds(pl.multiple_of(t * 128, 128), 128)
+    own_block = 2 * t + y
     x3_t = R.X3[...].astype(F32).T.astype(BF)
     total_2 = [
-        SumPlane(me, R.P2, R.by_y_2, R.by_z_2, R.s_g2.at[i], slice(256 * i, 256 * i + 256))
+        SumPlaneDirect(me, R.P2, R.by_y_2, R.by_z_2, R.s_g2.at[i], slice(256 * i, 256 * i + 256))
         for i in range(4)
     ]
     for i in range(4):
@@ -1517,20 +1548,21 @@
         total_2[i].start()
     hidden_t = R.H[...].astype(F32).T.astype(BF)
     d_down = dot(hidden_t, R.DO[...].reshape(512, 768)).astype(BF)
-    for t in range(8):
-        R.DNG[t] = d_down[64 * t : 64 * t + 64]
-    total_n = SumPlane(me, R.DNG, R.by_y_n, R.by_z_n, R.s_gn)
+    for i in range(8):
+        R.DNG[i] = d_down[64 * i : 64 * i + 64]
+    total_n = SumPlaneDirect(me, R.DNG, R.by_y_n, R.by_z_n, R.s_gn)
     total_n.start()
     part, gain_grad_three = norm_back(R.SECOND[own, :], gain_three, sum_dx.end())
-    second_grad = R.DO[g].astype(F32) + part
+    second_grad = R.DO[t].astype(F32) + part
     R.SGRAD[...] = second_grad
-    R.DS4[g] = second_grad.astype(BF)
-    share_s = Gather4(me, R.DS4, R.s_s)
+    R.DS4[t] = second_grad.astype(BF)
+    share_s = Gather4(me, R.DS4, R.s_s, tokens=True)
     share_s.start()
     total_2[0].fold()
     share_s.forward()
     sum_out.to_x()
     total_2[1].fold()
+    total_2[0].pass_one()
     share_s.arrive()
 
     dsec = R.DS4[...].reshape(512, 768)
@@ -1545,10 +1577,9 @@
         share_3[h].start()
         if h == 0:
             total_2[2].fold()
-            total_2[0].pass_one()
         if h == 1:
             share_3[0].forward()
-            total_2[1].pass_one()
+            total_2[0].pass_two()
 
     def pack_24(whole, pieces):
         for t in range(8):
@@ -1563,7 +1594,7 @@
         return carry
 
     total_2[3].fold()
-    total_2[0].pass_two()
+    total_2[1].pass_one()
     lax.fori_loop(0, 4, memory_grad_pair, 0)
     sum_m = Sum8(me, R.MG, R.by_c_m, R.by_x_m, R.by_y_m, R.s_gm)
     share_3[1].forward()
@@ -1572,15 +1603,12 @@
     total_c.start()
     R.W1G[...] = dot(R.MDKV[...], R.M[...].reshape(1024, 768)).T
     pack(R.W1G, R.PB, 0, 384)
-    R.TURN[:192, :] = dot(R.DCQT[...], R.X2[...])
-    R.TURN[192:, :] = jnp.zeros((64, 768), F32)
-    pack(R.TURN[...].T, R.PB, 384, 256)
-    total_b = SumPlane(me, R.PB, R.by_y_b, R.by_z_b, R.s_gb)
+    total_b = SumPlane(me, R.PB, R.by_y_b, R.by_z_b, R.s_gb, slice(0, 384))
     total_b.start()
     share_3[2].forward()
     sum_m.start()
     back = [
-        Move(me, src, dst, R.s_back.at[i], back=True)
+        Move(me, src, dst, R.s_back.at[i])
         for i, (src, dst) in enumerate(
             ((R.TBLOCK, R.tokens_out), (R.LBLOCK, R.layer_out), (R.MBLOCK, R.memory_out))
         )
@@ -1597,24 +1625,15 @@
         dx2 = dot(R.WQ[...], R.DC4[:, :, :, rows].reshape(768, 256)).T
         part, ignored = norm_back(R.FIRST[rows, :], gain_two, dx2)
         R.DFIRST[rows, :] = (dsec[rows].astype(F32) + part).astype(BF)
-    dx2 = dot(R.WQ[...], R.DC4[:, :, :, own].reshape(768, 128)).T
-    part, gain_grad_two = norm_back(R.FIRST[own, :], gain_two, dx2)
-    R.SGRAD[...] += part
-
     R.OUTER[...] = dot_nt(R.WO[mine_192, :], R.DFIRST[...]).astype(BF)
     sum_m.to_x()
     total_n.fold()
     total_2[3].pass_one()
+
     for h in range(3):
         attend_back_head(
             h, R.info, R.QT, R.KV, R.KVT, R.OUTER, R.OUT1, R.LSE1, R.DQT, R.DKV, R.dk, R.dv, True
         )
-        if h == 0:
-            total_c.fold()
-            total_2[2].pass_two()
-        if h == 1:
-            total_n.pass_one()
-            total_2[3].pass_two()
 
     def token_grad_pair(i, carry):
         lanes = pl.ds(pl.multiple_of(i * 256, 256), 256)
@@ -1628,36 +1647,50 @@
     lax.fori_loop(0, 4, token_grad_pair, 0)
     sum_t = Sum8(me, R.TG, R.by_c_t, R.by_x_t, R.by_y_t, R.s_gt)
     sum_t.start()
+    pack_24(dot(R.A4[g].reshape(192, 512), R.DFIRST[...]), R.SO8)
+    total_s = SumPlane(me, R.SO8, R.by_y_s, R.by_z_s, R.s_gs)
+    total_s.start()
+    dx2 = dot(R.WQ[...], R.DC4[:, :, :, own].reshape(768, 128)).T
+    part, gain_grad_two = norm_back(R.FIRST[own, :], gain_two, dx2)
+    R.SGRAD[...] += part
+    sum_t.to_x()
     sum_m.to_y()
+    total_c.fold()
+    total_n.pass_one()
+    total_2[2].pass_two()
     R.W1G[...] = dot(R.DKV[...], R.X1[...].reshape(1024, 768)).T
     pack(R.W1G, R.PA, 0, 384)
     total_a = SumPlane(me, R.PA, R.by_y_a, R.by_z_a, R.s_ga, slice(0, 384))
-    sum_t.to_x()
+    R.TURN[:192, :] = dot(R.DQT[...], mine_rows(R.X1))
+    R.TURN[192:, :] = dot(R.DCQT[...], R.X2[...])
+    R.W1G[...] = R.TURN[...].T
+    pack(R.W1G, R.PB, 384, 384)
+    total_q = SumPlane(me, R.PB, R.by_y_b, R.by_z_b, R.s_gq, slice(384, 768))
+    total_b.fold()
+    total_2[3].pass_two()
+    sum_t.to_y()
     total_a.start()
-    R.TURN[:192, :] = dot(R.DQT[...], mine_rows(R.X1))
-    pack_24(dot(R.A4[g].reshape(192, 512), R.DFIRST[...]), R.SO8)
-    total_s = SumPlane(me, R.SO8, R.by_y_s, R.by_z_s, R.s_gs)
-    total_b.fold()
+    total_q.start()
     total_c.pass_one()
     total_n.pass_two()
+    total_s.fold()
+    total_b.pass_one()
     R.MBLOCK[...] = sum_m.end().T.astype(BF)
     back[2].start()
-    sum_t.to_y()
-    total_s.start()
-    total_b.pass_one()
-    total_c.pass_two()
-    total_a.fold()
     dx1 = sum_t.end().T
     part, gain_grad_one = norm_back(R.X[own_block].astype(F32), gain_one, dx1)
-    R.TURN[192:193, :] = gain_grad_one
-    R.TURN[193:194, :] = gain_grad_two
-    R.TURN[194:195, :] = gain_grad_three
-    pack(R.TURN[...].T, R.PA, 384, 256)
-    total_g = SumPlane(me, R.PA, R.by_y_a, R.by_z_a, R.s_gg, slice(384, 640))
-    total_g.start()
     R.TBLOCK[...] = (R.SGRAD[...] + part).astype(BF)
     back[0].start()
+    R.GT[0:1, :] = gain_grad_one
+    R.GT[1:2, :] = gain_grad_two
+    R.GT[2:3, :] = gain_grad_three
+    pack(R.GT[...].T, R.PG, 0, 128)
+    total_g = SumPlane(me, R.PG, R.by_y_g, R.by_z_g, R.s_gg)
+    total_g.start()
+    total_c.pass_two()
+    total_s.pass_one()
     total_b.pass_two()
+    total_a.fold()
     for one in total_2:
         one.end()
     rows_2 = R.P2[s].astype(F32)
@@ -1667,27 +1700,34 @@
     last_b = to_group(R.stage_b, R.quarters_b, R.s_last_b)
     for one in last_b:
         one.start()
-    total_s.fold()
+    total_n.end()
+    total_q.fold()
+    total_s.pass_two()
     total_a.pass_one()
     total_g.fold()
-    total_n.end()
     total_c.end()
+    total_b.end()
+    total_q.pass_one()
     total_a.pass_two()
-    total_s.pass_one()
     total_g.pass_one()
-    total_b.end()
-    total_s.pass_two()
+    total_s.end()
+    total_q.pass_two()
     total_g.pass_two()
     total_a.end()
+    total_q.end()
     total_g.end()
-    rows_a, rows_b = R.PA[s].astype(F32), R.PB[s].astype(F32)
+    rows_a, rows_b = R.PA[s, :, :384].astype(F32), R.PB[s].astype(F32)
+    rows_g = R.PG[s].astype(F32)
     for r in range(4):
         rows = slice(24 * r, 24 * r + 24)
-        R.stage_z[r] = jnp.concatenate([rows_a[rows], rows_b[rows]], axis=0).astype(BF)
+        top = [rows_a[rows], rows_b[rows, 384:576], rows_g[rows, :64]]
+        bottom = [rows_b[rows, :384], rows_b[rows, 576:], blank]
+        R.stage_z[r] = jnp.concatenate(
+            [jnp.concatenate(top, axis=1), jnp.concatenate(bottom, axis=1)], axis=0
+        ).astype(BF)
     last_a = to_group(R.stage_z, R.quarters_a, R.s_last_a)
     for one in last_a:
         one.start()
-    total_s.end()
     near = [
         pltpu.make_async_copy(src, dst, R.s_near.at[1 + i])
         for i, (src, dst) in enumerate(
@@ -1719,7 +1759,7 @@
         one.finish()
     for one in share_1 + share_2 + share_3 + total_2:
         one.finish()
-    for one in (total_a, total_g, total_b, total_n, total_c, total_s):
+    for one in (total_a, total_q, total_g, total_b, total_n, total_c, total_s):
         one.finish()
 
 
@@ -1748,7 +1788,7 @@
         s_fetch=dma(len(FETCHED)),
         tabs=pltpu.VMEM((8, 128), jnp.int32), TAB=pltpu.VMEM((8, 128), jnp.int32),
         X=low(8, n, d), M=low(8, n, d), DO=low(4, n, d),
-        PA=low(8, 96, 640), PB=low(8, 96, 640), P2=low(8, 96, 1024), DN=low(8, 64, d),
+        PA=low(8, 96, 640), PB=low(8, 96, 768), PG=low(8, 96, 128), P2=low(8, 96, 1024), DN=low(8, 64, d),
         FO=low(4, 8, 48, 384), FC=low(4, 8, 48, 384), FQ=low(4, 8, 48, 384),
         WA=low(768, 640), WB=low(768, 384), WCQ=low(768, 192), W2=low(768, 1024), WO=low(d, d), WC=low(d, d), WQ=low(d, d),
         info=pltpu.VMEM((8, 512), jnp.int32),
@@ -1769,16 +1809,15 @@
         SO8=low(8, 48, 384), by_y_s=low(4, 48, 384), by_z_s=low(5, 48, 384),
         MG=low(8, d, n), by_c_m=low(2, 2, d, n), by_x_m=low(2, d, n), by_y_m=low(d, n),
         TG=low(8, d, n), by_c_t=low(2, 2, d, n), by_x_t=low(2, d, n), by_y_t=low(d, n),
-        DFIRST=low(512, d), W1G=full(768, 384), TURN=full(256, 768),
-        by_y_a=low(4, 96, 640), by_z_a=low(5, 96, 640), by_y_b=low(4, 96, 640), by_z_b=low(5, 96, 640),
+        DFIRST=low(512, d), W1G=full(768, 384), TURN=full(384, 768), GT=full(128, 768),
+        by_y_a=low(4, 96, 384), by_z_a=low(5, 96, 384), by_y_b=low(4, 96, 768), by_z_b=low(5, 96, 768),
+        by_y_g=low(4, 96, 128), by_z_g=low(5, 96, 128),
         TBLOCK=low(n, d), LBLOCK=low(n, d), MBLOCK=low(n, d),
-        s_move=dma(4, 2), s_near=dma(6), s_part_a=dma(2, 3), s_part_b=dma(2, 3),
-        s_last_a=dma(2, 3), s_last_b=dma(2, 3), s_back=dma(3, 2),
-        s_x=dma(14), s_m=dma(14), s_d=dma(6), s_wo=dma(6), s_wc=dma(6), s_wq=dma(6), s_s=dma(6),
-        s_a=dma(2, 12), s_b=dma(2, 12), s_2=dma(2, 12), s_n=dma(2, 12), s_fo=dma(2, 12), s_fc=dma(2, 12), s_fq=dma(2, 12),
-        s_share1=dma(3, 6), s_share2=dma(3, 6), s_share3=dma(3, 6),
-        s_dx=dma(2, 3), s_out=dma(2, 3), s_gm=dma(2, 7), s_gt=dma(2, 7),
-        s_ga=dma(2, 11), s_gb=dma(2, 11), s_gg=dma(2, 11), s_g2=dma(4, 2, 11), s_gn=dma(2, 11), s_gc=dma(2, 11), s_gs=dma(2, 11),
+        s_move=dma(4, 2), s_near=dma(6), s_back=dma(3, 2),
+        **{name: dma(4) for name in ("s_part_a", "s_part_b", "s_last_a", "s_last_b", "s_d", "s_wo", "s_wc", "s_wq", "s_s", "s_dx", "s_out")},
+        **{name: dma(8) for name in ("s_x", "s_m", "s_gm", "s_gt", "s_a", "s_b", "s_fo", "s_fc", "s_fq")},
+        s_2=dma(13), s_n=dma(13), s_share1=dma(3, 4), s_share2=dma(3, 4), s_share3=dma(3, 4), s_g2=dma(4, 10),
+        **{name: dma(10) for name in ("s_ga", "s_gb", "s_gq", "s_gg", "s_gn", "s_gc", "s_gs")},
     )
     names = tuple(inputs) + tuple(outs) + tuple(scratch)
     return pl.pallas_call(
@@ -1794,31 +1833,75 @@
     )(*[a for a, _ in inputs.values()])
 
 
-def outputs_kernel(
-    qa, qb, co, so, down, tokens, layer, memory,
-    layer_out, tokens_out, memory_out, gains_out,
-    sq, sk, sv, so_out, cq, ck, cv, co_out, gate, up, down_out,
-):
-    layer_out[...] = layer[...]
-    tokens_out[...] = tokens[...]
-    memory_out[...] = memory[...]
-    down_out[...] = down[...].astype(F32)
+def outputs_kernel(names, *refs):
+    R = Names()
+    for name, ref in zip(names, refs, strict=True):
+        setattr(R, name, ref)
+
+    def copies(pairs, sems):
+        made = [pltpu.make_async_copy(a, b, sems.at[i]) for i, (a, b) in enumerate(pairs)]
+        for one in made:
+            one.start()
+        return made
+
+    arrive = copies(
+        ((R.qa, R.v_qa), (R.qb, R.v_qb), (R.co, R.v_co), (R.so, R.v_so), (R.down, R.v_down)), R.s_in
+    )
+    blocks = copies([(getattr(R, n), getattr(R, "v_" + n)) for n in BLOCKS], R.s_block)
+    for one in arrive:
+        one.wait()
     gains = jnp.zeros((24, 128), F32)
     for k in range(4):
-        piece = qa[k].astype(F32)
+        piece = R.v_qa[k].astype(F32)
         gains = gains + piece[:24, 512:]
         narrow = slice(192 * k, 192 * k + 192)
-        for row, outs in ((0, (sk, sv, sq)), (24, (ck, cv, cq))):
+        for row, outs in ((0, (R.w_sk, R.w_sv, R.w_sq)), (24, (R.w_ck, R.w_cv, R.w_cq))):
             for i, out in enumerate(outs):
                 out[:, narrow] = piece[row : row + 24, 192 * i : 192 * i + 192]
-        piece = qb[k].astype(F32)
-        gate[:, 512 * k : 512 * k + 512] = piece[:24]
-        up[:, 512 * k : 512 * k + 512] = piece[24:]
-    gains_out[...] = gains
-    for piece, out in ((so, so_out), (co, co_out)):
+        piece = R.v_qb[k].astype(F32)
+        R.w_gate[:, 512 * k : 512 * k + 512] = piece[:24]
+        R.w_up[:, 512 * k : 512 * k + 512] = piece[24:]
+    for piece, out in ((R.v_so, R.w_so), (R.v_co, R.w_co)):
         rows = piece[...].astype(F32)
         out[:, :384] = rows[:24]
         out[:, 384:] = rows[24:]
+    R.w_down[...] = R.v_down[...].astype(F32)
+    turned = jnp.concatenate([gains, jnp.zeros((104, 128), F32)], axis=0).T
+    for i, out in enumerate((R.w_g1, R.w_g2, R.w_g3)):
+        out[...] = turned[64 + i : 65 + i, :24]
+    leave = copies([(getattr(R, "w_" + n), getattr(R, "o_" + n)) for n in WEIGHTS], R.s_out)
+    for one in blocks:
+        one.wait()
+    leave += copies([(getattr(R, "v_" + n), getattr(R, "o_" + n)) for n in BLOCKS], R.s_direct)
+    for one in leave:
+        one.wait()
+
+
+BLOCKS = ("layer", "tokens", "memory")
+WEIGHTS = ("g1", "sq", "sk", "sv", "so", "g2", "cq", "ck", "cv", "co", "g3", "gate", "up", "down")
+
+
+def write_outputs(results):
+    ins = ("qa", "qb", "co", "so", "down", "tokens", "layer", "memory")
+    blocks = BLOCKS
+    shapes = {name: (24, 768) for name in WEIGHTS}
+    shapes |= {name: (1, 24) for name in ("g1", "g2", "g3")}
+    shapes |= dict(gate=(24, 2048), up=(24, 2048), down=(64, 768))
+    outs = [jax.ShapeDtypeStruct((128, 768), BF) for _ in blocks]
+    outs += [jax.ShapeDtypeStruct(shapes[n], F32) for n in WEIGHTS]
+    scratch = {"v_" + n: pltpu.VMEM(a.shape, BF) for n, a in zip(ins, results)}
+    scratch |= {"w_" + n: pltpu.VMEM(shapes[n], F32) for n in WEIGHTS}
+    scratch |= dict(s_in=dma(5), s_direct=dma(3), s_block=dma(3), s_out=dma(len(WEIGHTS)))
+    names = ins + tuple("o_" + n for n in blocks + WEIGHTS) + tuple(scratch)
+    return pl.pallas_call(
+        functools.partial(outputs_kernel, names),
+        out_shape=tuple(outs),
+        in_specs=[ANYWHERE] * len(ins),
+        out_specs=tuple([ANYWHERE] * len(outs)),
+        scratch_shapes=list(scratch.values()),
+        compiler_params=pltpu.CompilerParams(vmem_limit_bytes=VMEM_LIMIT),
+        name="outputs",
+    )(*results)
 
 
 def body_planes(
@@ -1827,36 +1910,19 @@
     cross_gain, cross_query, cross_key, cross_value, cross_output,
     mlp_gain, mlp_gate, mlp_up, mlp_down,
 ):
-    gains = jnp.stack([self_gain, cross_gain, mlp_gain], axis=1)
-    gains = jnp.pad(gains, ((0, 0), (0, 61)))
     in_smem = pl.BlockSpec(memory_space=pltpu.SMEM)
     results = run_layer(
         dict(
             tok=(tokens[0], ANYWHERE), mem=(memory[0], ANYWHERE), dout=(out_grad[0], ANYWHERE),
-            lengths=(table_lengths, in_smem), plots=(table_plots, in_smem), gains=(gains, ANYWHERE),
+            lengths=(table_lengths, in_smem), plots=(table_plots, in_smem), g1=(self_gain[None], IN_VMEM), g2=(cross_gain[None], IN_VMEM), g3=(mlp_gain[None], IN_VMEM),
             sq=(self_query, ANYWHERE), sk=(self_key, ANYWHERE), sv=(self_value, ANYWHERE), so=(self_output, ANYWHERE),
             cq=(cross_query, ANYWHERE), ck=(cross_key, ANYWHERE), cv=(cross_value, ANYWHERE), co=(cross_output, ANYWHERE),
             gate=(mlp_gate, ANYWHERE), up=(mlp_up, ANYWHERE), down=(mlp_down, ANYWHERE),
         )
     )
-    block = jax.ShapeDtypeStruct((128, 768), BF)
-    rows = jax.ShapeDtypeStruct((24, 768), F32)
-    wide = jax.ShapeDtypeStruct((24, 2048), F32)
-    outs = pl.pallas_call(
-        outputs_kernel,
-        out_shape=(block,) * 3
-        + (jax.ShapeDtypeStruct((24, 128), F32),)
-        + (rows,) * 8
-        + (wide, wide, jax.ShapeDtypeStruct((64, 768), F32)),
-        name="outputs",
-    )(*results)
-    layer, tokens_mine, memory_mine, gain_sums, sq, sk, sv, so, cq, ck, cv, co, gate, up, down = outs
-    return (
-        layer[None], tokens_mine[None], memory_mine[None],
-        gain_sums[:, 64], sq, sk, sv, so,
-        gain_sums[:, 65], cq, ck, cv, co,
-        gain_sums[:, 66], gate, up, down,
-    )
+    outs = write_outputs(results)
+    blocks = tuple(a[None] for a in outs[:3])
+    return blocks + tuple(a[0] if a.shape[0] == 1 else a for a in outs[3:])
 
 
 def solution(mesh):

time: 186 us -> 176 us (0.946)
  Pallas kernels: 182 us -> 175 us
  local copies, waits for them, and re-layouts: 2.8 us -> 0 us
    pallas_call x1, Pallas kernels: 180 us -> 172 us  [run_layer(): pl.pallas_call(functools.partial(layer_kernel, names), out_shape=tuple((j...]
where the time goes in v3:
time: 176 us
  Pallas kernels  175 us (99%)
    pallas_call x1, Pallas kernels, run_layer(): pl.pallas_call(functools.partial(layer_kernel, names), out_shape=tuple((j...  172 us

profile of v3, /device:TPU:0, one launch (start us, length us, event | category | flops | bytes accessed | tf_op | source)
XLA Modules:
  0.0 176.1 jit_solution(4922420495240479734)
XLA Ops:
  0.7 172.3 %layer.1 = (bf16[4,48,640]{2,1,0:T(8,128)(2,1)}, bf16[4,48,512]{2,1,0:T(8,128)(2,1)}, bf16[48,384]{1,0:T(8,128)(2,1)}, bf16[48,384]{1,0:T(8,128)(2,1)}, bf16[64,...) custom-call(bf16[128,768]{1,0:T(8,128)(2,1)} %bitcast.12, ...), custom_call_target="tpu_custom_call" | custom-call | tf_op jit(solution)/shard_map/layer/pallas_call | solution.py:1823
  173.0 2.9 %outputs.1 = (bf16[128,768]{1,0:T(8,128)(2,1)}, bf16[128,768]{1,0:T(8,128)(2,1)}, bf16[128,768]{1,0:T(8,128)(2,1)}, f32[1,24]{1,0:T(1,128)}, f32[24,768]{1,0:T(8...) custom-call(bf16[4,48,640]{2,1,0:T(8,128)(2,1)} %get-tuple-element.4, ...), custom_call_target="tpu_custom_call" | custom-call | tf_op jit(solution)/shard_map/outputs/pallas_call | solution.py:1896

commit v4 on v3

--- a/solution.py
+++ b/solution.py
@@ -536,7 +536,7 @@
 BF = jnp.bfloat16
 F32 = jnp.float32
 QW = 1152
-VMEM_LIMIT = 60 * 1024 * 1024
+VMEM_LIMIT = 62 * 1024 * 1024
 
 
 def coords():
@@ -1291,6 +1291,10 @@
     gather_o.start_across()
     R.FQ[g, s] = halves_stacked(R.v_cq)
     R.FC[g, s] = halves_stacked(R.v_co)
+    gather_q.start_across()
+    gather_c.start_across()
+    near_dn.wait()
+    gather_n.start_across()
     for one in parts_a:
         one.wait_recv()
     whole = []
@@ -1301,9 +1305,9 @@
     R.PA[s] = whole[:, :640]
     R.PB[s, :, :384] = whole[:, 640:]
     gather_a.start_across()
+    gather_a.start_along()
     move_x.arrive()
     gather_x.start()
-    gather_a.start_along()
     parts_b = to_group(R.stage_b, R.land_b, R.s_part_b)
     for one in parts_b:
         one.start()
@@ -1312,25 +1316,22 @@
     gather_q.start_along()
     gather_c.start_along()
     move_d.start()
+    gather_x.forward()
+    gather_a.forward(1)
     for k in (1, 3, 2):
         gather_o.forward(k)
-    gather_a.forward(1)
-    gather_x.forward()
-    gather_b.start_across()
     for one in parts_b:
         one.wait_recv()
     for half in range(2):
         rows = [R.land_b[r].astype(F32)[24 * half : 24 * half + 24] for r in range(4)]
         R.P2[s, :, 512 * half : 512 * half + 512] = jnp.concatenate(rows, axis=0).astype(BF)
     gather_2.start_along()
-    near_dn.wait()
     gather_x.forward_far()
     gather_o.arrive()
     whole_o.start()
     gather_a.forward(3)
     gather_a.forward(2)
-    gather_q.start_across()
-    gather_c.start_across()
+    gather_b.start_across()
     move_t.arrive()
     end_one, end_two = R.TAB[0:1, 0:1], R.TAB[1:2, 0:1]
     plot_one, plot_two = R.TAB[2:3, 0:1], R.TAB[3:4, 0:1]
@@ -1410,7 +1411,6 @@
     gather_2.forward(1)
     gather_n.start_along()
     gather_2.start_across()
-    gather_n.start_across()
     whole_o.arrive()
 
     def unpack_full(pieces, whole):
@@ -1442,6 +1442,8 @@
     gather_q.arrive()
     whole_q.start()
     gather_m.forward_far()
+    gather_2.forward(2)
+    gather_n.forward(1)
     gather_b.arrive()
     unpack(R.PB, R.WB, 384, 128)
     gather_c.arrive()
@@ -1454,8 +1456,6 @@
         return carry
 
     lax.fori_loop(0, 4, memory_pair, 0)
-    gather_2.forward(2)
-    gather_n.forward(1)
     whole_q.forward()
     whole_q.arrive()
     unpack_full(R.FQ, R.WQ)
@@ -1474,13 +1474,15 @@
         attend_head(h, R.info, R.CQT, R.MKV, R.MKVT, R.OUT2, R.LSE2, False)
         R.C4[g, h] = R.OUT2[64 * h : 64 * h + 64, :].astype(BF)
         share_2[h].start()
+        if h == 1:
+            gather_2.forward(3)
+            gather_n.forward(2)
     gather_d.start()
     whole_c.forward()
-    gather_2.forward(3)
-    gather_n.forward(2)
-    for h in range(3):
-        share_2[h].forward()
+    share_2[0].forward()
+    share_2[1].forward()
     gather_n.forward(3)
+    share_2[2].forward()
     whole_c.arrive()
     unpack_full(R.FC, R.WC)
     for one in share_2:
@@ -1498,52 +1500,59 @@
     gather_2.finish()
     gather_a.finish()
     gather_b.finish()
-    gather_d.arrive()
-    gather_n.arrive()
-
     sum_dx = Sum4(me, R.DXP, R.by_c_dx, R.by_x_dx, R.s_dx)
     sum_out = Sum4(me, R.OP, R.by_c_out, R.by_x_out, R.s_out)
 
-    def feed(core):
+    def feed_in(core):
         at = pl.ds(pl.multiple_of(core * 256, 256), 256)
         x3 = R.X3[at, :]
         gate, up = dot(x3, R.W2[:, :512]), dot(x3, R.W2[:, 512:])
         active, slope = gelu_parts(gate)
-        hidden = (active * up).astype(BF)
+        R.ACTIVE[at, :] = active.astype(BF)
+        R.FALL[at, :] = (up * slope).astype(BF)
+        R.H[at, :] = (active * up).astype(BF)
+
+    def feed_out(core):
+        at = pl.ds(pl.multiple_of(core * 256, 256), 256)
         outer = jnp.concatenate([R.DO[2 * core + px] for px in range(2)], axis=0)
         w_down = R.DN[...].reshape(512, 768)
         hidden_grad = dot_nt(outer, w_down)
-        gate_grad = (hidden_grad * up * slope).astype(BF)
-        up_grad = (hidden_grad * active).astype(BF)
+        gate_grad = (hidden_grad * R.FALL[at, :].astype(F32)).astype(BF)
+        up_grad = (hidden_grad * R.ACTIVE[at, :].astype(F32)).astype(BF)
         dx3 = (dot_nt(gate_grad, R.W2[:, :512]) + dot_nt(up_grad, R.W2[:, 512:])).astype(BF)
-        out = dot(hidden, w_down).astype(BF)
-        R.H[at, :] = hidden
         R.GG[at, :512] = gate_grad
         R.GG[at, 512:] = up_grad
         for px in range(2):
-            half = slice(128 * px, 128 * px + 128)
-            R.DXP[2 * core + px] = dx3[half]
-            R.OP[2 * core + px] = out[half]
+            R.DXP[2 * core + px] = dx3[128 * px : 128 * px + 128]
+
+    def feed_sum(core):
+        at = pl.ds(pl.multiple_of(core * 256, 256), 256)
+        out = dot(R.H[at, :], R.DN[...].reshape(512, 768)).astype(BF)
+        for px in range(2):
+            R.OP[2 * core + px] = out[128 * px : 128 * px + 128]
 
     def pack(whole, pieces, start, width):
         for t in range(8):
             rows = [whole[(8 * r + t) * 24 : (8 * r + t) * 24 + 24, :] for r in range(4)]
             pieces[t, :, start : start + width] = jnp.concatenate(rows, axis=0).astype(BF)
 
-    feed(1 - c)
+    feed_in(1 - c)
+    feed_in(c)
+    R.X3T[...] = R.X3[...].astype(F32).T.astype(BF)
+    gather_n.arrive()
+    gather_d.arrive()
+    feed_out(1 - c)
     sum_dx.start()
-    feed(c)
+    feed_out(c)
     sum_dx.to_x()
-    sum_out.start()
     own = pl.ds(pl.multiple_of(t * 128, 128), 128)
     own_block = 2 * t + y
-    x3_t = R.X3[...].astype(F32).T.astype(BF)
     total_2 = [
         SumPlaneDirect(me, R.P2, R.by_y_2, R.by_z_2, R.s_g2.at[i], slice(256 * i, 256 * i + 256))
         for i in range(4)
     ]
     for i in range(4):
-        R.W2G[...] = dot(x3_t, R.GG[:, 256 * i : 256 * i + 256])
+        R.W2G[...] = dot(R.X3T[...], R.GG[:, 256 * i : 256 * i + 256])
         pack(R.W2G, R.P2, 256 * i, 256)
         total_2[i].start()
     hidden_t = R.H[...].astype(F32).T.astype(BF)
@@ -1552,6 +1561,9 @@
         R.DNG[i] = d_down[64 * i : 64 * i + 64]
     total_n = SumPlaneDirect(me, R.DNG, R.by_y_n, R.by_z_n, R.s_gn)
     total_n.start()
+    feed_sum(1 - c)
+    feed_sum(c)
+    sum_out.start()
     part, gain_grad_three = norm_back(R.SECOND[own, :], gain_three, sum_dx.end())
     second_grad = R.DO[t].astype(F32) + part
     R.SGRAD[...] = second_grad
@@ -1649,7 +1661,6 @@
     sum_t.start()
     pack_24(dot(R.A4[g].reshape(192, 512), R.DFIRST[...]), R.SO8)
     total_s = SumPlane(me, R.SO8, R.by_y_s, R.by_z_s, R.s_gs)
-    total_s.start()
     dx2 = dot(R.WQ[...], R.DC4[:, :, :, own].reshape(768, 128)).T
     part, gain_grad_two = norm_back(R.FIRST[own, :], gain_two, dx2)
     R.SGRAD[...] += part
@@ -1661,22 +1672,25 @@
     R.W1G[...] = dot(R.DKV[...], R.X1[...].reshape(1024, 768)).T
     pack(R.W1G, R.PA, 0, 384)
     total_a = SumPlane(me, R.PA, R.by_y_a, R.by_z_a, R.s_ga, slice(0, 384))
+    total_a.start()
     R.TURN[:192, :] = dot(R.DQT[...], mine_rows(R.X1))
     R.TURN[192:, :] = dot(R.DCQT[...], R.X2[...])
     R.W1G[...] = R.TURN[...].T
     pack(R.W1G, R.PB, 384, 384)
-    total_q = SumPlane(me, R.PB, R.by_y_b, R.by_z_b, R.s_gq, slice(384, 768))
+    total_q = SumPlaneDirect(me, R.PB, R.by_y_b, R.by_z_b, R.s_gq, slice(384, 768))
     total_b.fold()
     total_2[3].pass_two()
     sum_t.to_y()
-    total_a.start()
     total_q.start()
+    total_s.start()
     total_c.pass_one()
     total_n.pass_two()
-    total_s.fold()
     total_b.pass_one()
     R.MBLOCK[...] = sum_m.end().T.astype(BF)
     back[2].start()
+    total_a.fold()
+    total_c.pass_two()
+    total_b.pass_two()
     dx1 = sum_t.end().T
     part, gain_grad_one = norm_back(R.X[own_block].astype(F32), gain_one, dx1)
     R.TBLOCK[...] = (R.SGRAD[...] + part).astype(BF)
@@ -1685,12 +1699,8 @@
     R.GT[1:2, :] = gain_grad_two
     R.GT[2:3, :] = gain_grad_three
     pack(R.GT[...].T, R.PG, 0, 128)
-    total_g = SumPlane(me, R.PG, R.by_y_g, R.by_z_g, R.s_gg)
+    total_g = SumPlaneDirect(me, R.PG, R.by_y_g, R.by_z_g, R.s_gg)
     total_g.start()
-    total_c.pass_two()
-    total_s.pass_one()
-    total_b.pass_two()
-    total_a.fold()
     for one in total_2:
         one.end()
     rows_2 = R.P2[s].astype(F32)
@@ -1701,38 +1711,46 @@
     for one in last_b:
         one.start()
     total_n.end()
+    total_a.pass_one()
     total_q.fold()
-    total_s.pass_two()
-    total_a.pass_one()
-    total_g.fold()
+    total_a.pass_two()
+    total_s.fold()
     total_c.end()
     total_b.end()
     total_q.pass_one()
-    total_a.pass_two()
+    total_g.fold()
+    total_s.pass_one()
+    total_a.end()
+    rows_a, rows_b = R.PA[s, :, :384].astype(F32), R.PB[s, :, :384].astype(F32)
+    for r in range(4):
+        rows = slice(24 * r, 24 * r + 24)
+        R.stage_z[r] = jnp.concatenate([rows_a[rows], rows_b[rows]], axis=0).astype(BF)
+    last_a = to_group(R.stage_z, R.quarters_a, R.s_last_a)
+    for one in last_a:
+        one.start()
+    total_q.pass_two()
     total_g.pass_one()
-    total_s.end()
-    total_q.pass_two()
+    total_s.pass_two()
     total_g.pass_two()
-    total_a.end()
     total_q.end()
     total_g.end()
-    rows_a, rows_b = R.PA[s, :, :384].astype(F32), R.PB[s].astype(F32)
+    rows_q = R.PB[s, :, 384:].astype(F32)
     rows_g = R.PG[s].astype(F32)
     for r in range(4):
         rows = slice(24 * r, 24 * r + 24)
-        top = [rows_a[rows], rows_b[rows, 384:576], rows_g[rows, :64]]
-        bottom = [rows_b[rows, :384], rows_b[rows, 576:], blank]
-        R.stage_z[r] = jnp.concatenate(
-            [jnp.concatenate(top, axis=1), jnp.concatenate(bottom, axis=1)], axis=0
-        ).astype(BF)
-    last_a = to_group(R.stage_z, R.quarters_a, R.s_last_a)
-    for one in last_a:
+        both = [rows_q[rows, :192], rows_g[rows, :64], rows_q[rows, 192:], blank]
+        both = jnp.concatenate(both, axis=1)
+        R.stage_q[r] = jnp.concatenate([both[:, :256], both[:, 256:]], axis=0).astype(BF)
+    last_q = to_group(R.stage_q, R.quarters_q, R.s_last_q)
+    for one in last_q:
         one.start()
+    total_s.end()
     near = [
         pltpu.make_async_copy(src, dst, R.s_near.at[1 + i])
         for i, (src, dst) in enumerate(
             (
                 (R.stage_z.at[g], R.quarters_a.at[g]),
+                (R.stage_q.at[g], R.quarters_q.at[g]),
                 (R.stage_b.at[g], R.quarters_b.at[g]),
                 (R.CO8.at[s], R.co_out),
                 (R.SO8.at[s], R.so_out),
@@ -1744,12 +1762,12 @@
         one.start()
     for one in near:
         one.wait()
-    for one in last_a + last_b:
+    for one in last_a + last_b + last_q:
         one.wait_recv()
     for one in back:
         one.arrive()
         one.finish()
-    for one in last_a + last_b:
+    for one in last_a + last_b + last_q:
         one.wait_send()
     for one in (move_x, move_t, move_m, move_d):
         one.finish()
@@ -1773,8 +1791,9 @@
         return pltpu.VMEM(shape, F32)
 
     outs = dict(
-        quarters_a=(4, 48, 640),
+        quarters_a=(4, 48, 384),
         quarters_b=(4, 48, 512),
+        quarters_q=(4, 48, 256),
         co_out=(48, 384),
         so_out=(48, 384),
         down_out=(64, d),
@@ -1783,7 +1802,7 @@
         memory_out=(n, d),
     )
     scratch = dict(
-        stage_a=low(4, 48, 512), land_a=low(4, 48, 512), stage_z=low(4, 48, 640), stage_b=low(4, 48, 512), land_b=low(4, 48, 512),
+        stage_a=low(4, 48, 512), land_a=low(4, 48, 512), stage_z=low(4, 48, 384), stage_q=low(4, 48, 256), stage_b=low(4, 48, 512), land_b=low(4, 48, 512),
         **{"v_" + name: pltpu.VMEM(inputs[name][0].shape, BF) for name in FETCHED},
         s_fetch=dma(len(FETCHED)),
         tabs=pltpu.VMEM((8, 128), jnp.int32), TAB=pltpu.VMEM((8, 128), jnp.int32),
@@ -1798,7 +1817,7 @@
         LSE1=full(8, 512), LSE2=full(8, 512),
         A4=low(4, 3, 64, 512), C4=low(4, 3, 64, 512), DC4=low(4, 3, 64, 512),
         FIRST=full(512, d), SECOND=full(512, d),
-        H=low(512, 512), GG=low(512, 1024), DXP=low(4, n, d), OP=low(4, n, d),
+        H=low(512, 512), ACTIVE=low(512, 512), FALL=low(512, 512), X3T=low(768, 512), GG=low(512, 1024), DXP=low(4, n, d), OP=low(4, n, d),
         by_c_dx=low(2, n, d), by_x_dx=low(n, d), by_c_out=low(2, n, d), by_x_out=low(n, d),
         W2G=full(768, 256), by_y_2=low(4, 96, 1024), by_z_2=low(5, 96, 1024),
         DNG=low(8, 64, d), by_y_n=low(4, 64, d), by_z_n=low(5, 64, d),
@@ -1813,8 +1832,8 @@
         by_y_a=low(4, 96, 384), by_z_a=low(5, 96, 384), by_y_b=low(4, 96, 768), by_z_b=low(5, 96, 768),
         by_y_g=low(4, 96, 128), by_z_g=low(5, 96, 128),
         TBLOCK=low(n, d), LBLOCK=low(n, d), MBLOCK=low(n, d),
-        s_move=dma(4, 2), s_near=dma(6), s_back=dma(3, 2),
-        **{name: dma(4) for name in ("s_part_a", "s_part_b", "s_last_a", "s_last_b", "s_d", "s_wo", "s_wc", "s_wq", "s_s", "s_dx", "s_out")},
+        s_move=dma(4, 2), s_near=dma(7), s_back=dma(3, 2),
+        **{name: dma(4) for name in ("s_part_a", "s_part_b", "s_last_a", "s_last_b", "s_last_q", "s_d", "s_wo", "s_wc", "s_wq", "s_s", "s_dx", "s_out")},
         **{name: dma(8) for name in ("s_x", "s_m", "s_gm", "s_gt", "s_a", "s_b", "s_fo", "s_fc", "s_fq")},
         s_2=dma(13), s_n=dma(13), s_share1=dma(3, 4), s_share2=dma(3, 4), s_share3=dma(3, 4), s_g2=dma(4, 10),
         **{name: dma(10) for name in ("s_ga", "s_gb", "s_gq", "s_gg", "s_gn", "s_gc", "s_gs")},
@@ -1845,19 +1864,22 @@
         return made
 
     arrive = copies(
-        ((R.qa, R.v_qa), (R.qb, R.v_qb), (R.co, R.v_co), (R.so, R.v_so), (R.down, R.v_down)), R.s_in
+        ((R.qa, R.v_qa), (R.qb, R.v_qb), (R.qq, R.v_qq), (R.co, R.v_co), (R.so, R.v_so), (R.down, R.v_down)), R.s_in
     )
     blocks = copies([(getattr(R, n), getattr(R, "v_" + n)) for n in BLOCKS], R.s_block)
     for one in arrive:
         one.wait()
     gains = jnp.zeros((24, 128), F32)
     for k in range(4):
-        piece = R.v_qa[k].astype(F32)
-        gains = gains + piece[:24, 512:]
+        piece, last = R.v_qa[k].astype(F32), R.v_qq[k].astype(F32)
+        gains = gains + last[:24, 128:]
         narrow = slice(192 * k, 192 * k + 192)
-        for row, outs in ((0, (R.w_sk, R.w_sv, R.w_sq)), (24, (R.w_ck, R.w_cv, R.w_cq))):
-            for i, out in enumerate(outs):
-                out[:, narrow] = piece[row : row + 24, 192 * i : 192 * i + 192]
+        R.w_sk[:, narrow] = piece[:24, :192]
+        R.w_sv[:, narrow] = piece[:24, 192:]
+        R.w_ck[:, narrow] = piece[24:, :192]
+        R.w_cv[:, narrow] = piece[24:, 192:]
+        R.w_sq[:, narrow] = last[:24, :192]
+        R.w_cq[:, narrow] = last[24:, :192]
         piece = R.v_qb[k].astype(F32)
         R.w_gate[:, 512 * k : 512 * k + 512] = piece[:24]
         R.w_up[:, 512 * k : 512 * k + 512] = piece[24:]
@@ -1882,7 +1904,7 @@
 
 
 def write_outputs(results):
-    ins = ("qa", "qb", "co", "so", "down", "tokens", "layer", "memory")
+    ins = ("qa", "qb", "qq", "co", "so", "down", "tokens", "layer", "memory")
     blocks = BLOCKS
     shapes = {name: (24, 768) for name in WEIGHTS}
     shapes |= {name: (1, 24) for name in ("g1", "g2", "g3")}
@@ -1891,7 +1913,7 @@
     outs += [jax.ShapeDtypeStruct(shapes[n], F32) for n in WEIGHTS]
     scratch = {"v_" + n: pltpu.VMEM(a.shape, BF) for n, a in zip(ins, results)}
     scratch |= {"w_" + n: pltpu.VMEM(shapes[n], F32) for n in WEIGHTS}
-    scratch |= dict(s_in=dma(5), s_direct=dma(3), s_block=dma(3), s_out=dma(len(WEIGHTS)))
+    scratch |= dict(s_in=dma(6), s_direct=dma(3), s_block=dma(3), s_out=dma(len(WEIGHTS)))
     names = ins + tuple("o_" + n for n in blocks + WEIGHTS) + tuple(scratch)
     return pl.pallas_call(
         functools.partial(outputs_kernel, names),

time: 176 us -> 171 us (0.972)
  Pallas kernels: 175 us -> 170 us
    pallas_call x1, Pallas kernels: 172 us -> 167 us  [run_layer(): pl.pallas_call(functools.partial(layer_kernel, names), out_shape=tuple((j...]
where the time goes in v4:
time: 171 us
  Pallas kernels  170 us (99%)
    pallas_call x1, Pallas kernels, run_layer(): pl.pallas_call(functools.partial(layer_kernel, names), out_shape=tuple((j...  167 us

profile of v4, /device:TPU:0, one launch (start us, length us, event | category | flops | bytes accessed | tf_op | source)
XLA Modules:
  0.0 171.2 jit_solution(10324902620604437150)
XLA Ops:
  0.7 167.4 %layer.1 = (bf16[4,48,384]{2,1,0:T(8,128)(2,1)}, bf16[4,48,512]{2,1,0:T(8,128)(2,1)}, bf16[4,48,256]{2,1,0:T(8,128)(2,1)}, bf16[48,384]{1,0:T(8,128)(2,1)}, bf16...) custom-call(bf16[128,768]{1,0:T(8,128)(2,1)} %bitcast.12, ...), custom_call_target="tpu_custom_call" | custom-call | tf_op jit(solution)/shard_map/layer/pallas_call | solution.py:1842
  168.1 2.9 %outputs.1 = (bf16[128,768]{1,0:T(8,128)(2,1)}, bf16[128,768]{1,0:T(8,128)(2,1)}, bf16[128,768]{1,0:T(8,128)(2,1)}, f32[1,24]{1,0:T(1,128)}, f32[24,768]{1,0:T(8...) custom-call(bf16[4,48,384]{2,1,0:T(8,128)(2,1)} %get-tuple-element.4, ...), custom_call_target="tpu_custom_call" | custom-call | tf_op jit(solution)/shard_map/outputs/pallas_call | solution.py:1918

commit v5 on v4

--- a/solution.py
+++ b/solution.py
@@ -1306,6 +1306,7 @@
     R.PB[s, :, :384] = whole[:, 640:]
     gather_a.start_across()
     gather_a.start_along()
+    gather_b.start_across()
     move_x.arrive()
     gather_x.start()
     parts_b = to_group(R.stage_b, R.land_b, R.s_part_b)
@@ -1331,7 +1332,7 @@
     whole_o.start()
     gather_a.forward(3)
     gather_a.forward(2)
-    gather_b.start_across()
+    gather_2.start_across()
     move_t.arrive()
     end_one, end_two = R.TAB[0:1, 0:1], R.TAB[1:2, 0:1]
     plot_one, plot_two = R.TAB[2:3, 0:1], R.TAB[3:4, 0:1]
@@ -1410,7 +1411,6 @@
         gather_c.forward(k)
     gather_2.forward(1)
     gather_n.start_along()
-    gather_2.start_across()
     whole_o.arrive()
 
     def unpack_full(pieces, whole):
@@ -1615,7 +1615,7 @@
     total_c.start()
     R.W1G[...] = dot(R.MDKV[...], R.M[...].reshape(1024, 768)).T
     pack(R.W1G, R.PB, 0, 384)
-    total_b = SumPlane(me, R.PB, R.by_y_b, R.by_z_b, R.s_gb, slice(0, 384))
+    total_b = SumPlaneDirect(me, R.PB, R.by_y_b, R.by_z_b, R.s_gb, slice(0, 384))
     total_b.start()
     share_3[2].forward()
     sum_m.start()

time: 171 us -> 170 us (level)
  no operation moved by 1% of the time
where the time goes in v5:
time: 170 us
  Pallas kernels  169 us (99%)
    pallas_call x1, Pallas kernels, run_layer(): pl.pallas_call(functools.partial(layer_kernel, names), out_shape=tuple((j...  166 us

profile of v5, /device:TPU:0, one launch (start us, length us, event | category | flops | bytes accessed | tf_op | source)
XLA Modules:
  0.0 169.6 jit_solution(15933064488486376676)
XLA Ops:
  0.7 165.9 %layer.1 = (bf16[4,48,384]{2,1,0:T(8,128)(2,1)}, bf16[4,48,512]{2,1,0:T(8,128)(2,1)}, bf16[4,48,256]{2,1,0:T(8,128)(2,1)}, bf16[48,384]{1,0:T(8,128)(2,1)}, bf16...) custom-call(bf16[128,768]{1,0:T(8,128)(2,1)} %bitcast.12, ...), custom_call_target="tpu_custom_call" | custom-call | tf_op jit(solution)/shard_map/layer/pallas_call | solution.py:1842
  166.5 2.9 %outputs.1 = (bf16[128,768]{1,0:T(8,128)(2,1)}, bf16[128,768]{1,0:T(8,128)(2,1)}, bf16[128,768]{1,0:T(8,128)(2,1)}, f32[1,24]{1,0:T(1,128)}, f32[24,768]{1,0:T(8...) custom-call(bf16[4,48,384]{2,1,0:T(8,128)(2,1)} %get-tuple-element.4, ...), custom_call_target="tpu_custom_call" | custom-call | tf_op jit(solution)/shard_map/outputs/pallas_call | solution.py:1918
